TPU v7x, 32 devices: a whole 2x2x4 slice. The times are simulated.
32 devices in a mesh: band: 2 (over core), dom: 16 (over z, y, x).
Axes of the slice: x: 2, y: 2, z: 4, core: 2. Of those that a mesh axis runs over, the one named last changes fastest.
Arguments:
- orbital_block: bfloat16 [4096, 1024], P('dom', 'band'), may hold values from -6 to 6
- cell_matrices: bfloat16 [64, 125, 125], P('dom'), may hold values from -0.09 to 0.09, as said below
- cell_nodes: int32 [125, 64], P(None, 'dom'), may hold values from 0 to 319, as said below
- shared_nodes: int32 [16, 64], P('dom'), may hold values from 0 to 255, as said below
- inv_sqrt_mass: float32 [4096], P('dom'), may hold values from 0.8 to 1.25
- potential: float32 [4096], P('dom'), may hold values from -0.5 to 0.3
- filter_center: float32 [1], replicated, may hold values from -0.1 to 0.1
- filter_halfwidth: float32 [1], replicated, may hold values from 0.8 to 1.2
Outputs:
- filtered: bfloat16 [4096, 1024], P('dom', 'band')
- intersection: float32 [1024, 1024], P(('band', 'dom'))
- projected: float32 [1024, 1024], P(('band', 'dom'))
Inputs may be any that keep to these rules, and one draw needn't show every extreme that they name: `cell_matrices`: each cell's matrix is symmetric. `cell_nodes`: column c lists the 125 nodes of cell c, a hexahedron of degree 4 with its nodes in lexicographic order, numbered as the device that holds the cell sees them: a value below 256 is one of its own nodes, a value 256 + j is entry j of the next device's (cyclically) shared list. Every own node and every shared entry is used by some cell. `shared_nodes`: row d holds 64 distinct own nodes of device d, which cells of device d - 1 (cyclically) also use.
All inputs are finite; a program needn't handle non-finite values.
Results may differ from a plain program's by a relative error of at most 0.024.
Values may be sent and summed in bfloat16 or wider, within the bound.
No kernel may reach another device: no remote copies, remote signals or barrier semaphores. Data moves between devices by JAX's collectives and lax.ppermute only.
A program may use at most 64 MiB of HBM per device.

v0:
```python
import jax
import jax.numpy as jnp
from jax import lax
from jax.sharding import PartitionSpec as P

FILTER_DEG = 4


def shifted(block, axis, distance):
    devices = range(lax.axis_size(axis))
    route = [((i - distance) % len(devices), i) for i in devices]
    return lax.ppermute(block, axis, route)


def hamilton(field, cell_matrices, cell_nodes, shared_local, inv_mass, potential):
    scaled = (inv_mass[:, None] * field).astype(jnp.bfloat16)
    ghost_rows = shifted(scaled[shared_local], "dom", -1)
    extended = jnp.concatenate([scaled, ghost_rows], axis=0)
    gathered = extended[cell_nodes]
    cell_out = jnp.einsum(
        "cij,jck->ick", cell_matrices, gathered, preferred_element_type=jnp.float32
    )
    node_count = field.shape[0]
    columns = field.shape[1]
    summed = jnp.zeros((node_count + ghost_rows.shape[0], columns), jnp.float32)
    summed = summed.at[cell_nodes.reshape(-1)].add(cell_out.reshape(-1, columns))
    incoming = shifted(summed[node_count:], "dom", 1)
    assembled = summed[:node_count].at[shared_local].add(incoming)
    return inv_mass[:, None] * assembled + potential[:, None] * field


def contract(left, right):
    return lax.dot_general(
        left, right, (((0,), (0,)), ((), ())), preferred_element_type=jnp.float32
    )


def shards(
    orbital_block,
    cell_matrices,
    cell_nodes,
    shared_nodes,
    inv_sqrt_mass,
    potential,
    filter_center,
    filter_halfwidth,
):
    shared_local = shared_nodes[0]
    center = filter_center[0]
    halfwidth = filter_halfwidth[0]

    def apply_ham(field):
        return hamilton(field, cell_matrices, cell_nodes, shared_local, inv_sqrt_mass, potential)

    def mapped(field):
        return (apply_ham(field) - center * field) / halfwidth

    previous = orbital_block.astype(jnp.float32)
    current = mapped(previous)
    for degree_step in range(FILTER_DEG - 1):
        following = 2.0 * mapped(current) - previous
        previous = current
        current = following
    filtered = current.astype(jnp.bfloat16)
    applied = apply_ham(filtered.astype(jnp.float32)).astype(jnp.bfloat16)
    band_count = lax.axis_size("band")
    dom_count = lax.axis_size("dom")
    my_group = lax.axis_index("band")
    block_width = filtered.shape[1]
    all_columns = block_width * band_count
    factor = 1.0 / (filtered.shape[0] * dom_count)
    intersection = jnp.zeros((block_width, all_columns), jnp.float32)
    projected = jnp.zeros((block_width, all_columns), jnp.float32)
    moving = filtered
    moving_applied = applied
    for cycle_step in range(band_count):
        if cycle_step > 0:
            moving, moving_applied = shifted((moving, moving_applied), "band", 1)
        source_group = (my_group - cycle_step) % band_count
        piece_intersection = contract(filtered, moving)
        piece_projected = contract(filtered, moving_applied)
        column_start = source_group * block_width
        zero_row = jnp.zeros((), jnp.int32)
        intersection = lax.dynamic_update_slice(
            intersection, piece_intersection, (zero_row, column_start)
        )
        projected = lax.dynamic_update_slice(projected, piece_projected, (zero_row, column_start))
    intersection, projected = (
        lax.psum_scatter(
            intersection.astype(jnp.bfloat16), "dom", scatter_dimension=0, tiled=True
        ).astype(jnp.float32),
        lax.psum_scatter(
            projected.astype(jnp.bfloat16), "dom", scatter_dimension=0, tiled=True
        ).astype(jnp.float32),
    )
    return (filtered, intersection * factor, projected * factor)


def solution(mesh):
    return jax.shard_map(
        shards,
        mesh=mesh,
        in_specs=(
            P("dom", "band"),
            P("dom", None, None),
            P(None, "dom"),
            P("dom", None),
            P("dom"),
            P("dom"),
            P(),
            P(),
        ),
        out_specs=(P("dom", "band"), P(("band", "dom"), None), P(("band", "dom"), None)),
        check_vma=False,
    )
```

profile of v0, /device:TPU:0, one launch (start us, length us, event | category | flops | bytes accessed | tf_op | source)
XLA Modules:
  0.0 273.3 jit_solution(2054081564574222735)
XLA Ops:
  10.4 7.0 %collective-permute-start = (bf16[64,512]{1,0:T(8,128)(2,1)S(1)}, bf16[64,512]{1,0:T(8,128)(2,1)S(1)}, u32[]{:S(2)}, u32[]{:S(2)}) collective-permute-start(bf16[64,512]{1,0:T(8,128)(2,1)S(1)} %gather_fusion), channel_id=1, source_target_pairs={{1,0},{2,1},{3,2},{4,3},{5,4},{6,5},{7,6},{8,7},{9,8},{10,9},{11,1... | collective-permute-start | bytes 196616 | tf_op jit(solution)/shard_map/ppermute | solution.py:12
  19.3 2.1 gather_fusion.1
  23.0 3.7 %scatter_custom_fusion = f32[320,512]{1,0:T(8,128)S(1)} fusion(s32[500]{0:T(512)S(1)} %bitcast.33, f32[500,512]{1,0:T(8,128)S(1)} %reshape.176, f32[]{:T(128)} %constant.14.clone.1), kind=kCustom, calls=%fused_computation.65 | custom fusion | flops 256000 | bytes 655364 | tf_op jit(solution)/shard_map/scatter-add | solution.py:26
  28.1 7.6 %collective-permute-done.1 = f32[64,512]{1,0:T(8,128)S(1)} collective-permute-done((f32[64,512]{1,0:T(8,128)S(1)}, f32[64,512]{1,0:T(8,128)S(1)}, u32[]{:S(2)}, u32[]{:S(2)}) %collective-permute-start.1) | collective-permute-done | bytes 131104 | tf_op jit(solution)/shard_map/ppermute | solution.py:12
  38.5 2.1 collective-permute-start.2
  40.7 2.4 collective-permute-done.2
  43.1 2.1 gather_fusion.3
  47.8 4.3 %scatter_custom_fusion.2 = f32[320,512]{1,0:T(8,128)S(1)} fusion(s32[500]{0:T(512)S(1)} %bitcast.34, f32[500,512]{1,0:T(8,128)} %reshape.192, f32[]{:T(128)} %constant.14.clone.1), kind=kCustom, calls=%fused_computation.63 | custom fusion | flops 256000 | bytes 655872 | tf_op jit(solution)/shard_map/scatter-add | solution.py:26
  52.2 8.5 %collective-permute-done.3 = f32[64,512]{1,0:T(8,128)S(1)} collective-permute-done((f32[64,512]{1,0:T(8,128)S(1)}, f32[64,512]{1,0:T(8,128)S(1)}, u32[]{:S(2)}, u32[]{:S(2)}) %collective-permute-start.3) | collective-permute-done | bytes 131104 | tf_op jit(solution)/shard_map/ppermute | solution.py:12
  63.0 2.3 collective-permute-start.4
  67.3 2.1 gather_fusion.5
  72.0 4.3 %scatter_custom_fusion.4 = f32[320,512]{1,0:T(8,128)S(1)} fusion(s32[500]{0:T(512)S(1)} %bitcast.35, f32[500,512]{1,0:T(8,128)} %reshape.208, f32[]{:T(128)} %constant.14.clone.1), kind=kCustom, calls=%fused_computation.61 | custom fusion | flops 256000 | bytes 655872 | tf_op jit(solution)/shard_map/scatter-add | solution.py:26
  76.5 8.8 %collective-permute-done.5 = f32[64,512]{1,0:T(8,128)S(1)} collective-permute-done((f32[64,512]{1,0:T(8,128)S(1)}, f32[64,512]{1,0:T(8,128)S(1)}, u32[]{:S(2)}, u32[]{:S(2)}) %collective-permute-start.5) | collective-permute-done | bytes 131104 | tf_op jit(solution)/shard_map/ppermute | solution.py:12
  89.8 2.3 collective-permute-done.6
  92.1 2.1 gather_fusion.7
  95.8 3.7 %scatter_custom_fusion.6 = f32[320,512]{1,0:T(8,128)S(1)} fusion(s32[500]{0:T(512)S(1)} %bitcast.36, f32[500,512]{1,0:T(8,128)S(1)} %reshape.224, f32[]{:T(128)} %constant.14.clone.1), kind=kCustom, calls=%fused_computation.59 | custom fusion | flops 256000 | bytes 655364 | tf_op jit(solution)/shard_map/scatter-add | solution.py:26
  99.7 8.5 %collective-permute-done.7 = f32[64,512]{1,0:T(8,128)S(1)} collective-permute-done((f32[64,512]{1,0:T(8,128)S(1)}, f32[64,512]{1,0:T(8,128)S(1)}, u32[]{:S(2)}, u32[]{:S(2)}) %collective-permute-start.7) | collective-permute-done | bytes 131104 | tf_op jit(solution)/shard_map/ppermute | solution.py:12
  113.3 2.3 collective-permute-start.9
  115.6 2.4 collective-permute-done.9
  117.9 2.1 gather_fusion.9
  121.6 3.7 %scatter_custom_fusion.8 = f32[320,512]{1,0:T(8,128)S(1)} fusion(s32[500]{0:T(512)S(1)} %bitcast.37, f32[500,512]{1,0:T(8,128)S(1)} %reshape.240, f32[]{:T(128)} %constant.14.clone.1), kind=kCustom, calls=%fused_computation.57 | custom fusion | flops 256000 | bytes 655364 | tf_op jit(solution)/shard_map/scatter-add | solution.py:26
  125.5 10.3 %collective-permute-done.10 = f32[64,512]{1,0:T(8,128)S(1)} collective-permute-done((f32[64,512]{1,0:T(8,128)S(1)}, f32[64,512]{1,0:T(8,128)S(1)}, u32[]{:S(2)}, u32[]{:S(2)}) %collective-permute-start.10) | collective-permute-done | bytes 131104 | tf_op jit(solution)/shard_map/ppermute | solution.py:12
  140.1 48.0 %reduce-scatter.3.cloned.1.call-done = bf16[32,1024]{1,0:T(8,128)(2,1)} async-done(((bf16[512,1024]{1,0:T(8,128)(2,1)}), bf16[32,1024]{1,0:T(8,128)(2,1)}) %reduce-scatter.3.cloned.1.call-update) | async-done | bytes 65552 | tf_op jit(solution)/shard_map/reduce_scatter | solution.py:89
  189.5 75.5 %reduce-scatter.5.cloned.1.call-done = bf16[32,1024]{1,0:T(8,128)(2,1)} async-done(((bf16[512,1024]{1,0:T(8,128)(2,1)}), bf16[32,1024]{1,0:T(8,128)(2,1)}) %reduce-scatter.5.cloned.1.call-update) | async-done | bytes 65552 | tf_op jit(solution)/shard_map/reduce_scatter | solution.py:92
  (100 shorter events, 39.1 us)
Async XLA Ops:
  7.2 14.5 %copy-start = (bf16[4,125,125]{2,0,1:T(4,128)(2,1)S(1)}, bf16[4,125,125]{2,0,1:T(4,128)(2,1)}, u32[]{:S(2)}) copy-start(bf16[4,125,125]{2,0,1:T(4,128)(2,1)} %param.9) | copy-start | bytes 375004
  7.2 180.8 %reduce-scatter.3.cloned.1.call-start = ((), (), s32[]{:S(2)}) async-start(), calls=%async_computation.2 | async-start | bytes 1114112 | tf_op jit(solution)/shard_map/reduce_scatter | solution.py:89
  7.9 0.7 copy-start.5
  9.7 7.7 %copy-start.7 = (s32[125,4]{0,1:T(4,128)S(1)}, s32[125,4]{0,1:T(4,128)}, u32[]{:S(2)}) copy-start(s32[125,4]{0,1:T(4,128)} %param.10) | copy-start | bytes 6004
  10.4 8.9 %collective-permute-start = (bf16[64,512]{1,0:T(8,128)(2,1)S(1)}, bf16[64,512]{1,0:T(8,128)(2,1)S(1)}, u32[]{:S(2)}, u32[]{:S(2)}) collective-permute-start(bf16[64,512]{1,0:T(8,128)(2,1)S(1)} %gather_fusion), channel_id=1, source_target_pairs={{1,0},{2,1},{3,2},{4,3},{5,4},{6,5},{7,6},{8,7},{9,8},{10,9},{11,1... | collective-permute-start | bytes 196616 | tf_op jit(solution)/shard_map/ppermute | solution.py:12
  26.7 9.1 %collective-permute-start.1 = (f32[64,512]{1,0:T(8,128)S(1)}, f32[64,512]{1,0:T(8,128)S(1)}, u32[]{:S(2)}, u32[]{:S(2)}) collective-permute-start(f32[64,512]{1,0:T(8,128)S(1)} %slice.61), channel_id=1, source_target_pairs={{15,0},{0,1},{1,2},{2,3},{3,4},{4,5},{5,6},{6,7},{7,8},{8,9},{9,10... | collective-permute-start | bytes 393224 | tf_op jit(solution)/shard_map/ppermute | solution.py:12
  28.1 8.9 %copy-start.4 = (bf16[256,512]{1,0:T(8,128)(2,1)S(1)}, bf16[256,512]{1,0:T(8,128)(2,1)}, u32[]{:S(2)}) copy-start(bf16[256,512]{1,0:T(8,128)(2,1)} %param.8) | copy-start | bytes 786436
  36.9 0.7 copy-start.6
  38.5 4.5 %collective-permute-start.2 = (bf16[64,512]{1,0:T(8,128)(2,1)S(1)}, bf16[64,512]{1,0:T(8,128)(2,1)S(1)}, u32[]{:S(2)}, u32[]{:S(2)}) collective-permute-start(bf16[64,512]{1,0:T(8,128)(2,1)S(1)} %gather_fusion.2), channel_id=1, source_target_pairs={{1,0},{2,1},{3,2},{4,3},{5,4},{6,5},{7,6},{8,7},{9,8},{10,9},{11,1... | collective-permute-start | bytes 196616 | tf_op jit(solution)/shard_map/ppermute | solution.py:12
  52.1 8.6 %collective-permute-start.3 = (f32[64,512]{1,0:T(8,128)S(1)}, f32[64,512]{1,0:T(8,128)S(1)}, u32[]{:S(2)}, u32[]{:S(2)}) collective-permute-start(f32[64,512]{1,0:T(8,128)S(1)} %slice.63), channel_id=1, source_target_pairs={{15,0},{0,1},{1,2},{2,3},{3,4},{4,5},{5,6},{6,7},{7,8},{8,9},{9,10... | collective-permute-start | bytes 393224 | tf_op jit(solution)/shard_map/ppermute | solution.py:12
  63.0 4.3 %collective-permute-start.4 = (bf16[64,512]{1,0:T(8,128)(2,1)S(1)}, bf16[64,512]{1,0:T(8,128)(2,1)S(1)}, u32[]{:S(2)}, u32[]{:S(2)}) collective-permute-start(bf16[64,512]{1,0:T(8,128)(2,1)S(1)} %gather_fusion.4), channel_id=1, source_target_pairs={{1,0},{2,1},{3,2},{4,3},{5,4},{6,5},{7,6},{8,7},{9,8},{10,9},{11,1... | collective-permute-start | bytes 196616 | tf_op jit(solution)/shard_map/ppermute | solution.py:12
  76.4 8.9 %collective-permute-start.5 = (f32[64,512]{1,0:T(8,128)S(1)}, f32[64,512]{1,0:T(8,128)S(1)}, u32[]{:S(2)}, u32[]{:S(2)}) collective-permute-start(f32[64,512]{1,0:T(8,128)S(1)} %slice.65), channel_id=1, source_target_pairs={{15,0},{0,1},{1,2},{2,3},{3,4},{4,5},{5,6},{6,7},{7,8},{8,9},{9,10... | collective-permute-start | bytes 393224 | tf_op jit(solution)/shard_map/ppermute | solution.py:12
  87.7 4.4 %collective-permute-start.6 = (bf16[64,512]{1,0:T(8,128)(2,1)S(1)}, bf16[64,512]{1,0:T(8,128)(2,1)S(1)}, u32[]{:S(2)}, u32[]{:S(2)}) collective-permute-start(bf16[64,512]{1,0:T(8,128)(2,1)S(1)} %gather_fusion.6), channel_id=1, source_target_pairs={{1,0},{2,1},{3,2},{4,3},{5,4},{6,5},{7,6},{8,7},{9,8},{10,9},{11,1... | collective-permute-start | bytes 196616 | tf_op jit(solution)/shard_map/ppermute | solution.py:12
  99.5 8.6 %collective-permute-start.7 = (f32[64,512]{1,0:T(8,128)S(1)}, f32[64,512]{1,0:T(8,128)S(1)}, u32[]{:S(2)}, u32[]{:S(2)}) collective-permute-start(f32[64,512]{1,0:T(8,128)S(1)} %slice.67), channel_id=1, source_target_pairs={{15,0},{0,1},{1,2},{2,3},{3,4},{4,5},{5,6},{6,7},{7,8},{8,9},{9,10... | collective-permute-start | bytes 393224 | tf_op jit(solution)/shard_map/ppermute | solution.py:12
  109.6 29.1 %copy-start.1 = (bf16[256,512]{1,0:T(8,128)(2,1)}, bf16[256,512]{1,0:T(8,128)(2,1)S(1)}, u32[]{:S(2)}) copy-start(bf16[256,512]{1,0:T(8,128)(2,1)S(1)} %get-tuple-element.4) | copy-start | bytes 786436
  109.6 1.6 collective-permute-start.8
  111.5 1.0 copy-start.3
  112.5 152.5 %reduce-scatter.5.cloned.1.call-start = ((), (), s32[]{:S(2)}) async-start(), calls=%async_computation.3 | async-start | bytes 1114112 | tf_op jit(solution)/shard_map/reduce_scatter | solution.py:92
  113.3 4.6 %collective-permute-start.9 = (bf16[64,512]{1,0:T(8,128)(2,1)S(1)}, bf16[64,512]{1,0:T(8,128)(2,1)S(1)}, u32[]{:S(2)}, u32[]{:S(2)}) collective-permute-start(bf16[64,512]{1,0:T(8,128)(2,1)S(1)} %gather_fusion.8), channel_id=1, source_target_pairs={{1,0},{2,1},{3,2},{4,3},{5,4},{6,5},{7,6},{8,7},{9,8},{10,9},{11,1... | collective-permute-start | bytes 196616 | tf_op jit(solution)/shard_map/ppermute | solution.py:12
  125.3 10.4 %collective-permute-start.10 = (f32[64,512]{1,0:T(8,128)S(1)}, f32[64,512]{1,0:T(8,128)S(1)}, u32[]{:S(2)}, u32[]{:S(2)}) collective-permute-start(f32[64,512]{1,0:T(8,128)S(1)} %slice.69), channel_id=1, source_target_pairs={{15,0},{0,1},{1,2},{2,3},{3,4},{4,5},{5,6},{6,7},{7,8},{8,9},{9,10... | collective-permute-start | bytes 393224 | tf_op jit(solution)/shard_map/ppermute | solution.py:12
  137.1 1.6 collective-permute-start.11
  139.0 1.0 copy-start.2
Sparse Core Ops, SparseCore 0:
  112.6 75.3 reduce-scatter.2
  190.4 74.5 reduce-scatter.4
where the time goes:
time: 274 us; the launch traced here: 273 us
  waiting for transfers between devices  180 us (66%)
  other arithmetic  32 us (12%)
  local copies, waits for them, and re-layouts  26.6 us (10%)
  starting transfers between devices  16.3 us (6%)
  between operations  16 us (6%)
  matrix products  2.85 us (1%)
    reduce_scatter x1, waiting for transfers between devices, shards(): lax.psum_scatter(projected.astype(jnp.bfloat16), 'dom', scatter_dimension...  75.5 us
    ppermute x12, waiting for transfers between devices, shifted(): return lax.ppermute(block, axis, route)  56.2 us
    reduce_scatter x1, waiting for transfers between devices, shards(): lax.psum_scatter(intersection.astype(jnp.bfloat16), 'dom', scatter_dimens...  48 us
    scatter-add x5, other arithmetic, hamilton(): summed.at[cell_nodes.reshape(-1)].add(cell_out.reshape(-1, columns))  19.7 us
    ppermute x12, starting transfers between devices, shifted(): return lax.ppermute(block, axis, route)  16.3 us
    gather x10, local copies, waits for them, and re-layouts, hamilton(): gathered = extended[cell_nodes]  11.7 us
    scatter-add x5, other arithmetic, hamilton(): assembled = summed[:node_count].at[shared_local].add(incoming)  6.1 us
  transfers between devices with their start and end apart: 14, of which 14 were waited for; matrix products, arithmetic and copies ran while one was open for 5% of the time, Pallas kernels for 0%

commit v1 on v0

v1 whole, which is shorter than its diff:
```python
import functools

import jax
import jax.numpy as jnp
from jax import lax
from jax.experimental import pallas as pl
from jax.experimental.pallas import tpu as pltpu
from jax.sharding import PartitionSpec as P

FILTER_DEG = 4
GROUP = 4
LANES = 128
EXTRA = 32
F32 = jnp.float32
BF16 = jnp.bfloat16
VMEM_LIMIT = 48 * 1024 * 1024


def dot(a, b):
    return jnp.dot(a, b, preferred_element_type=F32)


def dot_nt(a, b):
    return lax.dot_general(a, b, (((1,), (1,)), ((), ())), preferred_element_type=F32)


def iota(shape, dim):
    return lax.broadcasted_iota(jnp.int32, shape, dim)


def split3(x):
    high = x.astype(BF16)
    rest = x - high.astype(F32)
    middle = rest.astype(BF16)
    low = (rest - middle.astype(F32)).astype(BF16)
    return high, middle, low


def pack_kernel(planes, place_ref, field_ref, cells_ref, nodes_ref, shared_ref, mass_ref, pot_ref, *outs):
    out_refs, turned = outs[:GROUP], outs[GROUP]
    place = place_ref[0]
    nodes, width = field_ref.shape
    cells, corners, _ = cells_ref.shape
    rows = LANES // planes
    source = iota((width, LANES), 0)
    target = iota((width, LANES), 1)
    turned[...] = jnp.zeros_like(turned)
    turned[0:corners, 0:cells] = nodes_ref[...].astype(F32)
    tables = jnp.transpose(turned[...])[0:8]
    lane = iota((8, LANES), 1)
    high = jnp.floor(tables * (1.0 / 64.0))
    low = tables - 64.0 * high
    high = jnp.where(lane < corners, high, -8.0)
    shared = jnp.concatenate(
        [shared_ref[...].astype(F32), jnp.zeros((1, LANES - shared_ref.shape[1]), F32)], axis=1
    )
    pieces = [high[0:cells], low[0:cells], shared]
    for value_ref in (mass_ref, pot_ref):
        pieces += [part.astype(F32) for part in split3(value_ref[...])]
    used = sum(piece.shape[0] for piece in pieces)
    pieces.append(jnp.zeros((EXTRA - used, LANES), F32))
    extra = jnp.concatenate(pieces, axis=0).astype(BF16)
    for k in range(GROUP):
        chunk = place ^ k
        pick = (target // rows) * (GROUP * rows) + chunk * rows + target % rows == source
        out_refs[k][0:nodes, :] = dot(field_ref[...], pick.astype(F32).astype(BF16)).astype(BF16)
        base = nodes
        for c in range(cells):
            out_refs[k][base + c * LANES : base + (c + 1) * LANES, :] = jnp.zeros((LANES, LANES), BF16)
            out_refs[k][base + c * LANES : base + c * LANES + corners, 0:corners] = cells_ref[c]
        out_refs[k][base + cells * LANES :, :] = extra


def apply_plane(own, down, up, fields, outside_u, outside_g, keep=None):
    shared = down[0].shape[0] // 2
    traces = [dot(down[i], fields[i]) for i in range(GROUP)]
    to_next = traces[GROUP - 1][:shared]
    to_previous = traces[0][shared:]
    w, g = outside_u, outside_g
    if callable(outside_u):
        w, g = outside_u(to_previous, to_next)
    sums = []
    for i in range(GROUP):
        if keep is not None and i not in keep:
            sums.append(None)
            continue
        below = w if i == 0 else traces[i - 1][:shared]
        above = g if i == GROUP - 1 else traces[i + 1][shared:]
        total = dot(own[i], fields[i])
        if below is None:
            below = jnp.zeros_like(to_next)
        if above is None:
            above = jnp.zeros_like(to_next)
        sides = jnp.concatenate([above, below], axis=0).astype(BF16)
        sums.append(total + dot(up[i], sides))
    return sums, traces


def first_kernel(
    cells, shared, place_ref, center_ref, half_ref, m0, m1, m2, m3,
    own_ref, down_ref, up_ref, mass_ref, scale_ref, diag_ref, start_ref, next_ref, previous_ref,
    raw, corner, cur, prev,
):
    place = place_ref[0]
    center, half = center_ref[0], half_ref[0]
    nodes = raw.shape[1]
    both = nodes + shared
    halves = nodes // LANES
    for k, ref in enumerate((m0, m1, m2, m3)):
        slab = place ^ k
        base = nodes + cells * LANES
        extra = ref[base : base + EXTRA, :].astype(F32)
        ids = (64.0 * extra[0:cells] + extra[cells : 2 * cells]).astype(jnp.int32)
        total = jnp.zeros((both, both), F32)
        for c in range(cells):
            pick = (iota((both, LANES), 0) == ids[c : c + 1]).astype(F32).astype(BF16)
            matrix = ref[nodes + c * LANES : nodes + (c + 1) * LANES, :]
            half_way = dot(pick, matrix).astype(BF16)
            total = total + dot_nt(half_way, pick)
        raw[slab] = total[:nodes, :nodes]
        corner[slab] = total[nodes:, nodes:]
        own_shared = extra[2 * cells : 2 * cells + 1, 0:shared].astype(jnp.int32)
        place_in = (iota((nodes, shared), 0) == own_shared).astype(F32)
        sides = jnp.concatenate([total[:nodes, nodes:], place_in], axis=1)
        up_ref[slab] = sides.astype(BF16)
        down_ref[slab] = jnp.transpose(sides).astype(BF16)
        row = 2 * cells + 1
        for h in range(halves):
            at = pl.ds(pl.multiple_of(slab * nodes + h * LANES, LANES), LANES)
            mass_row = sum(extra[row + j * halves + h : row + j * halves + h + 1] for j in range(3))
            off = row + 3 * halves
            pot_row = sum(extra[off + j * halves + h : off + j * halves + h + 1] for j in range(3))
            mass = jnp.transpose(jnp.broadcast_to(mass_row, (LANES, LANES)))
            pot = jnp.transpose(jnp.broadcast_to(pot_row, (LANES, LANES)))
            mass_ref[at, :] = mass
            scale_ref[at, :] = mass / half
            diag_ref[at, :] = (pot - center) / half
        start_ref[pl.ds(pl.multiple_of(slab * nodes, nodes), nodes), :] = ref[0:nodes, :]
    own_ref[0] = raw[0].astype(BF16)
    for i in range(1, GROUP):
        place_in = up_ref[i][:, shared:]
        moved = dot(place_in, corner[i - 1].astype(BF16)).astype(BF16)
        own_ref[i] = (raw[i] + dot_nt(moved, place_in)).astype(BF16)

    cur[:, 0:LANES] = start_ref[...].astype(F32)
    cur[:, LANES:] = jnp.zeros((GROUP * nodes, 2 * shared), F32)
    top = (GROUP - 1) * nodes
    first = up_ref[0].astype(F32)
    last = up_ref[GROUP - 1].astype(F32)
    lane = iota((nodes, 2 * shared), 1)
    swapped = jnp.concatenate([first[:, shared:], first[:, :shared]], axis=1)
    cur[0:nodes, LANES:] = jnp.where(lane < shared, swapped * scale_ref[0:nodes, :], 0.0)
    swapped = jnp.concatenate([last[:, shared:], last[:, :shared]], axis=1)
    cur[top:, LANES:] = cur[top:, LANES:] + jnp.where(lane >= shared, swapped * scale_ref[top:, :], 0.0)
    prev[...] = jnp.zeros_like(prev)

    own = [own_ref[i] for i in range(GROUP)]
    down = [down_ref[i] for i in range(GROUP)]
    up = [up_ref[i] for i in range(GROUP)]

    def wide(ref, i):
        part = ref[i * nodes : (i + 1) * nodes, :]
        return jnp.concatenate([part, part], axis=1)

    next_parts, previous_parts = [], []
    for k in range(FILTER_DEG):
        last_step = k == FILTER_DEG - 1
        if last_step:
            field0 = (mass_ref[0:nodes, :] * cur[0:nodes, 0:LANES]).astype(BF16)
            field3 = (mass_ref[top:, :] * cur[top:, 0:LANES]).astype(BF16)
            next_ref[k * shared : (k + 1) * shared, :] = dot(down[GROUP - 1], field3)[:shared].astype(BF16)
            previous_ref[k * shared : (k + 1) * shared, :] = dot(down[0], field0)[shared:].astype(BF16)
            break
        fields = [(wide(mass_ref, i) * cur[i * nodes : (i + 1) * nodes, :]).astype(BF16) for i in range(GROUP)]
        keep = None if k < FILTER_DEG - 2 else (0, GROUP - 1)
        sums, traces = apply_plane(own, down, up, fields, None, None, keep)
        to_next = traces[GROUP - 1][:shared]
        to_previous = traces[0][shared:]
        next_ref[k * shared : (k + 1) * shared, :] = to_next[:, 0:LANES].astype(BF16)
        previous_ref[k * shared : (k + 1) * shared, :] = to_previous[:, 0:LANES].astype(BF16)
        next_parts.append(to_next[:, LANES + shared :])
        previous_parts.append(to_previous[:, LANES : LANES + shared])
        for i in range(GROUP):
            if sums[i] is None:
                continue
            at = slice(i * nodes, (i + 1) * nodes)
            now = cur[at, :]
            image = wide(scale_ref, i) * sums[i] + wide(diag_ref, i) * now
            if k == 0:
                factor = jnp.where(iota((1, 2 * LANES), 1) < LANES, 1.0, 2.0)
                new = factor * image
            else:
                new = 2.0 * image - prev[at, :]
            prev[at, :] = now
            cur[at, :] = new
    at = FILTER_DEG * shared
    next_parts.append(corner[GROUP - 1])
    previous_parts.append(jnp.zeros((shared, shared), F32))
    for j in range(2):
        next_ref[at + j * shared : at + (j + 1) * shared, :] = jnp.concatenate(
            next_parts[2 * j : 2 * j + 2], axis=1
        ).astype(BF16)
        previous_ref[at + j * shared : at + (j + 1) * shared, :] = jnp.concatenate(
            previous_parts[2 * j : 2 * j + 2], axis=1
        ).astype(BF16)


def second_kernel(
    shared, own_ref, down_ref, up_ref, mass_ref, scale_ref, diag_ref, start_ref, sent_ref, below_ref, above_ref,
    filtered_ref, next_ref, previous_ref, cur, prev,
):
    nodes = own_ref.shape[1]
    own = [own_ref[i] for i in range(GROUP)]
    down = [down_ref[i] for i in range(GROUP)]
    up = [up_ref[i] for i in range(GROUP)]
    at = FILTER_DEG * shared
    near_b, far_b = below_ref[at : at + shared, :], below_ref[at + shared : at + 2 * shared, :]
    near_a, far_a = above_ref[at : at + shared, :], above_ref[at + shared : at + 2 * shared, :]
    mine = sent_ref[at + shared : at + 2 * shared, :]
    zero = jnp.zeros((shared, LANES), BF16)
    cur[...] = start_ref[...].astype(F32)
    prev[...] = jnp.zeros_like(prev)
    below_past, above_past = [], []

    def past(items, lag):
        if lag > len(items):
            return zero
        item = items[len(items) - lag]
        return item if lag == len(items) else item * 2

    def pair(a, b):
        return jnp.concatenate([a, b], axis=0)

    for k in range(FILTER_DEG):

        def outside(to_previous, to_next, k=k):
            here = to_previous.astype(BF16)
            below = below_ref[k * shared : (k + 1) * shared, :].astype(F32)
            below = below + dot(near_b, pair(past(below_past, 1), past(below_past, 2)))
            below = below + dot(far_b, pair(past(below_past, 3), here))
            above = above_ref[k * shared : (k + 1) * shared, :].astype(F32)
            above = above + dot(near_a, pair(past(above_past, 1), past(above_past, 2)))
            above = above + dot(far_a, pair(past(above_past, 3), zero))
            force = to_next + dot(mine, pair(zero, above.astype(BF16)))
            below_past.append(here)
            above_past.append(force.astype(BF16))
            return below, above

        fields = [
            (mass_ref[i * nodes : (i + 1) * nodes, :] * cur[i * nodes : (i + 1) * nodes, :]).astype(BF16)
            for i in range(GROUP)
        ]
        sums, _ = apply_plane(own, down, up, fields, outside, None)
        for i in range(GROUP):
            rows = slice(i * nodes, (i + 1) * nodes)
            now = cur[rows, :]
            image = scale_ref[rows, :] * sums[i] + diag_ref[rows, :] * now
            new = image if k == 0 else 2.0 * image - prev[rows, :]
            prev[rows, :] = now
            cur[rows, :] = new
    filtered_ref[...] = cur[...].astype(BF16)
    top = (GROUP - 1) * nodes
    field0 = (mass_ref[0:nodes, :] * filtered_ref[0:nodes, :].astype(F32)).astype(BF16)
    field3 = (mass_ref[top:, :] * filtered_ref[top:, :].astype(F32)).astype(BF16)
    next_ref[...] = dot(down[GROUP - 1], field3)[:shared].astype(BF16)
    previous_ref[...] = dot(down[0], field0)[shared:].astype(BF16)


def third_kernel(
    shared, center_ref, half_ref, own_ref, down_ref, up_ref, mass_ref, diag_ref, filtered_ref, corner_ref, below_ref,
    above_ref, applied_ref,
):
    nodes = own_ref.shape[1]
    center, half = center_ref[0], half_ref[0]
    own = [own_ref[i] for i in range(GROUP)]
    down = [down_ref[i] for i in range(GROUP)]
    up = [up_ref[i] for i in range(GROUP)]
    at = FILTER_DEG * shared
    far_b = corner_ref[at + shared : at + 2 * shared, :]
    zero = jnp.zeros((shared, LANES), BF16)

    def outside(to_previous, to_next):
        below = below_ref[...].astype(F32)
        below = below + dot(far_b, jnp.concatenate([zero, to_previous.astype(BF16)], axis=0))
        return below, above_ref[...].astype(F32)

    values = [filtered_ref[i * nodes : (i + 1) * nodes, :].astype(F32) for i in range(GROUP)]
    fields = [(mass_ref[i * nodes : (i + 1) * nodes, :] * values[i]).astype(BF16) for i in range(GROUP)]
    sums, _ = apply_plane(own, down, up, fields, outside, None)
    for i in range(GROUP):
        rows = slice(i * nodes, (i + 1) * nodes)
        pot = diag_ref[rows, :] * half + center
        applied_ref[rows, :] = (mass_ref[rows, :] * sums[i] + pot * values[i]).astype(BF16)


def call(kernel, outs, args, scalars=0, scratch=(), flops=0):
    in_specs = [pl.BlockSpec(memory_space=pltpu.SMEM)] * scalars
    in_specs += [pl.BlockSpec(memory_space=pltpu.VMEM)] * (len(args) - scalars)
    return pl.pallas_call(
        kernel,
        out_shape=[jax.ShapeDtypeStruct(shape, dtype) for shape, dtype in outs],
        in_specs=in_specs,
        out_specs=[pl.BlockSpec(memory_space=pltpu.VMEM)] * len(outs),
        scratch_shapes=list(scratch),
        compiler_params=pltpu.CompilerParams(vmem_limit_bytes=VMEM_LIMIT),
        cost_estimate=pl.CostEstimate(flops=flops, bytes_accessed=1 << 21, transcendentals=0),
    )(*args)


def contract(left, right):
    return lax.dot_general(left, right, (((0,), (0,)), ((), ())), preferred_element_type=F32)


def shards(
    orbital_block, cell_matrices, cell_nodes, shared_nodes, inv_sqrt_mass, potential, filter_center, filter_halfwidth
):
    band_count = lax.axis_size("band")
    dom_count = lax.axis_size("dom")
    planes = dom_count // GROUP
    nodes, width = orbital_block.shape
    cells = cell_matrices.shape[0]
    shared = shared_nodes.shape[1]
    rows = width // dom_count
    here = lax.axis_index("dom")
    band = lax.axis_index("band")
    plane, place = here // GROUP, here % GROUP
    place_arg = place.astype(jnp.int32).reshape(1)
    everyone = range(dom_count)

    def in_plane(block, k):
        return lax.ppermute(block, "dom", [(i, i ^ k) for i in everyone])

    def to_plane(block, k):
        route = [(i, (i // GROUP + k) % planes * GROUP + i % GROUP) for i in everyone]
        return lax.ppermute(block, "dom", route)

    def to_band(block, k):
        return lax.ppermute(block, "band", [(i, (i + k) % band_count) for i in range(band_count)])

    message = ((nodes + cells * LANES + EXTRA, LANES), BF16)
    messages = call(
        functools.partial(pack_kernel, planes),
        [message] * GROUP,
        (
            place_arg, orbital_block, cell_matrices, cell_nodes, shared_nodes,
            inv_sqrt_mass.reshape(-1, LANES), potential.reshape(-1, LANES),
        ),
        scalars=1,
        scratch=[pltpu.VMEM((LANES, LANES), F32)],
    )
    messages = [messages[0]] + [in_plane(messages[k], k) for k in range(1, GROUP)]
    height = GROUP * nodes
    column = ((height, LANES), F32)
    trace = ((FILTER_DEG * shared + 2 * shared, LANES), BF16)
    own, down, up, mass, scale, diag, start, next_msg, previous_msg = call(
        functools.partial(first_kernel, cells, shared),
        [
            ((GROUP, nodes, nodes), BF16), ((GROUP, 2 * shared, nodes), BF16), ((GROUP, nodes, 2 * shared), BF16),
            column, column, column, ((height, LANES), BF16), trace, trace,
        ],
        (place_arg, filter_center, filter_halfwidth, *messages),
        scalars=3,
        scratch=[
            pltpu.VMEM((GROUP, nodes, nodes), F32), pltpu.VMEM((GROUP, shared, shared), F32),
            pltpu.VMEM((height, 2 * LANES), F32), pltpu.VMEM((height, 2 * LANES), F32),
        ],
        flops=1 << 30,
    )
    below = to_plane(next_msg, 1)
    above = to_plane(previous_msg, -1)
    mine, next_msg, previous_msg = call(
        functools.partial(second_kernel, shared),
        [((height, LANES), BF16), ((shared, LANES), BF16), ((shared, LANES), BF16)],
        (own, down, up, mass, scale, diag, start, next_msg, below, above),
        scratch=[pltpu.VMEM((height, LANES), F32), pltpu.VMEM((height, LANES), F32)],
        flops=1 << 30,
    )
    below_now = to_plane(next_msg, 1)
    above_now = to_plane(previous_msg, -1)
    others = [in_plane(mine, k) for k in range(1, GROUP)]
    (applied,) = call(
        functools.partial(third_kernel, shared),
        [((height, LANES), BF16)],
        (filter_center, filter_halfwidth, own, down, up, mass, diag, mine, below, below_now, above_now),
        scalars=2,
        flops=1 << 28,
    )

    lefts = [applied] + [to_band(applied, k) for k in range(1, band_count)]
    lefts += [mine] + [to_band(mine, k) for k in range(1, band_count)]
    left = jnp.concatenate(lefts, axis=1)
    right = jnp.concatenate([mine] + others, axis=1)
    product = contract(left, right).reshape(2 * band_count, planes, rows, width)

    def part_for(k):
        return lax.dynamic_index_in_dim(product, (plane + k) % planes, 1, keepdims=False)

    total = part_for(0)
    for k in range(1, planes):
        total = total + to_plane(part_for(k).astype(BF16), k).astype(F32)

    total = total.reshape(2, band_count, rows, width)
    own_rows = total[:, 0]
    pieces = [own_rows] + [to_band(total[:, j], -j) for j in range(1, band_count)]
    stacked = jnp.stack(pieces)
    stacked = stacked.reshape(band_count, 2, rows, GROUP, LANES)
    ordered = jnp.stack(
        [
            jnp.stack([
                lax.dynamic_index_in_dim(
                    lax.dynamic_index_in_dim(stacked, (b - band) % band_count, 0, keepdims=False),
                    place ^ c, 2, keepdims=False,
                )
                for c in range(GROUP)
            ], axis=2)
            for b in range(band_count)
        ],
        axis=2,
    )
    ordered = ordered.reshape(2, rows, band_count, GROUP, planes, rows)
    ordered = jnp.transpose(ordered, (0, 1, 2, 4, 3, 5)).reshape(2, rows, band_count * width)
    factor = 1.0 / (nodes * dom_count)
    outcome = ordered * factor

    chunks = jnp.stack([mine] + others).reshape(GROUP, GROUP, nodes, LANES)
    chunks = lax.dynamic_index_in_dim(chunks, place, 1, keepdims=False)
    chunks = jnp.stack(
        [lax.dynamic_index_in_dim(chunks, place ^ c, 0, keepdims=False) for c in range(GROUP)], axis=1
    )
    chunks = chunks.reshape(nodes, GROUP, planes, rows)
    filtered = jnp.transpose(chunks, (0, 2, 1, 3)).reshape(nodes, width)
    return filtered, outcome[1], outcome[0]


def solution(mesh):
    return jax.shard_map(
        shards,
        mesh=mesh,
        in_specs=(
            P("dom", "band"),
            P("dom", None, None),
            P(None, "dom"),
            P("dom", None),
            P("dom"),
            P("dom"),
            P(),
            P(),
        ),
        out_specs=(P("dom", "band"), P(("band", "dom"), None), P(("band", "dom"), None)),
        check_vma=False,
    )
```

time: 274 us -> 68.4 us (0.25)
  waiting for transfers between devices: 180 us -> 22.6 us
  other arithmetic: 32 us -> 1.46 us
  local copies, waits for them, and re-layouts: 26.6 us -> 10.3 us
  between operations: 16 us -> 2.23 us
  Pallas kernels: 0 us -> 8.55 us
  starting transfers between devices: 16.3 us -> 21.7 us
    reduce_scatter x2 -> x0, waiting for transfers between devices: 123 us -> none  [the longest x1 75.5 us: shards(): lax.psum_scatter(projected.astype(jnp.bfloat16), 'dom', scatter_dimension...]
    ppermute x12 -> x16, waiting for transfers between devices: 56.2 us -> 22.6 us  [the longest x7 11.3 us: to_plane(): return lax.ppermute(block, 'dom', route)]
    scatter-add x10 -> x0, other arithmetic: 25.8 us -> none  [the longest x5 19.7 us: hamilton(): summed.at[cell_nodes.reshape(-1)].add(cell_out.reshape(-1, columns))]
    gather x15 -> x0, local copies, waits for them, and re-layouts: 15.2 us -> none  [the longest x10 11.7 us: hamilton(): gathered = extended[cell_nodes]]
    pallas_call x0 -> x4, Pallas kernels: none -> 8.55 us  [call(): pl.pallas_call(kernel, out_shape=[jax.ShapeDtypeStruct(shape, dtype) for...]
    ppermute x12 -> x16, starting transfers between devices: 16.3 us -> 21.7 us  [the longest x7 13 us: to_plane(): return lax.ppermute(block, 'dom', route)]
    reshape x6 -> x0, local copies, waits for them, and re-layouts: 3.85 us -> none  [the longest x5 3.74 us: hamilton(): cell_out.reshape(-1, columns)]
    transpose x5 -> x1, local copies, waits for them, and re-layouts: 3.31 us -> 0.02 us  [shards(): filtered = jnp.transpose(chunks, (0, 2, 1, 3)).reshape(nodes, width)]
  transfers between devices with their start and end apart: 14 -> 16, of which waited for: 14 -> 10; matrix products, arithmetic and copies ran while one was open for 5% -> 2% of each run, Pallas kernels for 0% -> 1%
where the time goes in v1:
time: 68.4 us; the launch traced here: 67.6 us
  waiting for transfers between devices  22.6 us (33%)
  starting transfers between devices  21.7 us (32%)
  local copies, waits for them, and re-layouts  10.3 us (15%)
  Pallas kernels  8.55 us (12%)
  between operations  2.23 us (3%)
  other arithmetic  1.46 us (2%)
  matrix products  0.74 us (1%)
    ppermute x7, starting transfers between devices, to_plane(): return lax.ppermute(block, 'dom', route)  13 us
    ppermute x7, waiting for transfers between devices, to_plane(): return lax.ppermute(block, 'dom', route)  11.3 us
    ppermute x6, waiting for transfers between devices, in_plane(): return lax.ppermute(block, 'dom', [(i, i ^ k) for i in everyone])  10 us
    pallas_call x4, Pallas kernels, call(): pl.pallas_call(kernel, out_shape=[jax.ShapeDtypeStruct(shape, dtype) for...  8.55 us
    ppermute x6, starting transfers between devices, in_plane(): return lax.ppermute(block, 'dom', [(i, i ^ k) for i in everyone])  8.1 us
    unnamed x12, local copies, waits for them, and re-layouts  5.54 us
    squeeze x2, local copies, waits for them, and re-layouts, shards(): return (filtered, outcome[1], outcome[0])  2.17 us
    another operation x8, local copies, waits for them, and re-layouts, shards(): jnp.stack([lax.dynamic_index_in_dim(lax.dynamic_index_in_dim(stacked, (b...  1.72 us
  transfers between devices with their start and end apart: 16, of which 10 were waited for; matrix products, arithmetic and copies ran while one was open for 2% of the time, Pallas kernels for 1%

profile of v1, /device:TPU:0, one launch (start us, length us, event | category | flops | bytes accessed | tf_op | source)
XLA Modules:
  0.0 67.6 jit_solution(8742771831405058217)
XLA Ops:
  2.4 0.9 %copy-done = bf16[256,512]{1,0:T(8,128)(2,1)S(1)} copy-done((bf16[256,512]{1,0:T(8,128)(2,1)S(1)}, bf16[256,512]{1,0:T(8,128)(2,1)}, u32[]{:S(2)}) %copy-start) | copy-done | bytes 262168
  5.8 3.0 %collective-permute-start = (bf16[800,128]{1,0:T(8,128)(2,1)S(1)}, bf16[800,128]{1,0:T(8,128)(2,1)S(1)}, u32[]{:S(2)}, u32[]{:S(2)}) collective-permute-start(bf16[800,128]{1,0:T(8,128)(2,1)S(1)} %get-tuple-element.20), channel_id=1, source_target_pairs={{0,1},{1,0},{2,3},{3,2},{4,5},{5,4},{6,7},{7,6},{8,9},{9,8},{10,11... | collective-permute-start | bytes 614408 | tf_op jit(solution)/shard_map/ppermute | solution.py:331
  8.8 1.5 %collective-permute-start.1 = (bf16[800,128]{1,0:T(8,128)(2,1)S(1)}, bf16[800,128]{1,0:T(8,128)(2,1)S(1)}, u32[]{:S(2)}, u32[]{:S(2)}) collective-permute-start(bf16[800,128]{1,0:T(8,128)(2,1)S(1)} %get-tuple-element.21), channel_id=1, source_target_pairs={{0,2},{1,3},{2,0},{3,1},{4,6},{5,7},{6,4},{7,5},{8,10},{9,11},{10,... | collective-permute-start | bytes 614408 | tf_op jit(solution)/shard_map/ppermute | solution.py:331
  11.7 3.1 %collective-permute-done.m1 = bf16[800,128]{1,0:T(8,128)(2,1)S(1)} collective-permute-done((bf16[800,128]{1,0:T(8,128)(2,1)S(1)}, bf16[800,128]{1,0:T(8,128)(2,1)S(1)}, u32[]{:S(2)}, u32[]{:S(2)}) %collective-permute-start) | collective-permute-done | bytes 204832 | tf_op jit(solution)/shard_map/ppermute | solution.py:331
  14.7 5.0 %collective-permute-done.1.m2 = bf16[800,128]{1,0:T(8,128)(2,1)S(1)} collective-permute-done((bf16[800,128]{1,0:T(8,128)(2,1)S(1)}, bf16[800,128]{1,0:T(8,128)(2,1)S(1)}, u32[]{:S(2)}, u32[]{:S(2)}) %collective-permute-start.1) | collective-permute-done | bytes 204832 | tf_op jit(solution)/shard_map/ppermute | solution.py:331
  19.7 4.8 %shard_map.104 = (bf16[4,256,256]{2,1,0:T(8,128)(2,1)S(1)}, bf16[4,128,256]{2,1,0:T(8,128)(2,1)S(1)}, bf16[4,256,128]{2,1,0:T(8,128)(2,1)S(1)}, f32[1024,128]{1,...) custom-call(s32[1]{0:T(128)} %bitcast.place_ref, ...), custom_call_target="tpu_custom_call" | custom-call | flops 1073741824 | bytes 2097152 | tf_op jit(solution)/shard_map/pallas_call | solution.py:299
  24.6 1.6 %collective-permute-start.3 = (bf16[384,128]{1,0:T(8,128)(2,1)S(1)}, bf16[384,128]{1,0:T(8,128)(2,1)S(1)}, u32[]{:S(2)}, u32[]{:S(2)}) collective-permute-start(bf16[384,128]{1,0:T(8,128)(2,1)S(1)} %get-tuple-element.30.sent_ref), channel_id=1, source_target_pairs={{0,4},{1,5},{2,6},{3,7},{4,8},{5,9},{6,10},{7,11},{8,12},{9,13},{1... | collective-permute-start | bytes 294920 | tf_op jit(solution)/shard_map/ppermute | solution.py:335
  26.2 2.2 %collective-permute-start.4 = (bf16[384,128]{1,0:T(8,128)(2,1)S(1)}, bf16[384,128]{1,0:T(8,128)(2,1)S(1)}, u32[]{:S(2)}, u32[]{:S(2)}) collective-permute-start(bf16[384,128]{1,0:T(8,128)(2,1)S(1)} %get-tuple-element.31), channel_id=1, source_target_pairs={{0,12},{1,13},{2,14},{3,15},{4,0},{5,1},{6,2},{7,3},{8,4},{9,5},{1... | collective-permute-start | bytes 294920 | tf_op jit(solution)/shard_map/ppermute | solution.py:335
  28.5 3.0 %collective-permute-done.3.below_ref.corner_ref = bf16[384,128]{1,0:T(8,128)(2,1)S(1)} collective-permute-done((bf16[384,128]{1,0:T(8,128)(2,1)S(1)}, bf16[384,128]{1,0:T(8,128)(2,1)S(1)}, u32[]{:S(2)}, u32[]{:S(2)}) %collective-permute-start.3) | collective-permute-done | bytes 98336 | tf_op jit(solution)/shard_map/ppermute | solution.py:335
  31.9 2.6 %shard_map.105 = (bf16[1024,128]{1,0:T(8,128)(2,1)S(1)}, bf16[64,128]{1,0:T(8,128)(2,1)S(1)}, bf16[64,128]{1,0:T(8,128)(2,1)S(1)}) custom-call(bf16[4,256,256]{2,1,0:T(8,128)(2,1)S(1)} %get-tuple-element.23.own_ref, bf16[4,128,256]{2,1,0:T(8,128)(2,1)S(1)} %get-tuple-element.24.down_ref, bf16[4,256,128]{2,1,0:T(8,128)(2,1)S(1)} %get-tuple-element.25.up_ref, ...), custom_call_target="tpu_custom_call" | custom-call | flops 1073741824 | bytes 2097152 | tf_op jit(solution)/shard_map/pallas_call | solution.py:299
  34.5 1.3 %collective-permute-start.5 = (bf16[1024,128]{1,0:T(8,128)(2,1)S(1)}, bf16[1024,128]{1,0:T(8,128)(2,1)S(1)}, u32[]{:S(2)}, u32[]{:S(2)}) collective-permute-start(bf16[1024,128]{1,0:T(8,128)(2,1)S(1)} %get-tuple-element.32.filtered_ref), channel_id=1, source_target_pairs={{0,1},{1,0},{2,3},{3,2},{4,5},{5,4},{6,7},{7,6},{8,9},{9,8},{10,11... | collective-permute-start | bytes 786440 | tf_op jit(solution)/shard_map/ppermute | solution.py:331
  36.6 1.4 %collective-permute-start.7 = (bf16[1024,128]{1,0:T(8,128)(2,1)S(1)}, bf16[1024,128]{1,0:T(8,128)(2,1)S(1)}, u32[]{:S(2)}, u32[]{:S(2)}) collective-permute-start(bf16[1024,128]{1,0:T(8,128)(2,1)S(1)} %get-tuple-element.32.filtered_ref), channel_id=1, source_target_pairs={{0,3},{1,2},{2,1},{3,0},{4,7},{5,6},{6,5},{7,4},{8,11},{9,10},{10,... | collective-permute-start | bytes 786440 | tf_op jit(solution)/shard_map/ppermute | solution.py:331
  38.0 1.1 %collective-permute-start.8 = (bf16[64,128]{1,0:T(8,128)(2,1)S(1)}, bf16[64,128]{1,0:T(8,128)(2,1)S(1)}, u32[]{:S(2)}, u32[]{:S(2)}) collective-permute-start(bf16[64,128]{1,0:T(8,128)(2,1)S(1)} %get-tuple-element.33), channel_id=1, source_target_pairs={{0,4},{1,5},{2,6},{3,7},{4,8},{5,9},{6,10},{7,11},{8,12},{9,13},{1... | collective-permute-start | bytes 49160 | tf_op jit(solution)/shard_map/ppermute | solution.py:335
  39.2 2.7 %collective-permute-start.9 = (bf16[64,128]{1,0:T(8,128)(2,1)S(1)}, bf16[64,128]{1,0:T(8,128)(2,1)S(1)}, u32[]{:S(2)}, u32[]{:S(2)}) collective-permute-start(bf16[64,128]{1,0:T(8,128)(2,1)S(1)} %get-tuple-element.34), channel_id=1, source_target_pairs={{0,12},{1,13},{2,14},{3,15},{4,0},{5,1},{6,2},{7,3},{8,4},{9,5},{1... | collective-permute-start | bytes 49160 | tf_op jit(solution)/shard_map/ppermute | solution.py:335
  41.9 1.7 %collective-permute-done.8.below_ref = bf16[64,128]{1,0:T(8,128)(2,1)S(1)} collective-permute-done((bf16[64,128]{1,0:T(8,128)(2,1)S(1)}, bf16[64,128]{1,0:T(8,128)(2,1)S(1)}, u32[]{:S(2)}, u32[]{:S(2)}) %collective-permute-start.8) | collective-permute-done | bytes 16416 | tf_op jit(solution)/shard_map/ppermute | solution.py:335
  45.1 1.9 %collective-permute-done.6 = bf16[1024,128]{1,0:T(8,128)(2,1)S(1)} collective-permute-done((bf16[1024,128]{1,0:T(8,128)(2,1)S(1)}, bf16[1024,128]{1,0:T(8,128)(2,1)S(1)}, u32[]{:S(2)}, u32[]{:S(2)}) %collective-permute-start.6) | collective-permute-done | bytes 262176 | tf_op jit(solution)/shard_map/ppermute | solution.py:331
  48.3 1.5 %collective-permute-start.12 = (bf16[4,32,512]{2,1,0:T(8,128)(2,1)S(1)}, bf16[4,32,512]{2,1,0:T(8,128)(2,1)S(1)}, u32[]{:S(2)}, u32[]{:S(2)}) collective-permute-start(bf16[4,32,512]{2,1,0:T(8,128)(2,1)S(1)} %get-tuple-element.40), channel_id=1, source_target_pairs={{0,4},{1,5},{2,6},{3,7},{4,8},{5,9},{6,10},{7,11},{8,12},{9,13},{1... | collective-permute-start | bytes 393224 | tf_op jit(solution)/shard_map/ppermute | solution.py:335
  49.8 3.1 %collective-permute-start.13 = (bf16[4,32,512]{2,1,0:T(8,128)(2,1)S(1)}, bf16[4,32,512]{2,1,0:T(8,128)(2,1)S(1)}, u32[]{:S(2)}, u32[]{:S(2)}) collective-permute-start(bf16[4,32,512]{2,1,0:T(8,128)(2,1)S(1)} %get-tuple-element.42), channel_id=1, source_target_pairs={{0,8},{1,9},{2,10},{3,11},{4,12},{5,13},{6,14},{7,15},{8,0},{9,1},... | collective-permute-start | bytes 393224 | tf_op jit(solution)/shard_map/ppermute | solution.py:335
  54.5 2.4 %collective-permute-done.12 = bf16[4,32,512]{2,1,0:T(8,128)(2,1)S(1)} collective-permute-done((bf16[4,32,512]{2,1,0:T(8,128)(2,1)S(1)}, bf16[4,32,512]{2,1,0:T(8,128)(2,1)S(1)}, u32[]{:S(2)}, u32[]{:S(2)}) %collective-permute-start.12) | collective-permute-done | bytes 131104 | tf_op jit(solution)/shard_map/ppermute | solution.py:335
  56.9 3.7 %collective-permute-done.13 = bf16[4,32,512]{2,1,0:T(8,128)(2,1)S(1)} collective-permute-done((bf16[4,32,512]{2,1,0:T(8,128)(2,1)S(1)}, bf16[4,32,512]{2,1,0:T(8,128)(2,1)S(1)}, u32[]{:S(2)}, u32[]{:S(2)}) %collective-permute-start.13) | collective-permute-done | bytes 131104 | tf_op jit(solution)/shard_map/ppermute | solution.py:335
  60.9 1.3 %collective-permute-done.15 = f32[2,32,512]{2,1,0:T(8,128)S(1)} collective-permute-done((f32[2,32,512]{2,1,0:T(8,128)S(1)}, f32[2,32,512]{2,1,0:T(8,128)S(1)}, u32[]{:S(2)}, u32[]{:S(2)}) %collective-permute-start.15) | collective-permute-done | bytes 131104 | tf_op jit(solution)/shard_map/ppermute | solution.py:338
  64.1 1.2 %fusion.15 = f32[2,32,2,4,4,32]{5,4,3,2,1,0:T(4,128)S(1)} fusion(f32[2,32,1,1,4,32]{5,3,4,2,1,0:T(1,128)S(1)} %stack.94, f32[2,32,1,1,4,32]{5,3,4,2,1,0:T(1,128)S(1)} %stack.93, f32[2,32,1,1,4,32]{5,3,4,2,1,0:T(1,128)S(1)} %stack.92, f32[2,32,1,1,4,32]{5,3,4,2,1,0:T(1,128)S(1)} %stack.91, f32[2,32,1,1,4,32]{5,3,4,2,1,0:T(1,128)S(1)} %stack.89, ...), kind=kLoop, calls=%fused_computation.17 | loop fusion | flops 524288 | bytes 524288 | tf_op jit(solution)/shard_map/mul | solution.py:423
  65.4 1.1 %squeeze.43 = f32[32,1024]{1,0:T(8,128)} reshape(f32[1,32,2,4,4,32]{5,4,3,2,1,0:T(4,128)S(1)} %get-tuple-element.39) | data formatting | bytes 262144 | tf_op jit(solution)/shard_map/squeeze | solution.py:432
  66.5 1.1 %squeeze.44 = f32[32,1024]{1,0:T(8,128)} reshape(f32[1,32,2,4,4,32]{5,4,3,2,1,0:T(4,128)S(1)} %get-tuple-element.38) | data formatting | bytes 262144 | tf_op jit(solution)/shard_map/squeeze | solution.py:432
  (52 shorter events, 11.9 us)
Async XLA Ops:
  2.4 0.9 %copy-start = (bf16[256,512]{1,0:T(8,128)(2,1)S(1)}, bf16[256,512]{1,0:T(8,128)(2,1)}, u32[]{:S(2)}) copy-start(bf16[256,512]{1,0:T(8,128)(2,1)} %field_ref.1) | copy-start | bytes 786436
  3.3 0.7 %copy-start.1 = (f32[256]{0:T(256)S(1)}, f32[256]{0:T(256)}, u32[]{:S(2)}) copy-start(f32[256]{0:T(256)} %param.12) | copy-start | bytes 3076
  4.0 0.7 %copy-start.2 = (f32[256]{0:T(256)S(1)}, f32[256]{0:T(256)}, u32[]{:S(2)}) copy-start(f32[256]{0:T(256)} %param.13) | copy-start | bytes 3076
  4.7 0.7 copy-start.3
  5.8 8.9 %collective-permute-start = (bf16[800,128]{1,0:T(8,128)(2,1)S(1)}, bf16[800,128]{1,0:T(8,128)(2,1)S(1)}, u32[]{:S(2)}, u32[]{:S(2)}) collective-permute-start(bf16[800,128]{1,0:T(8,128)(2,1)S(1)} %get-tuple-element.20), channel_id=1, source_target_pairs={{0,1},{1,0},{2,3},{3,2},{4,5},{5,4},{6,7},{7,6},{8,9},{9,8},{10,11... | collective-permute-start | bytes 614408 | tf_op jit(solution)/shard_map/ppermute | solution.py:331
  8.8 10.9 %collective-permute-start.1 = (bf16[800,128]{1,0:T(8,128)(2,1)S(1)}, bf16[800,128]{1,0:T(8,128)(2,1)S(1)}, u32[]{:S(2)}, u32[]{:S(2)}) collective-permute-start(bf16[800,128]{1,0:T(8,128)(2,1)S(1)} %get-tuple-element.21), channel_id=1, source_target_pairs={{0,2},{1,3},{2,0},{3,1},{4,6},{5,7},{6,4},{7,5},{8,10},{9,11},{10,... | collective-permute-start | bytes 614408 | tf_op jit(solution)/shard_map/ppermute | solution.py:331
  10.3 9.4 %collective-permute-start.2 = (bf16[800,128]{1,0:T(8,128)(2,1)S(1)}, bf16[800,128]{1,0:T(8,128)(2,1)S(1)}, u32[]{:S(2)}, u32[]{:S(2)}) collective-permute-start(bf16[800,128]{1,0:T(8,128)(2,1)S(1)} %get-tuple-element.22), channel_id=1, source_target_pairs={{0,3},{1,2},{2,1},{3,0},{4,7},{5,6},{6,5},{7,4},{8,11},{9,10},{10,... | collective-permute-start | bytes 614408 | tf_op jit(solution)/shard_map/ppermute | solution.py:331
  24.6 6.9 %collective-permute-start.3 = (bf16[384,128]{1,0:T(8,128)(2,1)S(1)}, bf16[384,128]{1,0:T(8,128)(2,1)S(1)}, u32[]{:S(2)}, u32[]{:S(2)}) collective-permute-start(bf16[384,128]{1,0:T(8,128)(2,1)S(1)} %get-tuple-element.30.sent_ref), channel_id=1, source_target_pairs={{0,4},{1,5},{2,6},{3,7},{4,8},{5,9},{6,10},{7,11},{8,12},{9,13},{1... | collective-permute-start | bytes 294920 | tf_op jit(solution)/shard_map/ppermute | solution.py:335
  26.2 5.7 %collective-permute-start.4 = (bf16[384,128]{1,0:T(8,128)(2,1)S(1)}, bf16[384,128]{1,0:T(8,128)(2,1)S(1)}, u32[]{:S(2)}, u32[]{:S(2)}) collective-permute-start(bf16[384,128]{1,0:T(8,128)(2,1)S(1)} %get-tuple-element.31), channel_id=1, source_target_pairs={{0,12},{1,13},{2,14},{3,15},{4,0},{5,1},{6,2},{7,3},{8,4},{9,5},{1... | collective-permute-start | bytes 294920 | tf_op jit(solution)/shard_map/ppermute | solution.py:335
  34.5 10.5 %collective-permute-start.5 = (bf16[1024,128]{1,0:T(8,128)(2,1)S(1)}, bf16[1024,128]{1,0:T(8,128)(2,1)S(1)}, u32[]{:S(2)}, u32[]{:S(2)}) collective-permute-start(bf16[1024,128]{1,0:T(8,128)(2,1)S(1)} %get-tuple-element.32.filtered_ref), channel_id=1, source_target_pairs={{0,1},{1,0},{2,3},{3,2},{4,5},{5,4},{6,7},{7,6},{8,9},{9,8},{10,11... | collective-permute-start | bytes 786440 | tf_op jit(solution)/shard_map/ppermute | solution.py:331
  35.8 11.3 %collective-permute-start.6 = (bf16[1024,128]{1,0:T(8,128)(2,1)S(1)}, bf16[1024,128]{1,0:T(8,128)(2,1)S(1)}, u32[]{:S(2)}, u32[]{:S(2)}) collective-permute-start(bf16[1024,128]{1,0:T(8,128)(2,1)S(1)} %get-tuple-element.32.filtered_ref), channel_id=1, source_target_pairs={{0,2},{1,3},{2,0},{3,1},{4,6},{5,7},{6,4},{7,5},{8,10},{9,11},{10,... | collective-permute-start | bytes 786440 | tf_op jit(solution)/shard_map/ppermute | solution.py:331
  36.6 10.6 %collective-permute-start.7 = (bf16[1024,128]{1,0:T(8,128)(2,1)S(1)}, bf16[1024,128]{1,0:T(8,128)(2,1)S(1)}, u32[]{:S(2)}, u32[]{:S(2)}) collective-permute-start(bf16[1024,128]{1,0:T(8,128)(2,1)S(1)} %get-tuple-element.32.filtered_ref), channel_id=1, source_target_pairs={{0,3},{1,2},{2,1},{3,0},{4,7},{5,6},{6,5},{7,4},{8,11},{9,10},{10,... | collective-permute-start | bytes 786440 | tf_op jit(solution)/shard_map/ppermute | solution.py:331
  38.0 5.5 %collective-permute-start.8 = (bf16[64,128]{1,0:T(8,128)(2,1)S(1)}, bf16[64,128]{1,0:T(8,128)(2,1)S(1)}, u32[]{:S(2)}, u32[]{:S(2)}) collective-permute-start(bf16[64,128]{1,0:T(8,128)(2,1)S(1)} %get-tuple-element.33), channel_id=1, source_target_pairs={{0,4},{1,5},{2,6},{3,7},{4,8},{5,9},{6,10},{7,11},{8,12},{9,13},{1... | collective-permute-start | bytes 49160 | tf_op jit(solution)/shard_map/ppermute | solution.py:335
  39.2 4.4 %collective-permute-start.9 = (bf16[64,128]{1,0:T(8,128)(2,1)S(1)}, bf16[64,128]{1,0:T(8,128)(2,1)S(1)}, u32[]{:S(2)}, u32[]{:S(2)}) collective-permute-start(bf16[64,128]{1,0:T(8,128)(2,1)S(1)} %get-tuple-element.34), channel_id=1, source_target_pairs={{0,12},{1,13},{2,14},{3,15},{4,0},{5,1},{6,2},{7,3},{8,4},{9,5},{1... | collective-permute-start | bytes 49160 | tf_op jit(solution)/shard_map/ppermute | solution.py:335
  43.6 3.9 %collective-permute-start.11 = (bf16[1024,128]{1,0:T(8,128)(2,1)S(1)}, bf16[1024,128]{1,0:T(8,128)(2,1)S(1)}, u32[]{:S(2)}, u32[]{:S(2)}) collective-permute-start(bf16[1024,128]{1,0:T(8,128)(2,1)S(1)} %get-tuple-element.32.filtered_ref), channel_id=1, source_target_pairs={{0,16},{16,0},{1,17},{17,1},{2,18},{18,2},{3,19},{19,3},{4,20},{20... | collective-permute-start | bytes 786440 | tf_op jit(solution)/shard_map/ppermute | solution.py:338
  44.2 3.3 %collective-permute-start.10 = (bf16[1024,128]{1,0:T(8,128)(2,1)S(1)}, bf16[1024,128]{1,0:T(8,128)(2,1)S(1)}, u32[]{:S(2)}, u32[]{:S(2)}) collective-permute-start(bf16[1024,128]{1,0:T(8,128)(2,1)S(1)} %shard_map.106), channel_id=1, source_target_pairs={{0,16},{16,0},{1,17},{17,1},{2,18},{18,2},{3,19},{19,3},{4,20},{20... | collective-permute-start | bytes 786440 | tf_op jit(solution)/shard_map/ppermute | solution.py:338
  48.3 8.6 %collective-permute-start.12 = (bf16[4,32,512]{2,1,0:T(8,128)(2,1)S(1)}, bf16[4,32,512]{2,1,0:T(8,128)(2,1)S(1)}, u32[]{:S(2)}, u32[]{:S(2)}) collective-permute-start(bf16[4,32,512]{2,1,0:T(8,128)(2,1)S(1)} %get-tuple-element.40), channel_id=1, source_target_pairs={{0,4},{1,5},{2,6},{3,7},{4,8},{5,9},{6,10},{7,11},{8,12},{9,13},{1... | collective-permute-start | bytes 393224 | tf_op jit(solution)/shard_map/ppermute | solution.py:335
  49.8 10.8 %collective-permute-start.13 = (bf16[4,32,512]{2,1,0:T(8,128)(2,1)S(1)}, bf16[4,32,512]{2,1,0:T(8,128)(2,1)S(1)}, u32[]{:S(2)}, u32[]{:S(2)}) collective-permute-start(bf16[4,32,512]{2,1,0:T(8,128)(2,1)S(1)} %get-tuple-element.42), channel_id=1, source_target_pairs={{0,8},{1,9},{2,10},{3,11},{4,12},{5,13},{6,14},{7,15},{8,0},{9,1},... | collective-permute-start | bytes 393224 | tf_op jit(solution)/shard_map/ppermute | solution.py:335
  52.9 7.7 %collective-permute-start.14 = (bf16[4,32,512]{2,1,0:T(8,128)(2,1)S(1)}, bf16[4,32,512]{2,1,0:T(8,128)(2,1)S(1)}, u32[]{:S(2)}, u32[]{:S(2)}) collective-permute-start(bf16[4,32,512]{2,1,0:T(8,128)(2,1)S(1)} %get-tuple-element.41), channel_id=1, source_target_pairs={{0,12},{1,13},{2,14},{3,15},{4,0},{5,1},{6,2},{7,3},{8,4},{9,5},{1... | collective-permute-start | bytes 393224 | tf_op jit(solution)/shard_map/ppermute | solution.py:335
  60.8 1.4 %collective-permute-start.15 = (f32[2,32,512]{2,1,0:T(8,128)S(1)}, f32[2,32,512]{2,1,0:T(8,128)S(1)}, u32[]{:S(2)}, u32[]{:S(2)}) collective-permute-start(f32[2,32,512]{2,1,0:T(8,128)S(1)} %get-tuple-element.55), channel_id=1, source_target_pairs={{0,16},{16,0},{1,17},{17,1},{2,18},{18,2},{3,19},{19,3},{4,20},{20... | collective-permute-start | bytes 393224 | tf_op jit(solution)/shard_map/ppermute | solution.py:338

commit v2 on v1

--- a/solution.py
+++ b/solution.py
@@ -13,7 +13,7 @@
 EXTRA = 32
 F32 = jnp.float32
 BF16 = jnp.bfloat16
-VMEM_LIMIT = 48 * 1024 * 1024
+VMEM_LIMIT = 20 * 1024 * 1024
 
 
 def dot(a, b):
@@ -36,39 +36,41 @@
     return high, middle, low
 
 
-def pack_kernel(planes, place_ref, field_ref, cells_ref, nodes_ref, shared_ref, mass_ref, pot_ref, *outs):
-    out_refs, turned = outs[:GROUP], outs[GROUP]
+def pack_kernel(planes, corners, place_ref, field_ref, cells_ref, small_ref, *refs):
+    out_refs, square = refs[:GROUP], refs[GROUP]
     place = place_ref[0]
     nodes, width = field_ref.shape
-    cells, corners, _ = cells_ref.shape
+    cells = cells_ref.shape[0]
     rows = LANES // planes
+    line, lane = iota((LANES, LANES), 0), iota((LANES, LANES), 1)
+    square[...] = jnp.zeros_like(square)
+    for c in range(cells):
+        square[c, 0:corners, 0:corners] = cells_ref[c].astype(F32)
+    for c in range(0, cells, 2):
+        first = square[c]
+        second = square[c + 1] if c + 1 < cells else jnp.zeros_like(first)
+        diagonal = 0.5 * jnp.sum(jnp.where(line == lane, second, 0.0), axis=0, keepdims=True)
+        packed = jnp.where(line < lane, first, jnp.where(line > lane, second, 0.5 * first))
+        packed = jnp.where(line == LANES - 1, diagonal, packed)
+        for out in out_refs:
+            out[nodes + c // 2 * LANES : nodes + (c // 2 + 1) * LANES, :] = packed.astype(BF16)
+    small = small_ref[...]
+    ids = small[0:cells, 0:LANES]
+    high = jnp.floor(ids * (1.0 / 64.0))
+    pieces = [high, ids - 64.0 * high, small[cells : cells + 1, 0:LANES]]
+    for j in (1, 2):
+        for part in split3(small[cells + j : cells + j + 1]):
+            pieces += [part[:, h * LANES : (h + 1) * LANES].astype(F32) for h in range(nodes // LANES)]
+    used = sum(piece.shape[0] for piece in pieces)
+    pieces.append(jnp.zeros((EXTRA - used, LANES), F32))
+    for out in out_refs:
+        out[nodes + (cells + 1) // 2 * LANES :, :] = jnp.concatenate(pieces, axis=0).astype(BF16)
     source = iota((width, LANES), 0)
     target = iota((width, LANES), 1)
-    turned[...] = jnp.zeros_like(turned)
-    turned[0:corners, 0:cells] = nodes_ref[...].astype(F32)
-    tables = jnp.transpose(turned[...])[0:8]
-    lane = iota((8, LANES), 1)
-    high = jnp.floor(tables * (1.0 / 64.0))
-    low = tables - 64.0 * high
-    high = jnp.where(lane < corners, high, -8.0)
-    shared = jnp.concatenate(
-        [shared_ref[...].astype(F32), jnp.zeros((1, LANES - shared_ref.shape[1]), F32)], axis=1
-    )
-    pieces = [high[0:cells], low[0:cells], shared]
-    for value_ref in (mass_ref, pot_ref):
-        pieces += [part.astype(F32) for part in split3(value_ref[...])]
-    used = sum(piece.shape[0] for piece in pieces)
-    pieces.append(jnp.zeros((EXTRA - used, LANES), F32))
-    extra = jnp.concatenate(pieces, axis=0).astype(BF16)
+    wanted = (target // rows) * (GROUP * rows) + target % rows
     for k in range(GROUP):
-        chunk = place ^ k
-        pick = (target // rows) * (GROUP * rows) + chunk * rows + target % rows == source
+        pick = wanted + (place ^ k) * rows == source
         out_refs[k][0:nodes, :] = dot(field_ref[...], pick.astype(F32).astype(BF16)).astype(BF16)
-        base = nodes
-        for c in range(cells):
-            out_refs[k][base + c * LANES : base + (c + 1) * LANES, :] = jnp.zeros((LANES, LANES), BF16)
-            out_refs[k][base + c * LANES : base + c * LANES + corners, 0:corners] = cells_ref[c]
-        out_refs[k][base + cells * LANES :, :] = extra
 
 
 def apply_plane(own, down, up, fields, outside_u, outside_g, keep=None):
@@ -96,46 +98,68 @@
     return sums, traces
 
 
-def first_kernel(
-    cells, shared, place_ref, center_ref, half_ref, m0, m1, m2, m3,
-    own_ref, down_ref, up_ref, mass_ref, scale_ref, diag_ref, start_ref, next_ref, previous_ref,
-    raw, corner, cur, prev,
+def build_kernel(
+    nodes, cells, corners, shared, center_ref, half_ref, ref, own_ref, corner_ref, up_ref, down_ref, mass_ref, scale_ref, diag_ref,
 ):
-    place = place_ref[0]
     center, half = center_ref[0], half_ref[0]
-    nodes = raw.shape[1]
     both = nodes + shared
     halves = nodes // LANES
-    for k, ref in enumerate((m0, m1, m2, m3)):
+    base = nodes + (cells + 1) // 2 * LANES
+    line, lane = iota((LANES, LANES), 0), iota((LANES, LANES), 1)
+    nothing = jnp.zeros((LANES, LANES), F32)
+    extra = ref[base : base + EXTRA, :].astype(F32)
+    ids = (64.0 * extra[0:cells] + extra[cells : 2 * cells]).astype(jnp.int32)
+    picks, parts = [], []
+    for c in range(cells):
+        square = ref[nodes + c // 2 * LANES : nodes + (c // 2 + 1) * LANES, :].astype(F32)
+        if c % 2 == 0:
+            matrix = jnp.where(line <= lane, square, nothing)
+        else:
+            matrix = jnp.where((line > lane) & (line < corners), square, nothing)
+            matrix = matrix + jnp.where(line == lane, square[LANES - 1 :], nothing)
+        pick = (iota((both, LANES), 0) == ids[c : c + 1]).astype(F32).astype(BF16)
+        picks.append(pick)
+        parts.append(dot(pick, matrix.astype(BF16)).astype(BF16))
+    total = dot_nt(jnp.concatenate(parts + picks, axis=1), jnp.concatenate(picks + parts, axis=1))
+    own_ref[...] = total[:nodes, :nodes]
+    corner_ref[...] = total[nodes:, nodes:]
+    own_shared = extra[2 * cells : 2 * cells + 1, 0:shared].astype(jnp.int32)
+    place_in = (iota((nodes, shared), 0) == own_shared).astype(F32)
+    sides = jnp.concatenate([total[:nodes, nodes:], place_in], axis=1)
+    up_ref[...] = sides.astype(BF16)
+    down_ref[...] = jnp.transpose(sides).astype(BF16)
+    row = 2 * cells + 1
+    for h in range(halves):
+        at = slice(h * LANES, (h + 1) * LANES)
+        mass_row = sum(extra[row + j * halves + h : row + j * halves + h + 1] for j in range(3))
+        off = row + 3 * halves
+        pot_row = sum(extra[off + j * halves + h : off + j * halves + h + 1] for j in range(3))
+        mass = jnp.transpose(jnp.broadcast_to(mass_row, (LANES, LANES)))
+        pot = jnp.transpose(jnp.broadcast_to(pot_row, (LANES, LANES)))
+        mass_ref[at, :] = mass
+        scale_ref[at, :] = mass / half
+        diag_ref[at, :] = (pot - center) / half
+
+
+def first_kernel(shared, place_ref, *refs):
+    messages, refs = refs[:GROUP], refs[GROUP:]
+    slabs = [refs[7 * k : 7 * k + 7] for k in range(GROUP)]
+    own_ref, down_ref, up_ref, mass_ref, scale_ref, diag_ref, start_ref = refs[7 * GROUP : 7 * GROUP + 7]
+    next_ref, previous_ref, raw, corner, cur, prev = refs[7 * GROUP + 7 :]
+    place = place_ref[0]
+    nodes = own_ref.shape[1]
+    for k in range(GROUP):
         slab = place ^ k
-        base = nodes + cells * LANES
-        extra = ref[base : base + EXTRA, :].astype(F32)
-        ids = (64.0 * extra[0:cells] + extra[cells : 2 * cells]).astype(jnp.int32)
-        total = jnp.zeros((both, both), F32)
-        for c in range(cells):
-            pick = (iota((both, LANES), 0) == ids[c : c + 1]).astype(F32).astype(BF16)
-            matrix = ref[nodes + c * LANES : nodes + (c + 1) * LANES, :]
-            half_way = dot(pick, matrix).astype(BF16)
-            total = total + dot_nt(half_way, pick)
-        raw[slab] = total[:nodes, :nodes]
-        corner[slab] = total[nodes:, nodes:]
-        own_shared = extra[2 * cells : 2 * cells + 1, 0:shared].astype(jnp.int32)
-        place_in = (iota((nodes, shared), 0) == own_shared).astype(F32)
-        sides = jnp.concatenate([total[:nodes, nodes:], place_in], axis=1)
-        up_ref[slab] = sides.astype(BF16)
-        down_ref[slab] = jnp.transpose(sides).astype(BF16)
-        row = 2 * cells + 1
-        for h in range(halves):
-            at = pl.ds(pl.multiple_of(slab * nodes + h * LANES, LANES), LANES)
-            mass_row = sum(extra[row + j * halves + h : row + j * halves + h + 1] for j in range(3))
-            off = row + 3 * halves
-            pot_row = sum(extra[off + j * halves + h : off + j * halves + h + 1] for j in range(3))
-            mass = jnp.transpose(jnp.broadcast_to(mass_row, (LANES, LANES)))
-            pot = jnp.transpose(jnp.broadcast_to(pot_row, (LANES, LANES)))
-            mass_ref[at, :] = mass
-            scale_ref[at, :] = mass / half
-            diag_ref[at, :] = (pot - center) / half
-        start_ref[pl.ds(pl.multiple_of(slab * nodes, nodes), nodes), :] = ref[0:nodes, :]
+        at = pl.ds(pl.multiple_of(slab * nodes, nodes), nodes)
+        own_k, corner_k, up_k, down_k, mass_k, scale_k, diag_k = slabs[k]
+        start_ref[at, :] = messages[k][0:nodes, :]
+        raw[slab] = own_k[...]
+        corner[slab] = corner_k[...]
+        up_ref[slab] = up_k[...]
+        down_ref[slab] = down_k[...]
+        mass_ref[at, :] = mass_k[...]
+        scale_ref[at, :] = scale_k[...]
+        diag_ref[at, :] = diag_k[...]
     own_ref[0] = raw[0].astype(BF16)
     for i in range(1, GROUP):
         place_in = up_ref[i][:, shared:]
@@ -293,18 +317,38 @@
         applied_ref[rows, :] = (mass_ref[rows, :] * sums[i] + pot * values[i]).astype(BF16)
 
 
-def call(kernel, outs, args, scalars=0, scratch=(), flops=0):
-    in_specs = [pl.BlockSpec(memory_space=pltpu.SMEM)] * scalars
-    in_specs += [pl.BlockSpec(memory_space=pltpu.VMEM)] * (len(args) - scalars)
+SPACES = {"s": pltpu.SMEM, "v": pltpu.VMEM, "a": pl.ANY}
+
+
+def call(kernel, outs, args, spaces=None, scratch=(), flops=0):
+    spaces = spaces or "v" * len(args)
     return pl.pallas_call(
         kernel,
         out_shape=[jax.ShapeDtypeStruct(shape, dtype) for shape, dtype in outs],
-        in_specs=in_specs,
+        in_specs=[pl.BlockSpec(memory_space=SPACES[space]) for space in spaces],
         out_specs=[pl.BlockSpec(memory_space=pltpu.VMEM)] * len(outs),
         scratch_shapes=list(scratch),
         compiler_params=pltpu.CompilerParams(vmem_limit_bytes=VMEM_LIMIT),
         cost_estimate=pl.CostEstimate(flops=flops, bytes_accessed=1 << 21, transcendentals=0),
     )(*args)
+
+
+def place_kernel(planes, factor, place_ref, band_ref, *refs):
+    pieces, outs = refs[:-2], refs[-2:]
+    place, band = place_ref[0], band_ref[0]
+    _, rows, width = pieces[0].shape
+    bands = len(pieces)
+    for j, piece in enumerate(pieces):
+        first = ((band + j) % bands) * width
+        for mat, out in enumerate(outs):
+            chunks = [
+                piece[mat, :, pl.ds(pl.multiple_of((place ^ c) * LANES, LANES), LANES)] * factor for c in range(GROUP)
+            ]
+            columns = [
+                jnp.concatenate([chunk[:, z * rows : (z + 1) * rows] for chunk in chunks], axis=1)
+                for z in range(planes)
+            ]
+            out[:, pl.ds(pl.multiple_of(first, LANES), width)] = jnp.concatenate(columns, axis=1)
 
 
 def contract(left, right):
@@ -318,7 +362,7 @@
     dom_count = lax.axis_size("dom")
     planes = dom_count // GROUP
     nodes, width = orbital_block.shape
-    cells = cell_matrices.shape[0]
+    cells, corners, _ = cell_matrices.shape
     shared = shared_nodes.shape[1]
     rows = width // dom_count
     here = lax.axis_index("dom")
@@ -334,32 +378,48 @@
         route = [(i, (i // GROUP + k) % planes * GROUP + i % GROUP) for i in everyone]
         return lax.ppermute(block, "dom", route)
 
+    def partner(index, k):
+        return index ^ k if planes & (planes - 1) == 0 else (2 * planes + k - index) % planes
+
     def to_band(block, k):
         return lax.ppermute(block, "band", [(i, (i + k) % band_count) for i in range(band_count)])
 
-    message = ((nodes + cells * LANES + EXTRA, LANES), BF16)
+    def line(values, fill):
+        return jnp.pad(values.astype(F32), ((0, 0), (0, nodes - values.shape[1])), constant_values=fill)
+
+    small = jnp.concatenate(
+        [line(cell_nodes.T, -512.0), line(shared_nodes, 0.0), inv_sqrt_mass[None], potential[None]], axis=0
+    )
     messages = call(
-        functools.partial(pack_kernel, planes),
-        [message] * GROUP,
-        (
-            place_arg, orbital_block, cell_matrices, cell_nodes, shared_nodes,
-            inv_sqrt_mass.reshape(-1, LANES), potential.reshape(-1, LANES),
-        ),
-        scalars=1,
-        scratch=[pltpu.VMEM((LANES, LANES), F32)],
+        functools.partial(pack_kernel, planes, corners),
+        [((nodes + (cells + 1) // 2 * LANES + EXTRA, LANES), BF16)] * GROUP,
+        (place_arg, orbital_block, cell_matrices, small),
+        spaces="svvv",
+        scratch=[pltpu.VMEM((cells, LANES, LANES), F32)],
     )
     messages = [messages[0]] + [in_plane(messages[k], k) for k in range(1, GROUP)]
+    slabs = []
+    for message in messages:
+        slabs += call(
+            functools.partial(build_kernel, nodes, cells, corners, shared),
+            [
+                ((nodes, nodes), F32), ((shared, shared), F32), ((nodes, 2 * shared), BF16), ((2 * shared, nodes), BF16),
+            ] + [((nodes, LANES), F32)] * 3,
+            (filter_center, filter_halfwidth, message),
+            spaces="ssv",
+            flops=1 << 28,
+        )
     height = GROUP * nodes
     column = ((height, LANES), F32)
     trace = ((FILTER_DEG * shared + 2 * shared, LANES), BF16)
     own, down, up, mass, scale, diag, start, next_msg, previous_msg = call(
-        functools.partial(first_kernel, cells, shared),
+        functools.partial(first_kernel, shared),
         [
             ((GROUP, nodes, nodes), BF16), ((GROUP, 2 * shared, nodes), BF16), ((GROUP, nodes, 2 * shared), BF16),
             column, column, column, ((height, LANES), BF16), trace, trace,
         ],
-        (place_arg, filter_center, filter_halfwidth, *messages),
-        scalars=3,
+        (place_arg, *messages, *slabs),
+        spaces="s" + "v" * (GROUP * 8),
         scratch=[
             pltpu.VMEM((GROUP, nodes, nodes), F32), pltpu.VMEM((GROUP, shared, shared), F32),
             pltpu.VMEM((height, 2 * LANES), F32), pltpu.VMEM((height, 2 * LANES), F32),
@@ -382,46 +442,36 @@
         functools.partial(third_kernel, shared),
         [((height, LANES), BF16)],
         (filter_center, filter_halfwidth, own, down, up, mass, diag, mine, below, below_now, above_now),
-        scalars=2,
+        spaces="ss" + "v" * 9,
         flops=1 << 28,
     )
 
+    applied, mine, *others = lax.optimization_barrier((applied, mine, *others))
     lefts = [applied] + [to_band(applied, k) for k in range(1, band_count)]
     lefts += [mine] + [to_band(mine, k) for k in range(1, band_count)]
     left = jnp.concatenate(lefts, axis=1)
-    right = jnp.concatenate([mine] + others, axis=1)
-    product = contract(left, right).reshape(2 * band_count, planes, rows, width)
-
-    def part_for(k):
-        return lax.dynamic_index_in_dim(product, (plane + k) % planes, 1, keepdims=False)
-
-    total = part_for(0)
-    for k in range(1, planes):
-        total = total + to_plane(part_for(k).astype(BF16), k).astype(F32)
-
-    total = total.reshape(2, band_count, rows, width)
-    own_rows = total[:, 0]
-    pieces = [own_rows] + [to_band(total[:, j], -j) for j in range(1, band_count)]
-    stacked = jnp.stack(pieces)
-    stacked = stacked.reshape(band_count, 2, rows, GROUP, LANES)
-    ordered = jnp.stack(
-        [
-            jnp.stack([
-                lax.dynamic_index_in_dim(
-                    lax.dynamic_index_in_dim(stacked, (b - band) % band_count, 0, keepdims=False),
-                    place ^ c, 2, keepdims=False,
-                )
-                for c in range(GROUP)
-            ], axis=2)
-            for b in range(band_count)
-        ],
-        axis=2,
-    )
-    ordered = ordered.reshape(2, rows, band_count, GROUP, planes, rows)
-    ordered = jnp.transpose(ordered, (0, 1, 2, 4, 3, 5)).reshape(2, rows, band_count * width)
-    factor = 1.0 / (nodes * dom_count)
-    outcome = ordered * factor
-
+    gathered = [mine] + others
+    totals = []
+    for part in ((0, 1, 2, 3),):
+        right = gathered[part[0]] if len(part) == 1 else jnp.concatenate([gathered[k] for k in part], axis=1)
+        product = contract(left, right).reshape(2 * band_count, planes, rows, len(part) * LANES)
+
+        def part_for(k, product=product):
+            return lax.dynamic_index_in_dim(product, partner(plane, k), 1, keepdims=False)
+
+        total = part_for(0)
+        for k in [*range(2, planes), 1]:
+            route = [(i, partner(i // GROUP, k) * GROUP + i % GROUP) for i in everyone]
+            total = total + lax.ppermute(part_for(k).astype(BF16), "dom", route).astype(F32)
+        totals.append(total)
+    total = jnp.concatenate(totals, axis=2).reshape(2, band_count, rows, width)
+    pieces = [total[:, 0]] + [to_band(total[:, j], -j) for j in range(1, band_count)]
+    projected, intersection = call(
+        functools.partial(place_kernel, planes, 1.0 / (nodes * dom_count)),
+        [((rows, band_count * width), F32)] * 2,
+        (place_arg, band.astype(jnp.int32).reshape(1), *pieces),
+        spaces="ss" + "v" * band_count,
+    )
     chunks = jnp.stack([mine] + others).reshape(GROUP, GROUP, nodes, LANES)
     chunks = lax.dynamic_index_in_dim(chunks, place, 1, keepdims=False)
     chunks = jnp.stack(
@@ -429,7 +479,7 @@
     )
     chunks = chunks.reshape(nodes, GROUP, planes, rows)
     filtered = jnp.transpose(chunks, (0, 2, 1, 3)).reshape(nodes, width)
-    return filtered, outcome[1], outcome[0]
+    return filtered, intersection, projected
 
 
 def solution(mesh):

time: 68.4 us -> 60.9 us (0.89)
  local copies, waits for them, and re-layouts: 10.3 us -> 3.42 us
  waiting for transfers between devices: 22.6 us -> 21.1 us
  Pallas kernels: 8.55 us -> 9.96 us
  other arithmetic: 1.46 us -> 2.28 us
  starting transfers between devices: 21.7 us -> 21 us
    ppermute x0 -> x3, waiting for transfers between devices: none -> 8.8 us  [shards(): lax.ppermute(part_for(k).astype(BF16), 'dom', route).astype(F32)]
    ppermute x7 -> x4, waiting for transfers between devices: 11.3 us -> 5.14 us  [to_plane(): return lax.ppermute(block, 'dom', route)]
    ppermute x7 -> x4, starting transfers between devices: 13 us -> 7.7 us  [to_plane(): return lax.ppermute(block, 'dom', route)]
    ppermute x0 -> x3, starting transfers between devices: none -> 4.62 us  [shards(): lax.ppermute(part_for(k).astype(BF16), 'dom', route).astype(F32)]
    ppermute x6, waiting for transfers between devices: 10 us -> 6.02 us  [in_plane(): return lax.ppermute(block, 'dom', [(i, i ^ k) for i in everyone])]
    unnamed x12 -> x4, local copies, waits for them, and re-layouts: 5.54 us -> 2.71 us
    squeeze x2 -> x0, local copies, waits for them, and re-layouts: 2.17 us -> none  [shards(): return (filtered, outcome[1], outcome[0])]
    another operation x11 -> x0, local copies, waits for them, and re-layouts: 1.83 us -> none  [the longest x8 1.72 us: shards(): jnp.stack([lax.dynamic_index_in_dim(lax.dynamic_index_in_dim(stacked, (b...]
  transfers between devices with their start and end apart: 16 -> 16, of which waited for: 10 -> 12; matrix products, arithmetic and copies ran while one was open for 2% -> 3% of each run, Pallas kernels for 1% -> 5%
where the time goes in v2:
time: 60.9 us; the launch traced here: 60.6 us
  waiting for transfers between devices  21.1 us (35%)
  starting transfers between devices  21 us (34%)
  Pallas kernels  9.96 us (16%)
  local copies, waits for them, and re-layouts  3.42 us (6%)
  other arithmetic  2.28 us (4%)
  between operations  2.12 us (3%)
  matrix products  0.73 us (1%)
    pallas_call x9, Pallas kernels, call(): pl.pallas_call(kernel, out_shape=[jax.ShapeDtypeStruct(shape, dtype) for...  9.96 us
    ppermute x3, waiting for transfers between devices, shards(): lax.ppermute(part_for(k).astype(BF16), 'dom', route).astype(F32)  8.8 us
    ppermute x6, starting transfers between devices, in_plane(): return lax.ppermute(block, 'dom', [(i, i ^ k) for i in everyone])  8.1 us
    ppermute x4, starting transfers between devices, to_plane(): return lax.ppermute(block, 'dom', route)  7.7 us
    ppermute x6, waiting for transfers between devices, in_plane(): return lax.ppermute(block, 'dom', [(i, i ^ k) for i in everyone])  6.02 us
    ppermute x4, waiting for transfers between devices, to_plane(): return lax.ppermute(block, 'dom', route)  5.14 us
    ppermute x3, starting transfers between devices, shards(): lax.ppermute(part_for(k).astype(BF16), 'dom', route).astype(F32)  4.62 us
    unnamed x4, local copies, waits for them, and re-layouts  2.71 us
  transfers between devices with their start and end apart: 16, of which 12 were waited for; matrix products, arithmetic and copies ran while one was open for 3% of the time, Pallas kernels for 5%

profile of v2, /device:TPU:0, one launch (start us, length us, event | category | flops | bytes accessed | tf_op | source)
XLA Modules:
  0.0 60.6 jit_solution(5145937751656728799)
XLA Ops:
  0.6 0.9 %copy.14.cells_ref = bf16[4,125,125]{2,1,0:T(8,128)(2,1)S(1)} copy(bf16[4,125,125]{2,0,1:T(4,128)(2,1)} %param.9) | data formatting | bytes 250000 | tf_op args[1]
  3.6 0.9 %copy-done = bf16[256,512]{1,0:T(8,128)(2,1)S(1)} copy-done((bf16[256,512]{1,0:T(8,128)(2,1)S(1)}, bf16[256,512]{1,0:T(8,128)(2,1)}, u32[]{:S(2)}) %copy-start) | copy-done | bytes 262168
  5.1 3.0 %collective-permute-start = (bf16[544,128]{1,0:T(8,128)(2,1)S(1)}, bf16[544,128]{1,0:T(8,128)(2,1)S(1)}, u32[]{:S(2)}, u32[]{:S(2)}) collective-permute-start(bf16[544,128]{1,0:T(8,128)(2,1)S(1)} %get-tuple-element.55), channel_id=1, source_target_pairs={{0,1},{1,0},{2,3},{3,2},{4,5},{5,4},{6,7},{7,6},{8,9},{9,8},{10,11... | collective-permute-start | bytes 417800 | tf_op jit(solution)/shard_map/ppermute | solution.py:375
  8.1 1.5 %collective-permute-start.1 = (bf16[544,128]{1,0:T(8,128)(2,1)S(1)}, bf16[544,128]{1,0:T(8,128)(2,1)S(1)}, u32[]{:S(2)}, u32[]{:S(2)}) collective-permute-start(bf16[544,128]{1,0:T(8,128)(2,1)S(1)} %get-tuple-element.56), channel_id=1, source_target_pairs={{0,2},{1,3},{2,0},{3,1},{4,6},{5,7},{6,4},{7,5},{8,10},{9,11},{10,... | collective-permute-start | bytes 417800 | tf_op jit(solution)/shard_map/ppermute | solution.py:375
  10.9 0.7 %shard_map.104 = (f32[256,256]{1,0:T(8,128)S(1)}, f32[64,64]{1,0:T(8,128)S(1)}, bf16[256,128]{1,0:T(8,128)(2,1)S(1)}, bf16[128,256]{1,0:T(8,128)(2,1)S(1)}, f32[...) custom-call(f32[1]{0:T(128)S(6)} %copy.31.center_ref, f32[1]{0:T(128)S(6)} %copy.32.half_ref, ...), custom_call_target="tpu_custom_call" | custom-call | flops 268435456 | bytes 2097152 | tf_op jit(solution)/shard_map/pallas_call | solution.py:325
  12.9 3.3 %collective-permute-done.1.ref.refs_2_ = bf16[544,128]{1,0:T(8,128)(2,1)S(1)} collective-permute-done((bf16[544,128]{1,0:T(8,128)(2,1)S(1)}, bf16[544,128]{1,0:T(8,128)(2,1)S(1)}, u32[]{:S(2)}, u32[]{:S(2)}) %collective-permute-start.1) | collective-permute-done | bytes 139296 | tf_op jit(solution)/shard_map/ppermute | solution.py:375
  17.0 0.7 %shard_map.107 = (f32[256,256]{1,0:T(8,128)S(1)}, f32[64,64]{1,0:T(8,128)S(1)}, bf16[256,128]{1,0:T(8,128)(2,1)S(1)}, bf16[128,256]{1,0:T(8,128)(2,1)S(1)}, f32[...) custom-call(f32[1]{0:T(128)S(6)} %copy.31.center_ref, f32[1]{0:T(128)S(6)} %copy.32.half_ref, ...), custom_call_target="tpu_custom_call" | custom-call | flops 268435456 | bytes 2097152 | tf_op jit(solution)/shard_map/pallas_call | solution.py:325
  17.7 2.3 %shard_map.108 = (bf16[4,256,256]{2,1,0:T(8,128)(2,1)S(1)}, bf16[4,128,256]{2,1,0:T(8,128)(2,1)S(1)}, bf16[4,256,128]{2,1,0:T(8,128)(2,1)S(1)}, f32[1024,128]{1,...) custom-call(s32[1]{0:T(128)} %bitcast.place_ref, ...), custom_call_target="tpu_custom_call" | custom-call | flops 1073741824 | bytes 2097152 | tf_op jit(solution)/shard_map/pallas_call | solution.py:325
  20.0 1.6 %collective-permute-start.3 = (bf16[384,128]{1,0:T(8,128)(2,1)S(1)}, bf16[384,128]{1,0:T(8,128)(2,1)S(1)}, u32[]{:S(2)}, u32[]{:S(2)}) collective-permute-start(bf16[384,128]{1,0:T(8,128)(2,1)S(1)} %get-tuple-element.93.sent_ref), channel_id=1, source_target_pairs={{0,4},{1,5},{2,6},{3,7},{4,8},{5,9},{6,10},{7,11},{8,12},{9,13},{1... | collective-permute-start | bytes 294920 | tf_op jit(solution)/shard_map/ppermute | solution.py:379
  21.6 2.2 %collective-permute-start.4 = (bf16[384,128]{1,0:T(8,128)(2,1)S(1)}, bf16[384,128]{1,0:T(8,128)(2,1)S(1)}, u32[]{:S(2)}, u32[]{:S(2)}) collective-permute-start(bf16[384,128]{1,0:T(8,128)(2,1)S(1)} %get-tuple-element.94), channel_id=1, source_target_pairs={{0,12},{1,13},{2,14},{3,15},{4,0},{5,1},{6,2},{7,3},{8,4},{9,5},{1... | collective-permute-start | bytes 294920 | tf_op jit(solution)/shard_map/ppermute | solution.py:379
  23.9 2.7 %collective-permute-done.3.below_ref.corner_ref = bf16[384,128]{1,0:T(8,128)(2,1)S(1)} collective-permute-done((bf16[384,128]{1,0:T(8,128)(2,1)S(1)}, bf16[384,128]{1,0:T(8,128)(2,1)S(1)}, u32[]{:S(2)}, u32[]{:S(2)}) %collective-permute-start.3) | collective-permute-done | bytes 98336 | tf_op jit(solution)/shard_map/ppermute | solution.py:379
  27.3 2.6 %shard_map.109 = (bf16[1024,128]{1,0:T(8,128)(2,1)S(1)}, bf16[64,128]{1,0:T(8,128)(2,1)S(1)}, bf16[64,128]{1,0:T(8,128)(2,1)S(1)}) custom-call(bf16[4,256,256]{2,1,0:T(8,128)(2,1)S(1)} %get-tuple-element.86.own_ref, bf16[4,128,256]{2,1,0:T(8,128)(2,1)S(1)} %get-tuple-element.87.down_ref, bf16[4,256,128]{2,1,0:T(8,128)(2,1)S(1)} %get-tuple-element.88.up_ref, ...), custom_call_target="tpu_custom_call" | custom-call | flops 1073741824 | bytes 2097152 | tf_op jit(solution)/shard_map/pallas_call | solution.py:325
  30.5 1.6 %collective-permute-start.8 = (bf16[1024,128]{1,0:T(8,128)(2,1)S(1)}, bf16[1024,128]{1,0:T(8,128)(2,1)S(1)}, u32[]{:S(2)}, u32[]{:S(2)}) collective-permute-start(bf16[1024,128]{1,0:T(8,128)(2,1)S(1)} %get-tuple-element.98.filtered_ref), channel_id=1, source_target_pairs={{0,2},{1,3},{2,0},{3,1},{4,6},{5,7},{6,4},{7,5},{8,10},{9,11},{10,... | collective-permute-start | bytes 786440 | tf_op jit(solution)/shard_map/ppermute | solution.py:375
  32.1 1.4 %collective-permute-start.9 = (bf16[1024,128]{1,0:T(8,128)(2,1)S(1)}, bf16[1024,128]{1,0:T(8,128)(2,1)S(1)}, u32[]{:S(2)}, u32[]{:S(2)}) collective-permute-start(bf16[1024,128]{1,0:T(8,128)(2,1)S(1)} %get-tuple-element.98.filtered_ref), channel_id=1, source_target_pairs={{0,3},{1,2},{2,1},{3,0},{4,7},{5,6},{6,5},{7,4},{8,11},{9,10},{10,... | collective-permute-start | bytes 786440 | tf_op jit(solution)/shard_map/ppermute | solution.py:375
  33.5 0.8 %collective-permute-start.5 = (bf16[64,128]{1,0:T(8,128)(2,1)S(1)}, bf16[64,128]{1,0:T(8,128)(2,1)S(1)}, u32[]{:S(2)}, u32[]{:S(2)}) collective-permute-start(bf16[64,128]{1,0:T(8,128)(2,1)S(1)} %get-tuple-element.96), channel_id=1, source_target_pairs={{0,4},{1,5},{2,6},{3,7},{4,8},{5,9},{6,10},{7,11},{8,12},{9,13},{1... | collective-permute-start | bytes 49160 | tf_op jit(solution)/shard_map/ppermute | solution.py:379
  34.3 3.0 %collective-permute-start.6 = (bf16[64,128]{1,0:T(8,128)(2,1)S(1)}, bf16[64,128]{1,0:T(8,128)(2,1)S(1)}, u32[]{:S(2)}, u32[]{:S(2)}) collective-permute-start(bf16[64,128]{1,0:T(8,128)(2,1)S(1)} %get-tuple-element.97), channel_id=1, source_target_pairs={{0,12},{1,13},{2,14},{3,15},{4,0},{5,1},{6,2},{7,3},{8,4},{9,5},{1... | collective-permute-start | bytes 49160 | tf_op jit(solution)/shard_map/ppermute | solution.py:379
  37.3 1.7 %collective-permute-done.5.below_ref = bf16[64,128]{1,0:T(8,128)(2,1)S(1)} collective-permute-done((bf16[64,128]{1,0:T(8,128)(2,1)S(1)}, bf16[64,128]{1,0:T(8,128)(2,1)S(1)}, u32[]{:S(2)}, u32[]{:S(2)}) %collective-permute-start.5) | collective-permute-done | bytes 16416 | tf_op jit(solution)/shard_map/ppermute | solution.py:379
  40.1 1.8 %collective-permute-done.9 = bf16[1024,128]{1,0:T(8,128)(2,1)S(1)} collective-permute-done((bf16[1024,128]{1,0:T(8,128)(2,1)S(1)}, bf16[1024,128]{1,0:T(8,128)(2,1)S(1)}, u32[]{:S(2)}, u32[]{:S(2)}) %collective-permute-start.9) | collective-permute-done | bytes 262176 | tf_op jit(solution)/shard_map/ppermute | solution.py:375
  43.8 0.7 %fusion = f32[512,512]{1,0:T(8,128)S(1)} fusion(bf16[1024,128]{1,0:T(8,128)(2,1)S(1)} %collective-permute-done.11, bf16[1024,128]{1,0:T(8,128)(2,1)S(1)} %get-tuple-element.98.filtered_ref, bf16[1024,128]{1,0:T(8,128)(2,1)S(1)} %collective-permute-done.10, bf16[1024,128]{1,0:T(8,128)(2,1)S(1)} %shard_map.110, ...), kind=kOutput, calls=%fused_computation.1 | convolution fusion | flops 545259520 | bytes 2883584 | tf_op jit(solution)/shard_map/dot_general | solution.py:355
  44.6 2.2 %collective-permute-start.12 = (bf16[4,32,512]{2,1,0:T(8,128)(2,1)S(1)}, bf16[4,32,512]{2,1,0:T(8,128)(2,1)S(1)}, u32[]{:S(2)}, u32[]{:S(2)}) collective-permute-start(bf16[4,32,512]{2,1,0:T(8,128)(2,1)S(1)} %get-tuple-element.108), channel_id=1, source_target_pairs={{0,8},{1,9},{2,10},{3,11},{4,12},{5,13},{6,14},{7,15},{8,0},{9,1},... | collective-permute-start | bytes 393224 | tf_op jit(solution)/shard_map/ppermute | solution.py:465
  46.8 1.9 %collective-permute-start.13 = (bf16[4,32,512]{2,1,0:T(8,128)(2,1)S(1)}, bf16[4,32,512]{2,1,0:T(8,128)(2,1)S(1)}, u32[]{:S(2)}, u32[]{:S(2)}) collective-permute-start(bf16[4,32,512]{2,1,0:T(8,128)(2,1)S(1)} %get-tuple-element.109), channel_id=1, source_target_pairs={{0,12},{1,13},{2,14},{3,15},{4,8},{5,9},{6,10},{7,11},{8,4},{9,5},... | collective-permute-start | bytes 393224 | tf_op jit(solution)/shard_map/ppermute | solution.py:465
  49.4 8.2 %collective-permute-done.12 = bf16[4,32,512]{2,1,0:T(8,128)(2,1)S(1)} collective-permute-done((bf16[4,32,512]{2,1,0:T(8,128)(2,1)S(1)}, bf16[4,32,512]{2,1,0:T(8,128)(2,1)S(1)}, u32[]{:S(2)}, u32[]{:S(2)}) %collective-permute-start.12) | collective-permute-done | bytes 131104 | tf_op jit(solution)/shard_map/ppermute | solution.py:465
  58.5 0.8 %copy.25 = bf16[256,512]{1,0:T(8,128)(2,1)} copy(bf16[256,512]{0,1:T(8,128)(2,1)S(1)} %bitcast.53) | data formatting | bytes 524288
  59.7 0.9 %shard_map.111 = (f32[32,1024]{1,0:T(8,128)}, f32[32,1024]{1,0:T(8,128)}) custom-call(s32[1]{0:T(128)} %bitcast.place_ref, s32[1]{0:T(128)} %bitcast.14.band_ref, f32[2,32,512]{2,1,0:T(8,128)S(1)} %get-tuple-element.116.refs_0_, f32[2,32,512]{2,1,0:T(8,128)S(1)} %collective-permute-done.15.refs_1_), custom_call_target="tpu_custom_call" | custom-call | bytes 2097152 | tf_op jit(solution)/shard_map/pallas_call | solution.py:325
  (36 shorter events, 10.6 us)
Async XLA Ops:
  3.6 1.0 %copy-start = (bf16[256,512]{1,0:T(8,128)(2,1)S(1)}, bf16[256,512]{1,0:T(8,128)(2,1)}, u32[]{:S(2)}) copy-start(bf16[256,512]{1,0:T(8,128)(2,1)} %field_ref.1) | copy-start | bytes 786436
  5.1 7.1 %collective-permute-start = (bf16[544,128]{1,0:T(8,128)(2,1)S(1)}, bf16[544,128]{1,0:T(8,128)(2,1)S(1)}, u32[]{:S(2)}, u32[]{:S(2)}) collective-permute-start(bf16[544,128]{1,0:T(8,128)(2,1)S(1)} %get-tuple-element.55), channel_id=1, source_target_pairs={{0,1},{1,0},{2,3},{3,2},{4,5},{5,4},{6,7},{7,6},{8,9},{9,8},{10,11... | collective-permute-start | bytes 417800 | tf_op jit(solution)/shard_map/ppermute | solution.py:375
  8.1 8.1 %collective-permute-start.1 = (bf16[544,128]{1,0:T(8,128)(2,1)S(1)}, bf16[544,128]{1,0:T(8,128)(2,1)S(1)}, u32[]{:S(2)}, u32[]{:S(2)}) collective-permute-start(bf16[544,128]{1,0:T(8,128)(2,1)S(1)} %get-tuple-element.56), channel_id=1, source_target_pairs={{0,2},{1,3},{2,0},{3,1},{4,6},{5,7},{6,4},{7,5},{8,10},{9,11},{10,... | collective-permute-start | bytes 417800 | tf_op jit(solution)/shard_map/ppermute | solution.py:375
  9.6 7.3 %collective-permute-start.2 = (bf16[544,128]{1,0:T(8,128)(2,1)S(1)}, bf16[544,128]{1,0:T(8,128)(2,1)S(1)}, u32[]{:S(2)}, u32[]{:S(2)}) collective-permute-start(bf16[544,128]{1,0:T(8,128)(2,1)S(1)} %get-tuple-element.57), channel_id=1, source_target_pairs={{0,3},{1,2},{2,1},{3,0},{4,7},{5,6},{6,5},{7,4},{8,11},{9,10},{10,... | collective-permute-start | bytes 417800 | tf_op jit(solution)/shard_map/ppermute | solution.py:375
  20.0 6.6 %collective-permute-start.3 = (bf16[384,128]{1,0:T(8,128)(2,1)S(1)}, bf16[384,128]{1,0:T(8,128)(2,1)S(1)}, u32[]{:S(2)}, u32[]{:S(2)}) collective-permute-start(bf16[384,128]{1,0:T(8,128)(2,1)S(1)} %get-tuple-element.93.sent_ref), channel_id=1, source_target_pairs={{0,4},{1,5},{2,6},{3,7},{4,8},{5,9},{6,10},{7,11},{8,12},{9,13},{1... | collective-permute-start | bytes 294920 | tf_op jit(solution)/shard_map/ppermute | solution.py:379
  21.6 5.7 %collective-permute-start.4 = (bf16[384,128]{1,0:T(8,128)(2,1)S(1)}, bf16[384,128]{1,0:T(8,128)(2,1)S(1)}, u32[]{:S(2)}, u32[]{:S(2)}) collective-permute-start(bf16[384,128]{1,0:T(8,128)(2,1)S(1)} %get-tuple-element.94), channel_id=1, source_target_pairs={{0,12},{1,13},{2,14},{3,15},{4,0},{5,1},{6,2},{7,3},{8,4},{9,5},{1... | collective-permute-start | bytes 294920 | tf_op jit(solution)/shard_map/ppermute | solution.py:379
  29.9 9.8 %collective-permute-start.7 = (bf16[1024,128]{1,0:T(8,128)(2,1)S(1)}, bf16[1024,128]{1,0:T(8,128)(2,1)S(1)}, u32[]{:S(2)}, u32[]{:S(2)}) collective-permute-start(bf16[1024,128]{1,0:T(8,128)(2,1)S(1)} %get-tuple-element.98.filtered_ref), channel_id=1, source_target_pairs={{0,1},{1,0},{2,3},{3,2},{4,5},{5,4},{6,7},{7,6},{8,9},{9,8},{10,11... | collective-permute-start | bytes 786440 | tf_op jit(solution)/shard_map/ppermute | solution.py:375
  30.5 9.6 %collective-permute-start.8 = (bf16[1024,128]{1,0:T(8,128)(2,1)S(1)}, bf16[1024,128]{1,0:T(8,128)(2,1)S(1)}, u32[]{:S(2)}, u32[]{:S(2)}) collective-permute-start(bf16[1024,128]{1,0:T(8,128)(2,1)S(1)} %get-tuple-element.98.filtered_ref), channel_id=1, source_target_pairs={{0,2},{1,3},{2,0},{3,1},{4,6},{5,7},{6,4},{7,5},{8,10},{9,11},{10,... | collective-permute-start | bytes 786440 | tf_op jit(solution)/shard_map/ppermute | solution.py:375
  32.1 9.9 %collective-permute-start.9 = (bf16[1024,128]{1,0:T(8,128)(2,1)S(1)}, bf16[1024,128]{1,0:T(8,128)(2,1)S(1)}, u32[]{:S(2)}, u32[]{:S(2)}) collective-permute-start(bf16[1024,128]{1,0:T(8,128)(2,1)S(1)} %get-tuple-element.98.filtered_ref), channel_id=1, source_target_pairs={{0,3},{1,2},{2,1},{3,0},{4,7},{5,6},{6,5},{7,4},{8,11},{9,10},{10,... | collective-permute-start | bytes 786440 | tf_op jit(solution)/shard_map/ppermute | solution.py:375
  33.5 5.5 %collective-permute-start.5 = (bf16[64,128]{1,0:T(8,128)(2,1)S(1)}, bf16[64,128]{1,0:T(8,128)(2,1)S(1)}, u32[]{:S(2)}, u32[]{:S(2)}) collective-permute-start(bf16[64,128]{1,0:T(8,128)(2,1)S(1)} %get-tuple-element.96), channel_id=1, source_target_pairs={{0,4},{1,5},{2,6},{3,7},{4,8},{5,9},{6,10},{7,11},{8,12},{9,13},{1... | collective-permute-start | bytes 49160 | tf_op jit(solution)/shard_map/ppermute | solution.py:379
  34.3 4.8 %collective-permute-start.6 = (bf16[64,128]{1,0:T(8,128)(2,1)S(1)}, bf16[64,128]{1,0:T(8,128)(2,1)S(1)}, u32[]{:S(2)}, u32[]{:S(2)}) collective-permute-start(bf16[64,128]{1,0:T(8,128)(2,1)S(1)} %get-tuple-element.97), channel_id=1, source_target_pairs={{0,12},{1,13},{2,14},{3,15},{4,0},{5,1},{6,2},{7,3},{8,4},{9,5},{1... | collective-permute-start | bytes 49160 | tf_op jit(solution)/shard_map/ppermute | solution.py:379
  41.9 1.5 %collective-permute-start.10 = (bf16[1024,128]{1,0:T(8,128)(2,1)S(1)}, bf16[1024,128]{1,0:T(8,128)(2,1)S(1)}, u32[]{:S(2)}, u32[]{:S(2)}) collective-permute-start(bf16[1024,128]{1,0:T(8,128)(2,1)S(1)} %shard_map.110), channel_id=1, source_target_pairs={{0,16},{16,0},{1,17},{17,1},{2,18},{18,2},{3,19},{19,3},{4,20},{20... | collective-permute-start | bytes 786440 | tf_op jit(solution)/shard_map/ppermute | solution.py:385
  41.9 1.9 %collective-permute-start.11 = (bf16[1024,128]{1,0:T(8,128)(2,1)S(1)}, bf16[1024,128]{1,0:T(8,128)(2,1)S(1)}, u32[]{:S(2)}, u32[]{:S(2)}) collective-permute-start(bf16[1024,128]{1,0:T(8,128)(2,1)S(1)} %get-tuple-element.98.filtered_ref), channel_id=1, source_target_pairs={{0,16},{16,0},{1,17},{17,1},{2,18},{18,2},{3,19},{19,3},{4,20},{20... | collective-permute-start | bytes 786440 | tf_op jit(solution)/shard_map/ppermute | solution.py:385
  44.6 13.0 %collective-permute-start.12 = (bf16[4,32,512]{2,1,0:T(8,128)(2,1)S(1)}, bf16[4,32,512]{2,1,0:T(8,128)(2,1)S(1)}, u32[]{:S(2)}, u32[]{:S(2)}) collective-permute-start(bf16[4,32,512]{2,1,0:T(8,128)(2,1)S(1)} %get-tuple-element.108), channel_id=1, source_target_pairs={{0,8},{1,9},{2,10},{3,11},{4,12},{5,13},{6,14},{7,15},{8,0},{9,1},... | collective-permute-start | bytes 393224 | tf_op jit(solution)/shard_map/ppermute | solution.py:465
  46.8 10.8 %collective-permute-start.13 = (bf16[4,32,512]{2,1,0:T(8,128)(2,1)S(1)}, bf16[4,32,512]{2,1,0:T(8,128)(2,1)S(1)}, u32[]{:S(2)}, u32[]{:S(2)}) collective-permute-start(bf16[4,32,512]{2,1,0:T(8,128)(2,1)S(1)} %get-tuple-element.109), channel_id=1, source_target_pairs={{0,12},{1,13},{2,14},{3,15},{4,8},{5,9},{6,10},{7,11},{8,4},{9,5},... | collective-permute-start | bytes 393224 | tf_op jit(solution)/shard_map/ppermute | solution.py:465
  48.8 9.4 %collective-permute-start.14 = (bf16[4,32,512]{2,1,0:T(8,128)(2,1)S(1)}, bf16[4,32,512]{2,1,0:T(8,128)(2,1)S(1)}, u32[]{:S(2)}, u32[]{:S(2)}) collective-permute-start(bf16[4,32,512]{2,1,0:T(8,128)(2,1)S(1)} %get-tuple-element.110), channel_id=1, source_target_pairs={{0,4},{1,5},{2,6},{3,7},{4,0},{5,1},{6,2},{7,3},{8,12},{9,13},{10,... | collective-permute-start | bytes 393224 | tf_op jit(solution)/shard_map/ppermute | solution.py:465
  58.3 1.4 %collective-permute-start.15 = (f32[2,32,512]{2,1,0:T(8,128)S(1)}, f32[2,32,512]{2,1,0:T(8,128)S(1)}, u32[]{:S(2)}, u32[]{:S(2)}) collective-permute-start(f32[2,32,512]{2,1,0:T(8,128)S(1)} %get-tuple-element.115), channel_id=1, source_target_pairs={{0,16},{16,0},{1,17},{17,1},{2,18},{18,2},{3,19},{19,3},{4,20},{20... | collective-permute-start | bytes 393224 | tf_op jit(solution)/shard_map/ppermute | solution.py:385

commit v3 on v2

--- a/solution.py
+++ b/solution.py
@@ -57,7 +57,8 @@
     small = small_ref[...]
     ids = small[0:cells, 0:LANES]
     high = jnp.floor(ids * (1.0 / 64.0))
-    pieces = [high, ids - 64.0 * high, small[cells : cells + 1, 0:LANES]]
+    high = jnp.where(iota((cells, LANES), 1) < corners, high, -8.0)
+    pieces = [high, ids - 64.0 * jnp.maximum(high, 0.0), small[cells : cells + 1, 0:LANES]]
     for j in (1, 2):
         for part in split3(small[cells + j : cells + j + 1]):
             pieces += [part[:, h * LANES : (h + 1) * LANES].astype(F32) for h in range(nodes // LANES)]
@@ -99,7 +100,7 @@
 
 
 def build_kernel(
-    nodes, cells, corners, shared, center_ref, half_ref, ref, own_ref, corner_ref, up_ref, down_ref, mass_ref, scale_ref, diag_ref,
+    nodes, cells, corners, shared, center_ref, half_ref, ref, _, own_ref, corner_ref, up_ref, down_ref, mass_ref, scale_ref, diag_ref,
 ):
     center, half = center_ref[0], half_ref[0]
     both = nodes + shared
@@ -141,11 +142,12 @@
         diag_ref[at, :] = (pot - center) / half
 
 
-def first_kernel(shared, place_ref, *refs):
+def first_kernel(shared, place_ref, odd_ref, *refs):
     messages, refs = refs[:GROUP], refs[GROUP:]
     slabs = [refs[7 * k : 7 * k + 7] for k in range(GROUP)]
     own_ref, down_ref, up_ref, mass_ref, scale_ref, diag_ref, start_ref = refs[7 * GROUP : 7 * GROUP + 7]
-    next_ref, previous_ref, raw, corner, cur, prev = refs[7 * GROUP + 7 :]
+    keep_ref, pair0_ref, pair1_ref, raw, corner, cur, prev, box = refs[7 * GROUP + 7 :]
+    next_ref, previous_ref = box.at[0], box.at[1]
     place = place_ref[0]
     nodes = own_ref.shape[1]
     for k in range(GROUP):
@@ -227,12 +229,20 @@
         previous_ref[at + j * shared : at + (j + 1) * shared, :] = jnp.concatenate(
             previous_parts[2 * j : 2 * j + 2], axis=1
         ).astype(BF16)
+    keep_ref[...] = next_ref[at + shared : at + 2 * shared, :]
+    odd = odd_ref[0]
+    pair0_ref[...] = box[odd]
+    pair1_ref[...] = box[1 - odd]
 
 
 def second_kernel(
-    shared, own_ref, down_ref, up_ref, mass_ref, scale_ref, diag_ref, start_ref, sent_ref, below_ref, above_ref,
-    filtered_ref, next_ref, previous_ref, cur, prev,
+    shared, odd_ref, own_ref, down_ref, up_ref, mass_ref, scale_ref, diag_ref, start_ref, keep_ref, from0_ref, from1_ref,
+    filtered_ref, corner_ref, pair0_ref, pair1_ref, cur, prev, box,
 ):
+    odd = odd_ref[0]
+    box[0] = from0_ref[...]
+    box[1] = from1_ref[...]
+    above_ref, below_ref = box.at[odd], box.at[1 - odd]
     nodes = own_ref.shape[1]
     own = [own_ref[i] for i in range(GROUP)]
     down = [down_ref[i] for i in range(GROUP)]
@@ -240,7 +250,8 @@
     at = FILTER_DEG * shared
     near_b, far_b = below_ref[at : at + shared, :], below_ref[at + shared : at + 2 * shared, :]
     near_a, far_a = above_ref[at : at + shared, :], above_ref[at + shared : at + 2 * shared, :]
-    mine = sent_ref[at + shared : at + 2 * shared, :]
+    mine = keep_ref[...]
+    corner_ref[...] = far_b
     zero = jnp.zeros((shared, LANES), BF16)
     cur[...] = start_ref[...].astype(F32)
     prev[...] = jnp.zeros_like(prev)
@@ -286,21 +297,26 @@
     top = (GROUP - 1) * nodes
     field0 = (mass_ref[0:nodes, :] * filtered_ref[0:nodes, :].astype(F32)).astype(BF16)
     field3 = (mass_ref[top:, :] * filtered_ref[top:, :].astype(F32)).astype(BF16)
-    next_ref[...] = dot(down[GROUP - 1], field3)[:shared].astype(BF16)
-    previous_ref[...] = dot(down[0], field0)[shared:].astype(BF16)
+    box[0, 0:shared, :] = dot(down[GROUP - 1], field3)[:shared].astype(BF16)
+    box[1, 0:shared, :] = dot(down[0], field0)[shared:].astype(BF16)
+    pair0_ref[...] = box[odd, 0:shared, :]
+    pair1_ref[...] = box[1 - odd, 0:shared, :]
 
 
 def third_kernel(
-    shared, center_ref, half_ref, own_ref, down_ref, up_ref, mass_ref, diag_ref, filtered_ref, corner_ref, below_ref,
-    above_ref, applied_ref,
+    shared, odd_ref, center_ref, half_ref, own_ref, down_ref, up_ref, mass_ref, diag_ref, filtered_ref, corner_ref,
+    from0_ref, from1_ref, left_ref, box,
 ):
     nodes = own_ref.shape[1]
     center, half = center_ref[0], half_ref[0]
     own = [own_ref[i] for i in range(GROUP)]
     down = [down_ref[i] for i in range(GROUP)]
     up = [up_ref[i] for i in range(GROUP)]
-    at = FILTER_DEG * shared
-    far_b = corner_ref[at + shared : at + 2 * shared, :]
+    odd = odd_ref[0]
+    box[0] = from0_ref[...]
+    box[1] = from1_ref[...]
+    above_ref, below_ref = box.at[odd], box.at[1 - odd]
+    far_b = corner_ref[...]
     zero = jnp.zeros((shared, LANES), BF16)
 
     def outside(to_previous, to_next):
@@ -314,7 +330,9 @@
     for i in range(GROUP):
         rows = slice(i * nodes, (i + 1) * nodes)
         pot = diag_ref[rows, :] * half + center
-        applied_ref[rows, :] = (mass_ref[rows, :] * sums[i] + pot * values[i]).astype(BF16)
+        applied = mass_ref[rows, :] * sums[i] + pot * values[i]
+        left_ref[0:LANES, rows] = jnp.transpose(applied).astype(BF16)
+        left_ref[LANES:, rows] = jnp.transpose(values[i]).astype(BF16)
 
 
 SPACES = {"s": pltpu.SMEM, "v": pltpu.VMEM, "a": pl.ANY}
@@ -333,26 +351,52 @@
     )(*args)
 
 
-def place_kernel(planes, factor, place_ref, band_ref, *refs):
-    pieces, outs = refs[:-2], refs[-2:]
+def product_kernel(planes, partner, plane_ref, left_ref, *refs):
+    chunks, outs, total = refs[: -planes - 1], refs[-planes - 1 : -1], refs[-1]
+    plane = plane_ref[0]
+    rows = LANES // planes
+    left = left_ref[...]
+    for c in range(0, len(chunks), 2):
+        right = jnp.concatenate([chunks[c][...], chunks[c + 1][...]], axis=1)
+        total[:, c * LANES : (c + 2) * LANES] = dot(left, right)
+    for k, out in enumerate(outs):
+        for mat in range(2):
+            at = pl.ds(pl.multiple_of(mat * LANES + partner(plane, k) * rows, rows), rows)
+            out[mat] = total[at, :].astype(out.dtype)
+
+
+def arrange_kernel(planes, place_ref, *refs):
+    chunks, out = refs[:GROUP], refs[GROUP]
+    place = place_ref[0]
+    nodes, width = out.shape
+    rows = LANES // planes
+    at = pl.ds(pl.multiple_of(place * nodes, nodes), nodes)
+    source = iota((LANES, width), 0)
+    target = iota((LANES, width), 1)
+    total = jnp.zeros((nodes, width), F32)
+    for k, chunk in enumerate(chunks):
+        wanted = (source // rows) * (GROUP * rows) + (place ^ k) * rows + source % rows
+        total = total + dot(chunk[at, :], (wanted == target).astype(F32).astype(BF16))
+    out[...] = total.astype(BF16)
+
+
+def place_kernel(planes, bands, factor, place_ref, band_ref, *refs):
+    parts, outs = refs[:planes], refs[planes:]
     place, band = place_ref[0], band_ref[0]
-    _, rows, width = pieces[0].shape
-    bands = len(pieces)
-    for j, piece in enumerate(pieces):
-        first = ((band + j) % bands) * width
-        for mat, out in enumerate(outs):
-            chunks = [
-                piece[mat, :, pl.ds(pl.multiple_of((place ^ c) * LANES, LANES), LANES)] * factor for c in range(GROUP)
-            ]
+    _, rows, width = parts[0].shape
+    width = width // bands
+    for mat, out in enumerate(outs):
+        for j in range(bands):
+            chunks = []
+            for c in range(GROUP):
+                at = pl.ds(pl.multiple_of(j * width + (place ^ c) * LANES, LANES), LANES)
+                chunks.append(sum(part[mat, :, at].astype(F32) for part in parts) * factor)
             columns = [
                 jnp.concatenate([chunk[:, z * rows : (z + 1) * rows] for chunk in chunks], axis=1)
                 for z in range(planes)
             ]
-            out[:, pl.ds(pl.multiple_of(first, LANES), width)] = jnp.concatenate(columns, axis=1)
-
-
-def contract(left, right):
-    return lax.dot_general(left, right, (((0,), (0,)), ((), ())), preferred_element_type=F32)
+            target = ((band + bands - j) % bands) * width
+            out[:, pl.ds(pl.multiple_of(target, LANES), width)] = jnp.concatenate(columns, axis=1)
 
 
 def shards(
@@ -374,22 +418,18 @@
     def in_plane(block, k):
         return lax.ppermute(block, "dom", [(i, i ^ k) for i in everyone])
 
-    def to_plane(block, k):
-        route = [(i, (i // GROUP + k) % planes * GROUP + i % GROUP) for i in everyone]
-        return lax.ppermute(block, "dom", route)
-
     def partner(index, k):
         return index ^ k if planes & (planes - 1) == 0 else (2 * planes + k - index) % planes
 
     def to_band(block, k):
         return lax.ppermute(block, "band", [(i, (i + k) % band_count) for i in range(band_count)])
 
-    def line(values, fill):
-        return jnp.pad(values.astype(F32), ((0, 0), (0, nodes - values.shape[1])), constant_values=fill)
-
-    small = jnp.concatenate(
-        [line(cell_nodes.T, -512.0), line(shared_nodes, 0.0), inv_sqrt_mass[None], potential[None]], axis=0
-    )
+    def line(values, row):
+        height, count = values.shape
+        return jnp.pad(values, ((row, 8 - row - height), (0, nodes - count)))
+
+    ids = line(cell_nodes.T, 0) + line(shared_nodes, cells)
+    small = ids.astype(F32) + line(inv_sqrt_mass[None], cells + 1) + line(potential[None], cells + 2)
     messages = call(
         functools.partial(pack_kernel, planes, corners),
         [((nodes + (cells + 1) // 2 * LANES + EXTRA, LANES), BF16)] * GROUP,
@@ -405,80 +445,87 @@
             [
                 ((nodes, nodes), F32), ((shared, shared), F32), ((nodes, 2 * shared), BF16), ((2 * shared, nodes), BF16),
             ] + [((nodes, LANES), F32)] * 3,
-            (filter_center, filter_halfwidth, message),
-            spaces="ssv",
+            (filter_center, filter_halfwidth, message, slabs[-6] if slabs else message),
+            spaces="ssva",
             flops=1 << 28,
         )
     height = GROUP * nodes
     column = ((height, LANES), F32)
     trace = ((FILTER_DEG * shared + 2 * shared, LANES), BF16)
-    own, down, up, mass, scale, diag, start, next_msg, previous_msg = call(
+    odd_arg = (plane % 2).astype(jnp.int32).reshape(1)
+    own, down, up, mass, scale, diag, start, keep, *pairs = call(
         functools.partial(first_kernel, shared),
         [
             ((GROUP, nodes, nodes), BF16), ((GROUP, 2 * shared, nodes), BF16), ((GROUP, nodes, 2 * shared), BF16),
-            column, column, column, ((height, LANES), BF16), trace, trace,
+            column, column, column, ((height, LANES), BF16), ((shared, LANES), BF16), trace, trace,
         ],
-        (place_arg, *messages, *slabs),
-        spaces="s" + "v" * (GROUP * 8),
+        (place_arg, odd_arg, *messages, *slabs),
+        spaces="ss" + "v" * (GROUP * 8),
         scratch=[
             pltpu.VMEM((GROUP, nodes, nodes), F32), pltpu.VMEM((GROUP, shared, shared), F32),
             pltpu.VMEM((height, 2 * LANES), F32), pltpu.VMEM((height, 2 * LANES), F32),
+            pltpu.VMEM((2, *trace[0]), BF16),
         ],
         flops=1 << 30,
     )
-    below = to_plane(next_msg, 1)
-    above = to_plane(previous_msg, -1)
-    mine, next_msg, previous_msg = call(
+
+    def with_neighbour(blocks):
+        firsts = [z ^ 1 for z in range(planes)]
+        seconds = [(z + 1 if z % 2 else z - 1) % planes for z in range(planes)]
+        routes = [[(i, to[i // GROUP] * GROUP + i % GROUP) for i in everyone] for to in (firsts, seconds)]
+        return [lax.ppermute(block, "dom", route) for block, route in zip(blocks, routes)]
+
+    heard = with_neighbour(pairs)
+    mine, corner, *pairs = call(
         functools.partial(second_kernel, shared),
-        [((height, LANES), BF16), ((shared, LANES), BF16), ((shared, LANES), BF16)],
-        (own, down, up, mass, scale, diag, start, next_msg, below, above),
-        scratch=[pltpu.VMEM((height, LANES), F32), pltpu.VMEM((height, LANES), F32)],
+        [((height, LANES), BF16)] + [((shared, LANES), BF16)] * 3,
+        (odd_arg, own, down, up, mass, scale, diag, start, keep, *heard),
+        spaces="s" + "v" * 10,
+        scratch=[pltpu.VMEM((height, LANES), F32), pltpu.VMEM((height, LANES), F32), pltpu.VMEM((2, *trace[0]), BF16)],
         flops=1 << 30,
     )
-    below_now = to_plane(next_msg, 1)
-    above_now = to_plane(previous_msg, -1)
+    heard = with_neighbour(pairs)
     others = [in_plane(mine, k) for k in range(1, GROUP)]
-    (applied,) = call(
+    first, others[0], *heard = lax.optimization_barrier((mine, others[0], *heard))
+    (left,) = call(
         functools.partial(third_kernel, shared),
-        [((height, LANES), BF16)],
-        (filter_center, filter_halfwidth, own, down, up, mass, diag, mine, below, below_now, above_now),
-        spaces="ss" + "v" * 9,
+        [((2 * LANES, height), BF16)],
+        (odd_arg, filter_center, filter_halfwidth, own, down, up, mass, diag, mine, corner, *heard),
+        spaces="sss" + "v" * 9,
+        scratch=[pltpu.VMEM((2, shared, LANES), BF16)],
         flops=1 << 28,
     )
 
-    applied, mine, *others = lax.optimization_barrier((applied, mine, *others))
-    lefts = [applied] + [to_band(applied, k) for k in range(1, band_count)]
-    lefts += [mine] + [to_band(mine, k) for k in range(1, band_count)]
-    left = jnp.concatenate(lefts, axis=1)
     gathered = [mine] + others
-    totals = []
-    for part in ((0, 1, 2, 3),):
-        right = gathered[part[0]] if len(part) == 1 else jnp.concatenate([gathered[k] for k in part], axis=1)
-        product = contract(left, right).reshape(2 * band_count, planes, rows, len(part) * LANES)
-
-        def part_for(k, product=product):
-            return lax.dynamic_index_in_dim(product, partner(plane, k), 1, keepdims=False)
-
-        total = part_for(0)
-        for k in [*range(2, planes), 1]:
-            route = [(i, partner(i // GROUP, k) * GROUP + i % GROUP) for i in everyone]
-            total = total + lax.ppermute(part_for(k).astype(BF16), "dom", route).astype(F32)
-        totals.append(total)
-    total = jnp.concatenate(totals, axis=2).reshape(2, band_count, rows, width)
-    pieces = [total[:, 0]] + [to_band(total[:, j], -j) for j in range(1, band_count)]
+    rights = list(gathered)
+    for k in range(1, band_count):
+        rights += [to_band(block, k) for block in [first] + others]
+    part = (2, rows, band_count * width)
+    parts = list(call(
+        functools.partial(product_kernel, planes, partner),
+        [(part, F32)] + [(part, BF16)] * (planes - 1),
+        (plane.astype(jnp.int32).reshape(1), left, *rights),
+        spaces="sv" + "v" * len(rights),
+        scratch=[pltpu.VMEM((2 * LANES, band_count * width), F32)],
+        flops=1 << 28,
+    ))
+    for k in [*range(2, planes), *range(1, min(planes, 2))]:
+        route = [(i, partner(i // GROUP, k) * GROUP + i % GROUP) for i in everyone]
+        parts[k] = lax.ppermute(parts[k], "dom", route)
+    early = [*range(2, planes), 1][0]
+    *gathered, parts[early] = lax.optimization_barrier((*gathered, parts[early]))
+    (filtered,) = call(
+        functools.partial(arrange_kernel, planes),
+        [((nodes, width), BF16)],
+        (place_arg, *gathered),
+        spaces="s" + "v" * GROUP,
+    )
     projected, intersection = call(
-        functools.partial(place_kernel, planes, 1.0 / (nodes * dom_count)),
+        functools.partial(place_kernel, planes, band_count, 1.0 / (nodes * dom_count)),
         [((rows, band_count * width), F32)] * 2,
-        (place_arg, band.astype(jnp.int32).reshape(1), *pieces),
-        spaces="ss" + "v" * band_count,
-    )
-    chunks = jnp.stack([mine] + others).reshape(GROUP, GROUP, nodes, LANES)
-    chunks = lax.dynamic_index_in_dim(chunks, place, 1, keepdims=False)
-    chunks = jnp.stack(
-        [lax.dynamic_index_in_dim(chunks, place ^ c, 0, keepdims=False) for c in range(GROUP)], axis=1
-    )
-    chunks = chunks.reshape(nodes, GROUP, planes, rows)
-    filtered = jnp.transpose(chunks, (0, 2, 1, 3)).reshape(nodes, width)
+        (place_arg, band.astype(jnp.int32).reshape(1), *parts),
+        spaces="ss" + "v" * planes,
+    )
     return filtered, intersection, projected
 
 

time: 60.9 us -> 57.8 us (0.949)
  other arithmetic: 2.28 us -> 0.01 us
  Pallas kernels: 9.96 us -> 12.1 us
  local copies, waits for them, and re-layouts: 3.42 us -> 1.65 us
  matrix products: 0.73 us -> 0 us
    pallas_call x9 -> x11, Pallas kernels: 9.96 us -> 12.1 us  [call(): pl.pallas_call(kernel, out_shape=[jax.ShapeDtypeStruct(shape, dtype) for...]
    convert_element_type x2 -> x0, other arithmetic: 1.34 us -> none  [line(): values.astype(F32)]
    ppermute x6, waiting for transfers between devices: 6.02 us -> 7.31 us  [in_plane(): return lax.ppermute(block, 'dom', [(i, i ^ k) for i in everyone])]
    unnamed x4 -> x11, local copies, waits for them, and re-layouts: 2.71 us -> 1.65 us
    dot_general x1 -> x0, matrix products: 0.73 us -> none  [contract(): lax.dot_general(left, right, (((0,), (0,)), ((), ())), preferred_element_...]
    concatenate x1 -> x0, other arithmetic: 0.71 us -> none  [shards(): jnp.concatenate([line(cell_nodes.T, -512.0), line(shared_nodes, 0.0), inv...]
    ppermute x7, waiting for transfers between devices: 13.9 us -> 13.3 us  [the longest x3 7.16 us: shards(): parts[k] = lax.ppermute(parts[k], 'dom', route)]
  transfers between devices with their start and end apart: 16 -> 17, of which waited for: 12 -> 12; matrix products, arithmetic and copies ran while one was open for 3% -> 0% of each run, Pallas kernels for 5% -> 7%
where the time goes in v3:
time: 57.8 us; the launch traced here: 57.6 us
  waiting for transfers between devices  21.3 us (37%)
  starting transfers between devices  20.5 us (35%)
  Pallas kernels  12.1 us (21%)
  between operations  2.09 us (4%)
  local copies, waits for them, and re-layouts  1.65 us (3%)
    pallas_call x11, Pallas kernels, call(): pl.pallas_call(kernel, out_shape=[jax.ShapeDtypeStruct(shape, dtype) for...  12.1 us
    ppermute x6, starting transfers between devices, in_plane(): return lax.ppermute(block, 'dom', [(i, i ^ k) for i in everyone])  8.1 us
    ppermute x4, starting transfers between devices, with_neighbour(): lax.ppermute(block, 'dom', route)  7.43 us
    ppermute x6, waiting for transfers between devices, in_plane(): return lax.ppermute(block, 'dom', [(i, i ^ k) for i in everyone])  7.31 us
    ppermute x3, waiting for transfers between devices, shards(): parts[k] = lax.ppermute(parts[k], 'dom', route)  7.16 us
    ppermute x4, waiting for transfers between devices, with_neighbour(): lax.ppermute(block, 'dom', route)  6.17 us
    ppermute x3, starting transfers between devices, shards(): parts[k] = lax.ppermute(parts[k], 'dom', route)  4.45 us
    unnamed x11, local copies, waits for them, and re-layouts  1.65 us
  transfers between devices with their start and end apart: 17, of which 12 were waited for; matrix products, arithmetic and copies ran while one was open for 0% of the time, Pallas kernels for 7%

profile of v3, /device:TPU:0, one launch (start us, length us, event | category | flops | bytes accessed | tf_op | source)
XLA Modules:
  0.0 57.6 jit_solution(14072017618246970784)
XLA Ops:
  0.7 1.0 %copy.11.cells_ref = bf16[4,125,125]{2,1,0:T(8,128)(2,1)S(1)} copy(bf16[4,125,125]{2,0,1:T(4,128)(2,1)} %param.9) | data formatting | bytes 250000 | tf_op args[1]
  2.9 3.0 %collective-permute-start = (bf16[544,128]{1,0:T(8,128)(2,1)S(1)}, bf16[544,128]{1,0:T(8,128)(2,1)S(1)}, u32[]{:S(2)}, u32[]{:S(2)}) collective-permute-start(bf16[544,128]{1,0:T(8,128)(2,1)S(1)} %get-tuple-element.65), channel_id=1, source_target_pairs={{0,1},{1,0},{2,3},{3,2},{4,5},{5,4},{6,7},{7,6},{8,9},{9,8},{10,11... | collective-permute-start | bytes 417800 | tf_op jit(solution)/shard_map/ppermute | solution.py:419
  5.9 1.5 %collective-permute-start.1 = (bf16[544,128]{1,0:T(8,128)(2,1)S(1)}, bf16[544,128]{1,0:T(8,128)(2,1)S(1)}, u32[]{:S(2)}, u32[]{:S(2)}) collective-permute-start(bf16[544,128]{1,0:T(8,128)(2,1)S(1)} %get-tuple-element.66), channel_id=1, source_target_pairs={{0,2},{1,3},{2,0},{3,1},{4,6},{5,7},{6,4},{7,5},{8,10},{9,11},{10,... | collective-permute-start | bytes 417800 | tf_op jit(solution)/shard_map/ppermute | solution.py:419
  10.7 3.3 %collective-permute-done.1.ref.refs_2_ = bf16[544,128]{1,0:T(8,128)(2,1)S(1)} collective-permute-done((bf16[544,128]{1,0:T(8,128)(2,1)S(1)}, bf16[544,128]{1,0:T(8,128)(2,1)S(1)}, u32[]{:S(2)}, u32[]{:S(2)}) %collective-permute-start.1) | collective-permute-done | bytes 139296 | tf_op jit(solution)/shard_map/ppermute | solution.py:419
  15.5 2.4 %shard_map.108 = (bf16[4,256,256]{2,1,0:T(8,128)(2,1)S(1)}, bf16[4,128,256]{2,1,0:T(8,128)(2,1)S(1)}, bf16[4,256,128]{2,1,0:T(8,128)(2,1)S(1)}, f32[1024,128]{1,...) custom-call(s32[1]{0:T(128)} %bitcast.place_ref, ...), custom_call_target="tpu_custom_call" | custom-call | flops 1073741824 | bytes 2097152 | tf_op jit(solution)/shard_map/pallas_call | solution.py:343
  17.9 1.6 %collective-permute-start.3 = (bf16[384,128]{1,0:T(8,128)(2,1)S(1)}, bf16[384,128]{1,0:T(8,128)(2,1)S(1)}, u32[]{:S(2)}, u32[]{:S(2)}) collective-permute-start(bf16[384,128]{1,0:T(8,128)(2,1)S(1)} %get-tuple-element.104), channel_id=1, source_target_pairs={{0,4},{1,5},{2,6},{3,7},{4,0},{5,1},{6,2},{7,3},{8,12},{9,13},{10,... | collective-permute-start | bytes 294920 | tf_op jit(solution)/shard_map/ppermute | solution.py:476
  19.5 2.5 %collective-permute-start.4 = (bf16[384,128]{1,0:T(8,128)(2,1)S(1)}, bf16[384,128]{1,0:T(8,128)(2,1)S(1)}, u32[]{:S(2)}, u32[]{:S(2)}) collective-permute-start(bf16[384,128]{1,0:T(8,128)(2,1)S(1)} %get-tuple-element.105), channel_id=1, source_target_pairs={{0,12},{1,13},{2,14},{3,15},{4,8},{5,9},{6,10},{7,11},{8,4},{9,5},... | collective-permute-start | bytes 294920 | tf_op jit(solution)/shard_map/ppermute | solution.py:476
  22.0 1.6 %collective-permute-done.3.from0_ref = bf16[384,128]{1,0:T(8,128)(2,1)S(1)} collective-permute-done((bf16[384,128]{1,0:T(8,128)(2,1)S(1)}, bf16[384,128]{1,0:T(8,128)(2,1)S(1)}, u32[]{:S(2)}, u32[]{:S(2)}) %collective-permute-start.3) | collective-permute-done | bytes 98336 | tf_op jit(solution)/shard_map/ppermute | solution.py:476
  23.6 2.3 %collective-permute-done.4.from1_ref = bf16[384,128]{1,0:T(8,128)(2,1)S(1)} collective-permute-done((bf16[384,128]{1,0:T(8,128)(2,1)S(1)}, bf16[384,128]{1,0:T(8,128)(2,1)S(1)}, u32[]{:S(2)}, u32[]{:S(2)}) %collective-permute-start.4) | collective-permute-done | bytes 98336 | tf_op jit(solution)/shard_map/ppermute | solution.py:476
  25.9 2.6 %shard_map.109 = (bf16[1024,128]{1,0:T(8,128)(2,1)S(1)}, bf16[64,128]{1,0:T(8,128)(2,1)S(1)}, bf16[64,128]{1,0:T(8,128)(2,1)S(1)}, bf16[64,128]{1,0:T(8,128)(2,1)S(1)}) custom-call(s32[1]{0:T(128)} %bitcast.1.odd_ref, bf16[4,256,256]{2,1,0:T(8,128)(2,1)S(1)} %get-tuple-element.96.own_ref, bf16[4,128,256]{2,1,0:T(8,128)(2,1)S(1)} %get-tuple-element.97.down_ref, ...), custom_call_target="tpu_custom_call" | custom-call | flops 1073741824 | bytes 2097152 | tf_op jit(solution)/shard_map/pallas_call | solution.py:343
  29.1 2.5 %collective-permute-start.9 = (bf16[1024,128]{1,0:T(8,128)(2,1)S(1)}, bf16[1024,128]{1,0:T(8,128)(2,1)S(1)}, u32[]{:S(2)}, u32[]{:S(2)}) collective-permute-start(bf16[1024,128]{1,0:T(8,128)(2,1)S(1)} %get-tuple-element.115.filtered_ref.refs_0_), channel_id=1, source_target_pairs={{0,3},{1,2},{2,1},{3,0},{4,7},{5,6},{6,5},{7,4},{8,11},{9,10},{10,... | collective-permute-start | bytes 786440 | tf_op jit(solution)/shard_map/ppermute | solution.py:419
  32.1 3.3 %collective-permute-start.7 = (bf16[64,128]{1,0:T(8,128)(2,1)S(1)}, bf16[64,128]{1,0:T(8,128)(2,1)S(1)}, u32[]{:S(2)}, u32[]{:S(2)}) collective-permute-start(bf16[64,128]{1,0:T(8,128)(2,1)S(1)} %get-tuple-element.108), channel_id=1, source_target_pairs={{0,12},{1,13},{2,14},{3,15},{4,8},{5,9},{6,10},{7,11},{8,4},{9,5},... | collective-permute-start | bytes 49160 | tf_op jit(solution)/shard_map/ppermute | solution.py:476
  35.9 1.8 %collective-permute-done.7.from1_ref = bf16[64,128]{1,0:T(8,128)(2,1)S(1)} collective-permute-done((bf16[64,128]{1,0:T(8,128)(2,1)S(1)}, bf16[64,128]{1,0:T(8,128)(2,1)S(1)}, u32[]{:S(2)}, u32[]{:S(2)}) %collective-permute-start.7) | collective-permute-done | bytes 16416 | tf_op jit(solution)/shard_map/ppermute | solution.py:476
  37.7 2.2 %collective-permute-done.9.refs_3_ = bf16[1024,128]{1,0:T(8,128)(2,1)S(1)} collective-permute-done((bf16[1024,128]{1,0:T(8,128)(2,1)S(1)}, bf16[1024,128]{1,0:T(8,128)(2,1)S(1)}, u32[]{:S(2)}, u32[]{:S(2)}) %collective-permute-start.9) | collective-permute-done | bytes 262176 | tf_op jit(solution)/shard_map/ppermute | solution.py:419
  39.9 1.3 %collective-permute-done.8.refs_2_ = bf16[1024,128]{1,0:T(8,128)(2,1)S(1)} collective-permute-done((bf16[1024,128]{1,0:T(8,128)(2,1)S(1)}, bf16[1024,128]{1,0:T(8,128)(2,1)S(1)}, u32[]{:S(2)}, u32[]{:S(2)}) %collective-permute-start.8) | collective-permute-done | bytes 262176 | tf_op jit(solution)/shard_map/ppermute | solution.py:419
  41.7 0.8 %shard_map.110.left_ref = bf16[256,1024]{1,0:T(8,128)(2,1)S(1)} custom-call(s32[1]{0:T(128)} %bitcast.1.odd_ref, f32[1]{0:T(128)S(6)} %copy.12.center_ref, f32[1]{0:T(128)S(6)} %copy.13.half_ref, bf16[4,256,256]{2,1,0:T(8,128)(2,1)S(1)} %get-tuple-element.96.own_ref, bf16[4,128,256]{2,1,0:T(8,128)(2,1)S(1)} %get-tuple-element.97.down_ref, ...), custom_call_target="tpu_custom_call" | custom-call | flops 268435456 | bytes 2097152 | tf_op jit(solution)/shard_map/pallas_call | solution.py:343
  43.1 0.8 %shard_map.111 = (f32[2,32,1024]{2,1,0:T(8,128)S(1)}, bf16[2,32,1024]{2,1,0:T(8,128)(2,1)S(1)}, bf16[2,32,1024]{2,1,0:T(8,128)(2,1)S(1)}, bf16[2,32,1024]{2,1,0:T(8,128)(2,1)S(1)}) custom-call(s32[1]{0:T(128)} %bitcast.5.plane_ref, bf16[256,1024]{1,0:T(8,128)(2,1)S(1)} %shard_map.110.left_ref, bf16[1024,128]{1,0:T(8,128)(2,1)S(1)} %get-tuple-element.115.filtered_ref.refs_0_, ...), custom_call_target="tpu_custom_call" | custom-call | flops 268435456 | bytes 2097152 | tf_op jit(solution)/shard_map/pallas_call | solution.py:343
  43.9 1.5 %collective-permute-start.14 = (bf16[2,32,1024]{2,1,0:T(8,128)(2,1)S(1)}, bf16[2,32,1024]{2,1,0:T(8,128)(2,1)S(1)}, u32[]{:S(2)}, u32[]{:S(2)}) collective-permute-start(bf16[2,32,1024]{2,1,0:T(8,128)(2,1)S(1)} %get-tuple-element.114), channel_id=1, source_target_pairs={{0,8},{1,9},{2,10},{3,11},{4,12},{5,13},{6,14},{7,15},{8,0},{9,1},... | collective-permute-start | bytes 393224 | tf_op jit(solution)/shard_map/ppermute | solution.py:514
  45.4 1.6 %collective-permute-start.15 = (bf16[2,32,1024]{2,1,0:T(8,128)(2,1)S(1)}, bf16[2,32,1024]{2,1,0:T(8,128)(2,1)S(1)}, u32[]{:S(2)}, u32[]{:S(2)}) collective-permute-start(bf16[2,32,1024]{2,1,0:T(8,128)(2,1)S(1)} %get-tuple-element.120), channel_id=1, source_target_pairs={{0,4},{1,5},{2,6},{3,7},{4,0},{5,1},{6,2},{7,3},{8,12},{9,13},{10,... | collective-permute-start | bytes 393224 | tf_op jit(solution)/shard_map/ppermute | solution.py:514
  47.0 1.3 %collective-permute-start.16 = (bf16[2,32,1024]{2,1,0:T(8,128)(2,1)S(1)}, bf16[2,32,1024]{2,1,0:T(8,128)(2,1)S(1)}, u32[]{:S(2)}, u32[]{:S(2)}) collective-permute-start(bf16[2,32,1024]{2,1,0:T(8,128)(2,1)S(1)} %get-tuple-element.122), channel_id=1, source_target_pairs={{0,12},{1,13},{2,14},{3,15},{4,8},{5,9},{6,10},{7,11},{8,4},{9,5},... | collective-permute-start | bytes 393224 | tf_op jit(solution)/shard_map/ppermute | solution.py:514
  48.3 6.2 %collective-permute-done.14.refs_2_ = bf16[2,32,1024]{2,1,0:T(8,128)(2,1)S(1)} collective-permute-done((bf16[2,32,1024]{2,1,0:T(8,128)(2,1)S(1)}, bf16[2,32,1024]{2,1,0:T(8,128)(2,1)S(1)}, u32[]{:S(2)}, u32[]{:S(2)}) %collective-permute-start.14) | collective-permute-done | bytes 131104 | tf_op jit(solution)/shard_map/ppermute | solution.py:514
  54.5 1.1 %shard_map.112 = bf16[256,512]{1,0:T(8,128)(2,1)} custom-call(s32[1]{0:T(128)} %bitcast.place_ref, bf16[1024,128]{1,0:T(8,128)(2,1)S(1)} %get-tuple-element.115.filtered_ref.refs_0_, bf16[1024,128]{1,0:T(8,128)(2,1)S(1)} %collective-permute-done.5.refs_1_, bf16[1024,128]{1,0:T(8,128)(2,1)S(1)} %collective-permute-done.8.refs_2_, ...), custom_call_target="tpu_custom_call" | custom-call | bytes 2097152 | tf_op jit(solution)/shard_map/pallas_call | solution.py:343
  55.7 0.9 %collective-permute-done.16.refs_3_ = bf16[2,32,1024]{2,1,0:T(8,128)(2,1)S(1)} collective-permute-done((bf16[2,32,1024]{2,1,0:T(8,128)(2,1)S(1)}, bf16[2,32,1024]{2,1,0:T(8,128)(2,1)S(1)}, u32[]{:S(2)}, u32[]{:S(2)}) %collective-permute-start.16) | collective-permute-done | bytes 131104 | tf_op jit(solution)/shard_map/ppermute | solution.py:514
  56.6 0.9 %shard_map.113 = (f32[32,1024]{1,0:T(8,128)}, f32[32,1024]{1,0:T(8,128)}) custom-call(s32[1]{0:T(128)} %bitcast.place_ref, s32[1]{0:T(128)} %bitcast.6.band_ref, f32[2,32,1024]{2,1,0:T(8,128)S(1)} %get-tuple-element.119.refs_0_, bf16[2,32,1024]{2,1,0:T(8,128)(2,1)S(1)} %collective-permute-done.15.refs_1_, ...), custom_call_target="tpu_custom_call" | custom-call | bytes 2097152 | tf_op jit(solution)/shard_map/pallas_call | solution.py:343
  (33 shorter events, 7.3 us)
Async XLA Ops:
  0.6 1.7 %copy-start = (bf16[256,512]{1,0:T(8,128)(2,1)S(1)}, bf16[256,512]{1,0:T(8,128)(2,1)}, u32[]{:S(2)}) copy-start(bf16[256,512]{1,0:T(8,128)(2,1)} %field_ref.1) | copy-start | bytes 786436
  1.6 0.7 %copy-start.3 = (f32[256]{0:T(256)S(1)}, f32[256]{0:T(256)}, u32[]{:S(2)}) copy-start(f32[256]{0:T(256)} %param.12) | copy-start | bytes 3076
  1.6 0.7 %copy-start.1 = (s32[125,4]{0,1:T(4,128)S(1)}, s32[125,4]{0,1:T(4,128)}, u32[]{:S(2)}) copy-start(s32[125,4]{0,1:T(4,128)} %param.10) | copy-start | bytes 6004
  1.7 0.7 %copy-start.2 = (f32[256]{0:T(256)S(1)}, f32[256]{0:T(256)}, u32[]{:S(2)}) copy-start(f32[256]{0:T(256)} %param.13) | copy-start | bytes 3076
  1.7 0.7 %copy-start.4 = (s32[1,64]{1,0:T(1,128)S(1)}, s32[1,64]{1,0:T(1,128)}, u32[]{:S(2)}) copy-start(s32[1,64]{1,0:T(1,128)} %param.11) | copy-start | bytes 772
  2.9 7.1 %collective-permute-start = (bf16[544,128]{1,0:T(8,128)(2,1)S(1)}, bf16[544,128]{1,0:T(8,128)(2,1)S(1)}, u32[]{:S(2)}, u32[]{:S(2)}) collective-permute-start(bf16[544,128]{1,0:T(8,128)(2,1)S(1)} %get-tuple-element.65), channel_id=1, source_target_pairs={{0,1},{1,0},{2,3},{3,2},{4,5},{5,4},{6,7},{7,6},{8,9},{9,8},{10,11... | collective-permute-start | bytes 417800 | tf_op jit(solution)/shard_map/ppermute | solution.py:419
  5.9 8.1 %collective-permute-start.1 = (bf16[544,128]{1,0:T(8,128)(2,1)S(1)}, bf16[544,128]{1,0:T(8,128)(2,1)S(1)}, u32[]{:S(2)}, u32[]{:S(2)}) collective-permute-start(bf16[544,128]{1,0:T(8,128)(2,1)S(1)} %get-tuple-element.66), channel_id=1, source_target_pairs={{0,2},{1,3},{2,0},{3,1},{4,6},{5,7},{6,4},{7,5},{8,10},{9,11},{10,... | collective-permute-start | bytes 417800 | tf_op jit(solution)/shard_map/ppermute | solution.py:419
  7.4 7.3 %collective-permute-start.2 = (bf16[544,128]{1,0:T(8,128)(2,1)S(1)}, bf16[544,128]{1,0:T(8,128)(2,1)S(1)}, u32[]{:S(2)}, u32[]{:S(2)}) collective-permute-start(bf16[544,128]{1,0:T(8,128)(2,1)S(1)} %get-tuple-element.67), channel_id=1, source_target_pairs={{0,3},{1,2},{2,1},{3,0},{4,7},{5,6},{6,5},{7,4},{8,11},{9,10},{10,... | collective-permute-start | bytes 417800 | tf_op jit(solution)/shard_map/ppermute | solution.py:419
  17.9 5.7 %collective-permute-start.3 = (bf16[384,128]{1,0:T(8,128)(2,1)S(1)}, bf16[384,128]{1,0:T(8,128)(2,1)S(1)}, u32[]{:S(2)}, u32[]{:S(2)}) collective-permute-start(bf16[384,128]{1,0:T(8,128)(2,1)S(1)} %get-tuple-element.104), channel_id=1, source_target_pairs={{0,4},{1,5},{2,6},{3,7},{4,0},{5,1},{6,2},{7,3},{8,12},{9,13},{10,... | collective-permute-start | bytes 294920 | tf_op jit(solution)/shard_map/ppermute | solution.py:476
  19.5 6.4 %collective-permute-start.4 = (bf16[384,128]{1,0:T(8,128)(2,1)S(1)}, bf16[384,128]{1,0:T(8,128)(2,1)S(1)}, u32[]{:S(2)}, u32[]{:S(2)}) collective-permute-start(bf16[384,128]{1,0:T(8,128)(2,1)S(1)} %get-tuple-element.105), channel_id=1, source_target_pairs={{0,12},{1,13},{2,14},{3,15},{4,8},{5,9},{6,10},{7,11},{8,4},{9,5},... | collective-permute-start | bytes 294920 | tf_op jit(solution)/shard_map/ppermute | solution.py:476
  28.6 9.1 %collective-permute-start.5 = (bf16[1024,128]{1,0:T(8,128)(2,1)S(1)}, bf16[1024,128]{1,0:T(8,128)(2,1)S(1)}, u32[]{:S(2)}, u32[]{:S(2)}) collective-permute-start(bf16[1024,128]{1,0:T(8,128)(2,1)S(1)} %get-tuple-element.115.filtered_ref.refs_0_), channel_id=1, source_target_pairs={{0,1},{1,0},{2,3},{3,2},{4,5},{5,4},{6,7},{7,6},{8,9},{9,8},{10,11... | collective-permute-start | bytes 786440 | tf_op jit(solution)/shard_map/ppermute | solution.py:419
  29.1 10.7 %collective-permute-start.9 = (bf16[1024,128]{1,0:T(8,128)(2,1)S(1)}, bf16[1024,128]{1,0:T(8,128)(2,1)S(1)}, u32[]{:S(2)}, u32[]{:S(2)}) collective-permute-start(bf16[1024,128]{1,0:T(8,128)(2,1)S(1)} %get-tuple-element.115.filtered_ref.refs_0_), channel_id=1, source_target_pairs={{0,3},{1,2},{2,1},{3,0},{4,7},{5,6},{6,5},{7,4},{8,11},{9,10},{10,... | collective-permute-start | bytes 786440 | tf_op jit(solution)/shard_map/ppermute | solution.py:419
  31.6 9.6 %collective-permute-start.8 = (bf16[1024,128]{1,0:T(8,128)(2,1)S(1)}, bf16[1024,128]{1,0:T(8,128)(2,1)S(1)}, u32[]{:S(2)}, u32[]{:S(2)}) collective-permute-start(bf16[1024,128]{1,0:T(8,128)(2,1)S(1)} %get-tuple-element.115.filtered_ref.refs_0_), channel_id=1, source_target_pairs={{0,2},{1,3},{2,0},{3,1},{4,6},{5,7},{6,4},{7,5},{8,10},{9,11},{10,... | collective-permute-start | bytes 786440 | tf_op jit(solution)/shard_map/ppermute | solution.py:419
  32.1 3.7 %collective-permute-start.6 = (bf16[64,128]{1,0:T(8,128)(2,1)S(1)}, bf16[64,128]{1,0:T(8,128)(2,1)S(1)}, u32[]{:S(2)}, u32[]{:S(2)}) collective-permute-start(bf16[64,128]{1,0:T(8,128)(2,1)S(1)} %get-tuple-element.107), channel_id=1, source_target_pairs={{0,4},{1,5},{2,6},{3,7},{4,0},{5,1},{6,2},{7,3},{8,12},{9,13},{10,... | collective-permute-start | bytes 49160 | tf_op jit(solution)/shard_map/ppermute | solution.py:476
  32.1 5.5 %collective-permute-start.7 = (bf16[64,128]{1,0:T(8,128)(2,1)S(1)}, bf16[64,128]{1,0:T(8,128)(2,1)S(1)}, u32[]{:S(2)}, u32[]{:S(2)}) collective-permute-start(bf16[64,128]{1,0:T(8,128)(2,1)S(1)} %get-tuple-element.108), channel_id=1, source_target_pairs={{0,12},{1,13},{2,14},{3,15},{4,8},{5,9},{6,10},{7,11},{8,4},{9,5},... | collective-permute-start | bytes 49160 | tf_op jit(solution)/shard_map/ppermute | solution.py:476
  37.7 5.1 %collective-permute-start.10 = (bf16[1024,128]{1,0:T(8,128)(2,1)S(1)}, bf16[1024,128]{1,0:T(8,128)(2,1)S(1)}, u32[]{:S(2)}, u32[]{:S(2)}) collective-permute-start(bf16[1024,128]{1,0:T(8,128)(2,1)S(1)} %get-tuple-element.115.filtered_ref.refs_0_), channel_id=1, source_target_pairs={{0,16},{16,0},{1,17},{17,1},{2,18},{18,2},{3,19},{19,3},{4,20},{20... | collective-permute-start | bytes 786440 | tf_op jit(solution)/shard_map/ppermute | solution.py:425
  39.9 2.6 %collective-permute-start.13 = (bf16[1024,128]{1,0:T(8,128)(2,1)S(1)}, bf16[1024,128]{1,0:T(8,128)(2,1)S(1)}, u32[]{:S(2)}, u32[]{:S(2)}) collective-permute-start(bf16[1024,128]{1,0:T(8,128)(2,1)S(1)} %collective-permute-done.9.refs_3_), channel_id=1, source_target_pairs={{0,16},{16,0},{1,17},{17,1},{2,18},{18,2},{3,19},{19,3},{4,20},{20... | collective-permute-start | bytes 786440 | tf_op jit(solution)/shard_map/ppermute | solution.py:425
  41.2 1.5 %collective-permute-start.12 = (bf16[1024,128]{1,0:T(8,128)(2,1)S(1)}, bf16[1024,128]{1,0:T(8,128)(2,1)S(1)}, u32[]{:S(2)}, u32[]{:S(2)}) collective-permute-start(bf16[1024,128]{1,0:T(8,128)(2,1)S(1)} %collective-permute-done.8.refs_2_), channel_id=1, source_target_pairs={{0,16},{16,0},{1,17},{17,1},{2,18},{18,2},{3,19},{19,3},{4,20},{20... | collective-permute-start | bytes 786440 | tf_op jit(solution)/shard_map/ppermute | solution.py:425
  41.2 1.9 %collective-permute-start.11 = (bf16[1024,128]{1,0:T(8,128)(2,1)S(1)}, bf16[1024,128]{1,0:T(8,128)(2,1)S(1)}, u32[]{:S(2)}, u32[]{:S(2)}) collective-permute-start(bf16[1024,128]{1,0:T(8,128)(2,1)S(1)} %collective-permute-done.5.refs_1_), channel_id=1, source_target_pairs={{0,16},{16,0},{1,17},{17,1},{2,18},{18,2},{3,19},{19,3},{4,20},{20... | collective-permute-start | bytes 786440 | tf_op jit(solution)/shard_map/ppermute | solution.py:425
  43.9 10.7 %collective-permute-start.14 = (bf16[2,32,1024]{2,1,0:T(8,128)(2,1)S(1)}, bf16[2,32,1024]{2,1,0:T(8,128)(2,1)S(1)}, u32[]{:S(2)}, u32[]{:S(2)}) collective-permute-start(bf16[2,32,1024]{2,1,0:T(8,128)(2,1)S(1)} %get-tuple-element.114), channel_id=1, source_target_pairs={{0,8},{1,9},{2,10},{3,11},{4,12},{5,13},{6,14},{7,15},{8,0},{9,1},... | collective-permute-start | bytes 393224 | tf_op jit(solution)/shard_map/ppermute | solution.py:514
  45.4 10.3 %collective-permute-start.15 = (bf16[2,32,1024]{2,1,0:T(8,128)(2,1)S(1)}, bf16[2,32,1024]{2,1,0:T(8,128)(2,1)S(1)}, u32[]{:S(2)}, u32[]{:S(2)}) collective-permute-start(bf16[2,32,1024]{2,1,0:T(8,128)(2,1)S(1)} %get-tuple-element.120), channel_id=1, source_target_pairs={{0,4},{1,5},{2,6},{3,7},{4,0},{5,1},{6,2},{7,3},{8,12},{9,13},{10,... | collective-permute-start | bytes 393224 | tf_op jit(solution)/shard_map/ppermute | solution.py:514
  47.0 9.6 %collective-permute-start.16 = (bf16[2,32,1024]{2,1,0:T(8,128)(2,1)S(1)}, bf16[2,32,1024]{2,1,0:T(8,128)(2,1)S(1)}, u32[]{:S(2)}, u32[]{:S(2)}) collective-permute-start(bf16[2,32,1024]{2,1,0:T(8,128)(2,1)S(1)} %get-tuple-element.122), channel_id=1, source_target_pairs={{0,12},{1,13},{2,14},{3,15},{4,8},{5,9},{6,10},{7,11},{8,4},{9,5},... | collective-permute-start | bytes 393224 | tf_op jit(solution)/shard_map/ppermute | solution.py:514

commit v4 on v3

--- a/solution.py
+++ b/solution.py
@@ -9,6 +9,7 @@
 
 FILTER_DEG = 4
 GROUP = 4
+HELD = (0, 1, 3, 2)
 LANES = 128
 EXTRA = 32
 F32 = jnp.float32
@@ -74,29 +75,22 @@
         out_refs[k][0:nodes, :] = dot(field_ref[...], pick.astype(F32).astype(BF16)).astype(BF16)
 
 
-def apply_plane(own, down, up, fields, outside_u, outside_g, keep=None):
-    shared = down[0].shape[0] // 2
-    traces = [dot(down[i], fields[i]) for i in range(GROUP)]
-    to_next = traces[GROUP - 1][:shared]
-    to_previous = traces[0][shared:]
-    w, g = outside_u, outside_g
-    if callable(outside_u):
-        w, g = outside_u(to_previous, to_next)
+def apply_plane(whole, up, fields, outside, keep=range(GROUP)):
+    shared = up[0].shape[1] // 2
+    nodes = up[0].shape[0]
+    products = [dot(matrix, field) for matrix, field in zip(whole, fields)]
+    to_next = [product[nodes : nodes + shared] for product in products]
+    to_previous = [product[nodes + shared :] for product in products]
+    nothing = jnp.zeros_like(to_next[0])
+    below, above = outside(to_previous[0], to_next[GROUP - 1]) if outside else (nothing, nothing)
     sums = []
     for i in range(GROUP):
-        if keep is not None and i not in keep:
+        if i not in keep:
             sums.append(None)
             continue
-        below = w if i == 0 else traces[i - 1][:shared]
-        above = g if i == GROUP - 1 else traces[i + 1][shared:]
-        total = dot(own[i], fields[i])
-        if below is None:
-            below = jnp.zeros_like(to_next)
-        if above is None:
-            above = jnp.zeros_like(to_next)
-        sides = jnp.concatenate([above, below], axis=0).astype(BF16)
-        sums.append(total + dot(up[i], sides))
-    return sums, traces
+        sides = [above if i == GROUP - 1 else to_previous[i + 1], below if i == 0 else to_next[i - 1]]
+        sums.append(products[i][:nodes] + dot(up[i], jnp.concatenate(sides, axis=0).astype(BF16)))
+    return sums, to_next[GROUP - 1], to_previous[0]
 
 
 def build_kernel(
@@ -109,8 +103,16 @@
     line, lane = iota((LANES, LANES), 0), iota((LANES, LANES), 1)
     nothing = jnp.zeros((LANES, LANES), F32)
     extra = ref[base : base + EXTRA, :].astype(F32)
-    ids = (64.0 * extra[0:cells] + extra[cells : 2 * cells]).astype(jnp.int32)
-    picks, parts = [], []
+    ids = 64.0 * extra[0:cells] + extra[cells : 2 * cells]
+    row = 2 * cells + 1
+    tables = [ids]
+    for first in (row, row + 3 * halves):
+        tables.append(sum(extra[first + j * halves : first + (j + 1) * halves] for j in range(3)))
+    tables.append(jnp.zeros((LANES - cells - 2 * halves, LANES), F32))
+    columns = jnp.transpose(jnp.concatenate(tables, axis=0))
+    ids = ids.astype(jnp.int32)
+    id_columns = columns[:, 0:cells].astype(jnp.int32)
+    lefts, rights = [], []
     for c in range(cells):
         square = ref[nodes + c // 2 * LANES : nodes + (c // 2 + 1) * LANES, :].astype(F32)
         if c % 2 == 0:
@@ -118,10 +120,11 @@
         else:
             matrix = jnp.where((line > lane) & (line < corners), square, nothing)
             matrix = matrix + jnp.where(line == lane, square[LANES - 1 :], nothing)
+        matrix = (matrix + jnp.transpose(matrix)).astype(BF16)
         pick = (iota((both, LANES), 0) == ids[c : c + 1]).astype(F32).astype(BF16)
-        picks.append(pick)
-        parts.append(dot(pick, matrix.astype(BF16)).astype(BF16))
-    total = dot_nt(jnp.concatenate(parts + picks, axis=1), jnp.concatenate(picks + parts, axis=1))
+        lefts.append(dot(pick, matrix).astype(BF16))
+        rights.append((iota((LANES, both), 1) == id_columns[:, c : c + 1]).astype(F32).astype(BF16))
+    total = dot(jnp.concatenate(lefts, axis=1), jnp.concatenate(rights, axis=0))
     own_ref[...] = total[:nodes, :nodes]
     corner_ref[...] = total[nodes:, nodes:]
     own_shared = extra[2 * cells : 2 * cells + 1, 0:shared].astype(jnp.int32)
@@ -129,14 +132,11 @@
     sides = jnp.concatenate([total[:nodes, nodes:], place_in], axis=1)
     up_ref[...] = sides.astype(BF16)
     down_ref[...] = jnp.transpose(sides).astype(BF16)
-    row = 2 * cells + 1
     for h in range(halves):
         at = slice(h * LANES, (h + 1) * LANES)
-        mass_row = sum(extra[row + j * halves + h : row + j * halves + h + 1] for j in range(3))
-        off = row + 3 * halves
-        pot_row = sum(extra[off + j * halves + h : off + j * halves + h + 1] for j in range(3))
-        mass = jnp.transpose(jnp.broadcast_to(mass_row, (LANES, LANES)))
-        pot = jnp.transpose(jnp.broadcast_to(pot_row, (LANES, LANES)))
+        mass = jnp.broadcast_to(columns[:, cells + h : cells + h + 1], (LANES, LANES))
+        off = cells + halves + h
+        pot = jnp.broadcast_to(columns[:, off : off + 1], (LANES, LANES))
         mass_ref[at, :] = mass
         scale_ref[at, :] = mass / half
         diag_ref[at, :] = (pot - center) / half
@@ -145,11 +145,11 @@
 def first_kernel(shared, place_ref, odd_ref, *refs):
     messages, refs = refs[:GROUP], refs[GROUP:]
     slabs = [refs[7 * k : 7 * k + 7] for k in range(GROUP)]
-    own_ref, down_ref, up_ref, mass_ref, scale_ref, diag_ref, start_ref = refs[7 * GROUP : 7 * GROUP + 7]
-    keep_ref, pair0_ref, pair1_ref, raw, corner, cur, prev, box = refs[7 * GROUP + 7 :]
+    whole_ref, up_ref, mass_ref, scale_ref, diag_ref, start_ref = refs[7 * GROUP : 7 * GROUP + 6]
+    keep_ref, pair0_ref, pair1_ref, raw, corner, cur, prev, box = refs[7 * GROUP + 6 :]
     next_ref, previous_ref = box.at[0], box.at[1]
     place = place_ref[0]
-    nodes = own_ref.shape[1]
+    nodes = whole_ref.shape[2]
     for k in range(GROUP):
         slab = place ^ k
         at = pl.ds(pl.multiple_of(slab * nodes, nodes), nodes)
@@ -158,15 +158,15 @@
         raw[slab] = own_k[...]
         corner[slab] = corner_k[...]
         up_ref[slab] = up_k[...]
-        down_ref[slab] = down_k[...]
+        whole_ref[slab, nodes:, :] = down_k[...]
         mass_ref[at, :] = mass_k[...]
         scale_ref[at, :] = scale_k[...]
         diag_ref[at, :] = diag_k[...]
-    own_ref[0] = raw[0].astype(BF16)
+    whole_ref[0, 0:nodes, :] = raw[0].astype(BF16)
     for i in range(1, GROUP):
-        place_in = up_ref[i][:, shared:]
-        moved = dot(place_in, corner[i - 1].astype(BF16)).astype(BF16)
-        own_ref[i] = (raw[i] + dot_nt(moved, place_in)).astype(BF16)
+        moved = dot(corner[i - 1].astype(BF16), whole_ref[i, nodes + shared :, :])
+        moved = jnp.concatenate([jnp.zeros_like(moved), moved], axis=0).astype(BF16)
+        whole_ref[i, 0:nodes, :] = (raw[i] + dot(up_ref[i], moved)).astype(BF16)
 
     cur[:, 0:LANES] = start_ref[...].astype(F32)
     cur[:, LANES:] = jnp.zeros((GROUP * nodes, 2 * shared), F32)
@@ -180,8 +180,7 @@
     cur[top:, LANES:] = cur[top:, LANES:] + jnp.where(lane >= shared, swapped * scale_ref[top:, :], 0.0)
     prev[...] = jnp.zeros_like(prev)
 
-    own = [own_ref[i] for i in range(GROUP)]
-    down = [down_ref[i] for i in range(GROUP)]
+    whole = [whole_ref[i] for i in range(GROUP)]
     up = [up_ref[i] for i in range(GROUP)]
 
     def wide(ref, i):
@@ -194,14 +193,12 @@
         if last_step:
             field0 = (mass_ref[0:nodes, :] * cur[0:nodes, 0:LANES]).astype(BF16)
             field3 = (mass_ref[top:, :] * cur[top:, 0:LANES]).astype(BF16)
-            next_ref[k * shared : (k + 1) * shared, :] = dot(down[GROUP - 1], field3)[:shared].astype(BF16)
-            previous_ref[k * shared : (k + 1) * shared, :] = dot(down[0], field0)[shared:].astype(BF16)
+            next_ref[k * shared : (k + 1) * shared, :] = dot(whole_ref[GROUP - 1, nodes:, :], field3)[:shared].astype(BF16)
+            previous_ref[k * shared : (k + 1) * shared, :] = dot(whole_ref[0, nodes:, :], field0)[shared:].astype(BF16)
             break
         fields = [(wide(mass_ref, i) * cur[i * nodes : (i + 1) * nodes, :]).astype(BF16) for i in range(GROUP)]
-        keep = None if k < FILTER_DEG - 2 else (0, GROUP - 1)
-        sums, traces = apply_plane(own, down, up, fields, None, None, keep)
-        to_next = traces[GROUP - 1][:shared]
-        to_previous = traces[0][shared:]
+        keep = range(GROUP) if k < FILTER_DEG - 2 else (0, GROUP - 1)
+        sums, to_next, to_previous = apply_plane(whole, up, fields, None, keep)
         next_ref[k * shared : (k + 1) * shared, :] = to_next[:, 0:LANES].astype(BF16)
         previous_ref[k * shared : (k + 1) * shared, :] = to_previous[:, 0:LANES].astype(BF16)
         next_parts.append(to_next[:, LANES + shared :])
@@ -236,16 +233,15 @@
 
 
 def second_kernel(
-    shared, odd_ref, own_ref, down_ref, up_ref, mass_ref, scale_ref, diag_ref, start_ref, keep_ref, from0_ref, from1_ref,
+    shared, odd_ref, whole_ref, up_ref, mass_ref, scale_ref, diag_ref, start_ref, keep_ref, from0_ref, from1_ref,
     filtered_ref, corner_ref, pair0_ref, pair1_ref, cur, prev, box,
 ):
     odd = odd_ref[0]
     box[0] = from0_ref[...]
     box[1] = from1_ref[...]
     above_ref, below_ref = box.at[odd], box.at[1 - odd]
-    nodes = own_ref.shape[1]
-    own = [own_ref[i] for i in range(GROUP)]
-    down = [down_ref[i] for i in range(GROUP)]
+    nodes = whole_ref.shape[2]
+    whole = [whole_ref[i] for i in range(GROUP)]
     up = [up_ref[i] for i in range(GROUP)]
     at = FILTER_DEG * shared
     near_b, far_b = below_ref[at : at + shared, :], below_ref[at + shared : at + 2 * shared, :]
@@ -253,8 +249,6 @@
     mine = keep_ref[...]
     corner_ref[...] = far_b
     zero = jnp.zeros((shared, LANES), BF16)
-    cur[...] = start_ref[...].astype(F32)
-    prev[...] = jnp.zeros_like(prev)
     below_past, above_past = [], []
 
     def past(items, lag):
@@ -281,36 +275,38 @@
             above_past.append(force.astype(BF16))
             return below, above
 
-        fields = [
-            (mass_ref[i * nodes : (i + 1) * nodes, :] * cur[i * nodes : (i + 1) * nodes, :]).astype(BF16)
-            for i in range(GROUP)
-        ]
-        sums, _ = apply_plane(own, down, up, fields, outside, None)
+        fields, values = [], []
         for i in range(GROUP):
             rows = slice(i * nodes, (i + 1) * nodes)
-            now = cur[rows, :]
-            image = scale_ref[rows, :] * sums[i] + diag_ref[rows, :] * now
+            values.append(start_ref[rows, :].astype(F32) if k == 0 else cur[rows, :])
+            fields.append((mass_ref[rows, :] * values[i]).astype(BF16))
+        sums, _, _ = apply_plane(whole, up, fields, outside)
+        for i in range(GROUP):
+            rows = slice(i * nodes, (i + 1) * nodes)
+            image = scale_ref[rows, :] * sums[i] + diag_ref[rows, :] * values[i]
             new = image if k == 0 else 2.0 * image - prev[rows, :]
-            prev[rows, :] = now
-            cur[rows, :] = new
-    filtered_ref[...] = cur[...].astype(BF16)
+            if k == FILTER_DEG - 1:
+                filtered_ref[rows, :] = new.astype(BF16)
+            else:
+                prev[rows, :] = values[i]
+                cur[rows, :] = new
     top = (GROUP - 1) * nodes
     field0 = (mass_ref[0:nodes, :] * filtered_ref[0:nodes, :].astype(F32)).astype(BF16)
     field3 = (mass_ref[top:, :] * filtered_ref[top:, :].astype(F32)).astype(BF16)
-    box[0, 0:shared, :] = dot(down[GROUP - 1], field3)[:shared].astype(BF16)
-    box[1, 0:shared, :] = dot(down[0], field0)[shared:].astype(BF16)
+    box[0, 0:shared, :] = dot(whole_ref[GROUP - 1, nodes:, :], field3)[:shared].astype(BF16)
+    box[1, 0:shared, :] = dot(whole_ref[0, nodes:, :], field0)[shared:].astype(BF16)
     pair0_ref[...] = box[odd, 0:shared, :]
     pair1_ref[...] = box[1 - odd, 0:shared, :]
 
 
 def third_kernel(
-    shared, odd_ref, center_ref, half_ref, own_ref, down_ref, up_ref, mass_ref, diag_ref, filtered_ref, corner_ref,
-    from0_ref, from1_ref, left_ref, box,
+    shared, odd_ref, center_ref, half_ref, whole_ref, up_ref, mass_ref, diag_ref, filtered_ref, corner_ref,
+    from0_ref, from1_ref, *refs,
 ):
-    nodes = own_ref.shape[1]
+    left_ref, box = refs[-2:]
+    nodes = whole_ref.shape[2]
     center, half = center_ref[0], half_ref[0]
-    own = [own_ref[i] for i in range(GROUP)]
-    down = [down_ref[i] for i in range(GROUP)]
+    whole = [whole_ref[i] for i in range(GROUP)]
     up = [up_ref[i] for i in range(GROUP)]
     odd = odd_ref[0]
     box[0] = from0_ref[...]
@@ -326,7 +322,7 @@
 
     values = [filtered_ref[i * nodes : (i + 1) * nodes, :].astype(F32) for i in range(GROUP)]
     fields = [(mass_ref[i * nodes : (i + 1) * nodes, :] * values[i]).astype(BF16) for i in range(GROUP)]
-    sums, _ = apply_plane(own, down, up, fields, outside, None)
+    sums, _, _ = apply_plane(whole, up, fields, outside)
     for i in range(GROUP):
         rows = slice(i * nodes, (i + 1) * nodes)
         pot = diag_ref[rows, :] * half + center
@@ -351,18 +347,25 @@
     )(*args)
 
 
-def product_kernel(planes, partner, plane_ref, left_ref, *refs):
+def product_kernel(left_ref, *refs):
+    chunks, out = refs[:-1], refs[-1]
+    left = left_ref[...]
+    for c in range(0, len(chunks), 2):
+        right = jnp.concatenate([chunks[c][...], chunks[c + 1][...]], axis=1)
+        out[:, c * LANES : (c + 2) * LANES] = dot(left, right).astype(out.dtype)
+
+
+def cut_kernel(planes, partner, plane_ref, left_ref, half_ref, *refs):
     chunks, outs, total = refs[: -planes - 1], refs[-planes - 1 : -1], refs[-1]
     plane = plane_ref[0]
     rows = LANES // planes
-    left = left_ref[...]
-    for c in range(0, len(chunks), 2):
-        right = jnp.concatenate([chunks[c][...], chunks[c + 1][...]], axis=1)
-        total[:, c * LANES : (c + 2) * LANES] = dot(left, right)
+    width = half_ref.shape[1]
+    product_kernel(left_ref, *chunks, total)
     for k, out in enumerate(outs):
         for mat in range(2):
             at = pl.ds(pl.multiple_of(mat * LANES + partner(plane, k) * rows, rows), rows)
-            out[mat] = total[at, :].astype(out.dtype)
+            out[mat, :, 0:width] = half_ref[at, :].astype(out.dtype)
+            out[mat, :, width:] = total[at, :].astype(out.dtype)
 
 
 def arrange_kernel(planes, place_ref, *refs):
@@ -375,7 +378,7 @@
     target = iota((LANES, width), 1)
     total = jnp.zeros((nodes, width), F32)
     for k, chunk in enumerate(chunks):
-        wanted = (source // rows) * (GROUP * rows) + (place ^ k) * rows + source % rows
+        wanted = (source // rows) * (GROUP * rows) + (place ^ HELD[k]) * rows + source % rows
         total = total + dot(chunk[at, :], (wanted == target).astype(F32).astype(BF16))
     out[...] = total.astype(BF16)
 
@@ -389,7 +392,9 @@
         for j in range(bands):
             chunks = []
             for c in range(GROUP):
-                at = pl.ds(pl.multiple_of(j * width + (place ^ c) * LANES, LANES), LANES)
+                slot = place ^ c
+                slot = jnp.where(slot > 1, 5 - slot, slot)
+                at = pl.ds(pl.multiple_of(j * width + slot * LANES, LANES), LANES)
                 chunks.append(sum(part[mat, :, at].astype(F32) for part in parts) * factor)
             columns = [
                 jnp.concatenate([chunk[:, z * rows : (z + 1) * rows] for chunk in chunks], axis=1)
@@ -453,10 +458,10 @@
     column = ((height, LANES), F32)
     trace = ((FILTER_DEG * shared + 2 * shared, LANES), BF16)
     odd_arg = (plane % 2).astype(jnp.int32).reshape(1)
-    own, down, up, mass, scale, diag, start, keep, *pairs = call(
+    whole, up, mass, scale, diag, start, keep, *pairs = call(
         functools.partial(first_kernel, shared),
         [
-            ((GROUP, nodes, nodes), BF16), ((GROUP, 2 * shared, nodes), BF16), ((GROUP, nodes, 2 * shared), BF16),
+            ((GROUP, nodes + 2 * shared, nodes), BF16), ((GROUP, nodes, 2 * shared), BF16),
             column, column, column, ((height, LANES), BF16), ((shared, LANES), BF16), trace, trace,
         ],
         (place_arg, odd_arg, *messages, *slabs),
@@ -479,19 +484,20 @@
     mine, corner, *pairs = call(
         functools.partial(second_kernel, shared),
         [((height, LANES), BF16)] + [((shared, LANES), BF16)] * 3,
-        (odd_arg, own, down, up, mass, scale, diag, start, keep, *heard),
-        spaces="s" + "v" * 10,
+        (odd_arg, whole, up, mass, scale, diag, start, keep, *heard),
+        spaces="s" + "v" * 9,
         scratch=[pltpu.VMEM((height, LANES), F32), pltpu.VMEM((height, LANES), F32), pltpu.VMEM((2, *trace[0]), BF16)],
         flops=1 << 30,
     )
     heard = with_neighbour(pairs)
-    others = [in_plane(mine, k) for k in range(1, GROUP)]
+    others = [in_plane(mine, k) for k in HELD[1:]]
     first, others[0], *heard = lax.optimization_barrier((mine, others[0], *heard))
+    swapped = [[to_band(block, k) for block in (first, others[0])] for k in range(1, band_count)]
     (left,) = call(
         functools.partial(third_kernel, shared),
         [((2 * LANES, height), BF16)],
-        (odd_arg, filter_center, filter_halfwidth, own, down, up, mass, diag, mine, corner, *heard),
-        spaces="sss" + "v" * 9,
+        (odd_arg, filter_center, filter_halfwidth, whole, up, mass, diag, mine, corner, *heard, *sum(swapped, [])),
+        spaces="sss" + "v" * 8 + "a" * 2 * (band_count - 1),
         scratch=[pltpu.VMEM((2, shared, LANES), BF16)],
         flops=1 << 28,
     )
@@ -499,14 +505,15 @@
     gathered = [mine] + others
     rights = list(gathered)
     for k in range(1, band_count):
-        rights += [to_band(block, k) for block in [first] + others]
+        rights += swapped[k - 1] + [to_band(block, k) for block in others[1:]]
     part = (2, rows, band_count * width)
+    (half,) = call(product_kernel, [((2 * LANES, width), F32)], (left, *rights[:GROUP]), flops=1 << 28)
     parts = list(call(
-        functools.partial(product_kernel, planes, partner),
+        functools.partial(cut_kernel, planes, partner),
         [(part, F32)] + [(part, BF16)] * (planes - 1),
-        (plane.astype(jnp.int32).reshape(1), left, *rights),
-        spaces="sv" + "v" * len(rights),
-        scratch=[pltpu.VMEM((2 * LANES, band_count * width), F32)],
+        (plane.astype(jnp.int32).reshape(1), left, half, *rights[GROUP:]),
+        spaces="svv" + "v" * (len(rights) - GROUP),
+        scratch=[pltpu.VMEM((2 * LANES, (band_count - 1) * width), F32)],
         flops=1 << 28,
     ))
     for k in [*range(2, planes), *range(1, min(planes, 2))]:

time: 57.8 us -> 56.7 us (0.981)
  waiting for transfers between devices: 21.3 us -> 19.9 us
    ppermute x6, waiting for transfers between devices: 7.31 us -> 6.24 us  [in_plane(): return lax.ppermute(block, 'dom', [(i, i ^ k) for i in everyone])]
    pallas_call x11 -> x12, Pallas kernels: 12.1 us -> 11.8 us  [call(): pl.pallas_call(kernel, out_shape=[jax.ShapeDtypeStruct(shape, dtype) for...]
  transfers between devices with their start and end apart: 17 -> 17, of which waited for: 12 -> 10; matrix products, arithmetic and copies ran while one was open for 0% -> 0% of each run, Pallas kernels for 7% -> 8%
where the time goes in v4:
time: 56.7 us; the launch traced here: 56.5 us
  starting transfers between devices  21 us (37%)
  waiting for transfers between devices  19.9 us (35%)
  Pallas kernels  11.8 us (21%)
  between operations  2.07 us (4%)
  local copies, waits for them, and re-layouts  1.65 us (3%)
    pallas_call x12, Pallas kernels, call(): pl.pallas_call(kernel, out_shape=[jax.ShapeDtypeStruct(shape, dtype) for...  11.8 us
    ppermute x6, starting transfers between devices, in_plane(): return lax.ppermute(block, 'dom', [(i, i ^ k) for i in everyone])  8.1 us
    ppermute x4, starting transfers between devices, with_neighbour(): lax.ppermute(block, 'dom', route)  7.42 us
    ppermute x3, waiting for transfers between devices, shards(): parts[k] = lax.ppermute(parts[k], 'dom', route)  7.37 us
    ppermute x6, waiting for transfers between devices, in_plane(): return lax.ppermute(block, 'dom', [(i, i ^ k) for i in everyone])  6.24 us
    ppermute x4, waiting for transfers between devices, with_neighbour(): lax.ppermute(block, 'dom', route)  6.18 us
    ppermute x3, starting transfers between devices, shards(): parts[k] = lax.ppermute(parts[k], 'dom', route)  4.45 us
    unnamed x11, local copies, waits for them, and re-layouts  1.65 us
  transfers between devices with their start and end apart: 17, of which 10 were waited for; matrix products, arithmetic and copies ran while one was open for 0% of the time, Pallas kernels for 8%

profile of v4, /device:TPU:0, one launch (start us, length us, event | category | flops | bytes accessed | tf_op | source)
XLA Modules:
  0.0 56.5 jit_solution(15488017969634667702)
XLA Ops:
  0.7 1.0 %copy.11.cells_ref = bf16[4,125,125]{2,1,0:T(8,128)(2,1)S(1)} copy(bf16[4,125,125]{2,0,1:T(4,128)(2,1)} %param.9) | data formatting | bytes 250000 | tf_op args[1]
  2.9 3.0 %collective-permute-start = (bf16[544,128]{1,0:T(8,128)(2,1)S(1)}, bf16[544,128]{1,0:T(8,128)(2,1)S(1)}, u32[]{:S(2)}, u32[]{:S(2)}) collective-permute-start(bf16[544,128]{1,0:T(8,128)(2,1)S(1)} %get-tuple-element.64), channel_id=1, source_target_pairs={{0,1},{1,0},{2,3},{3,2},{4,5},{5,4},{6,7},{7,6},{8,9},{9,8},{10,11... | collective-permute-start | bytes 417800 | tf_op jit(solution)/shard_map/ppermute | solution.py:424
  5.9 1.5 %collective-permute-start.1 = (bf16[544,128]{1,0:T(8,128)(2,1)S(1)}, bf16[544,128]{1,0:T(8,128)(2,1)S(1)}, u32[]{:S(2)}, u32[]{:S(2)}) collective-permute-start(bf16[544,128]{1,0:T(8,128)(2,1)S(1)} %get-tuple-element.65), channel_id=1, source_target_pairs={{0,2},{1,3},{2,0},{3,1},{4,6},{5,7},{6,4},{7,5},{8,10},{9,11},{10,... | collective-permute-start | bytes 417800 | tf_op jit(solution)/shard_map/ppermute | solution.py:424
  10.6 3.4 %collective-permute-done.1.ref.refs_2_ = bf16[544,128]{1,0:T(8,128)(2,1)S(1)} collective-permute-done((bf16[544,128]{1,0:T(8,128)(2,1)S(1)}, bf16[544,128]{1,0:T(8,128)(2,1)S(1)}, u32[]{:S(2)}, u32[]{:S(2)}) %collective-permute-start.1) | collective-permute-done | bytes 139296 | tf_op jit(solution)/shard_map/ppermute | solution.py:424
  14.6 0.6 %shard_map.107 = (f32[256,256]{1,0:T(8,128)S(1)}, f32[64,64]{1,0:T(8,128)S(1)}, bf16[256,128]{1,0:T(8,128)(2,1)S(1)}, bf16[128,256]{1,0:T(8,128)(2,1)S(1)}, f32[...) custom-call(f32[1]{0:T(128)S(6)} %copy.12.center_ref, f32[1]{0:T(128)S(6)} %copy.13.half_ref, ...), custom_call_target="tpu_custom_call" | custom-call | flops 268435456 | bytes 2097152 | tf_op jit(solution)/shard_map/pallas_call | solution.py:339
  15.3 2.3 %shard_map.108 = (bf16[4,384,256]{2,1,0:T(8,128)(2,1)S(1)}, bf16[4,256,128]{2,1,0:T(8,128)(2,1)S(1)}, f32[1024,128]{1,0:T(8,128)S(1)}, f32[1024,128]{1,0:T(8,128...) custom-call(s32[1]{0:T(128)} %bitcast.place_ref, ...), custom_call_target="tpu_custom_call" | custom-call | flops 1073741824 | bytes 2097152 | tf_op jit(solution)/shard_map/pallas_call | solution.py:339
  17.6 1.6 %collective-permute-start.3 = (bf16[384,128]{1,0:T(8,128)(2,1)S(1)}, bf16[384,128]{1,0:T(8,128)(2,1)S(1)}, u32[]{:S(2)}, u32[]{:S(2)}) collective-permute-start(bf16[384,128]{1,0:T(8,128)(2,1)S(1)} %get-tuple-element.102), channel_id=1, source_target_pairs={{0,4},{1,5},{2,6},{3,7},{4,0},{5,1},{6,2},{7,3},{8,12},{9,13},{10,... | collective-permute-start | bytes 294920 | tf_op jit(solution)/shard_map/ppermute | solution.py:481
  19.2 2.5 %collective-permute-start.4 = (bf16[384,128]{1,0:T(8,128)(2,1)S(1)}, bf16[384,128]{1,0:T(8,128)(2,1)S(1)}, u32[]{:S(2)}, u32[]{:S(2)}) collective-permute-start(bf16[384,128]{1,0:T(8,128)(2,1)S(1)} %get-tuple-element.103), channel_id=1, source_target_pairs={{0,12},{1,13},{2,14},{3,15},{4,8},{5,9},{6,10},{7,11},{8,4},{9,5},... | collective-permute-start | bytes 294920 | tf_op jit(solution)/shard_map/ppermute | solution.py:481
  21.7 1.6 %collective-permute-done.3.from0_ref = bf16[384,128]{1,0:T(8,128)(2,1)S(1)} collective-permute-done((bf16[384,128]{1,0:T(8,128)(2,1)S(1)}, bf16[384,128]{1,0:T(8,128)(2,1)S(1)}, u32[]{:S(2)}, u32[]{:S(2)}) %collective-permute-start.3) | collective-permute-done | bytes 98336 | tf_op jit(solution)/shard_map/ppermute | solution.py:481
  23.3 2.3 %collective-permute-done.4.from1_ref = bf16[384,128]{1,0:T(8,128)(2,1)S(1)} collective-permute-done((bf16[384,128]{1,0:T(8,128)(2,1)S(1)}, bf16[384,128]{1,0:T(8,128)(2,1)S(1)}, u32[]{:S(2)}, u32[]{:S(2)}) %collective-permute-start.4) | collective-permute-done | bytes 98336 | tf_op jit(solution)/shard_map/ppermute | solution.py:481
  25.6 2.7 %shard_map.109 = (bf16[1024,128]{1,0:T(8,128)(2,1)S(1)}, bf16[64,128]{1,0:T(8,128)(2,1)S(1)}, bf16[64,128]{1,0:T(8,128)(2,1)S(1)}, bf16[64,128]{1,0:T(8,128)(2,1)S(1)}) custom-call(s32[1]{0:T(128)} %bitcast.1.odd_ref, bf16[4,384,256]{2,1,0:T(8,128)(2,1)S(1)} %get-tuple-element.95.whole_ref, bf16[4,256,128]{2,1,0:T(8,128)(2,1)S(1)} %get-tuple-element.96.up_ref, ...), custom_call_target="tpu_custom_call" | custom-call | flops 1073741824 | bytes 2097152 | tf_op jit(solution)/shard_map/pallas_call | solution.py:339
  28.4 0.6 %collective-permute-start.5 = (bf16[1024,128]{1,0:T(8,128)(2,1)S(1)}, bf16[1024,128]{1,0:T(8,128)(2,1)S(1)}, u32[]{:S(2)}, u32[]{:S(2)}) collective-permute-start(bf16[1024,128]{1,0:T(8,128)(2,1)S(1)} %get-tuple-element.113.filtered_ref.refs_0_), channel_id=1, source_target_pairs={{0,1},{1,0},{2,3},{3,2},{4,5},{5,4},{6,7},{7,6},{8,9},{9,8},{10,11... | collective-permute-start | bytes 786440 | tf_op jit(solution)/shard_map/ppermute | solution.py:424
  29.0 1.5 %collective-permute-start.9 = (bf16[1024,128]{1,0:T(8,128)(2,1)S(1)}, bf16[1024,128]{1,0:T(8,128)(2,1)S(1)}, u32[]{:S(2)}, u32[]{:S(2)}) collective-permute-start(bf16[1024,128]{1,0:T(8,128)(2,1)S(1)} %get-tuple-element.113.filtered_ref.refs_0_), channel_id=1, source_target_pairs={{0,2},{1,3},{2,0},{3,1},{4,6},{5,7},{6,4},{7,5},{8,10},{9,11},{10,... | collective-permute-start | bytes 786440 | tf_op jit(solution)/shard_map/ppermute | solution.py:424
  30.5 1.4 %collective-permute-start.8 = (bf16[1024,128]{1,0:T(8,128)(2,1)S(1)}, bf16[1024,128]{1,0:T(8,128)(2,1)S(1)}, u32[]{:S(2)}, u32[]{:S(2)}) collective-permute-start(bf16[1024,128]{1,0:T(8,128)(2,1)S(1)} %get-tuple-element.113.filtered_ref.refs_0_), channel_id=1, source_target_pairs={{0,3},{1,2},{2,1},{3,0},{4,7},{5,6},{6,5},{7,4},{8,11},{9,10},{10,... | collective-permute-start | bytes 786440 | tf_op jit(solution)/shard_map/ppermute | solution.py:424
  31.9 3.3 %collective-permute-start.7 = (bf16[64,128]{1,0:T(8,128)(2,1)S(1)}, bf16[64,128]{1,0:T(8,128)(2,1)S(1)}, u32[]{:S(2)}, u32[]{:S(2)}) collective-permute-start(bf16[64,128]{1,0:T(8,128)(2,1)S(1)} %get-tuple-element.106), channel_id=1, source_target_pairs={{0,12},{1,13},{2,14},{3,15},{4,8},{5,9},{6,10},{7,11},{8,4},{9,5},... | collective-permute-start | bytes 49160 | tf_op jit(solution)/shard_map/ppermute | solution.py:481
  35.6 1.8 %collective-permute-done.7.from1_ref = bf16[64,128]{1,0:T(8,128)(2,1)S(1)} collective-permute-done((bf16[64,128]{1,0:T(8,128)(2,1)S(1)}, bf16[64,128]{1,0:T(8,128)(2,1)S(1)}, u32[]{:S(2)}, u32[]{:S(2)}) %collective-permute-start.7) | collective-permute-done | bytes 16416 | tf_op jit(solution)/shard_map/ppermute | solution.py:481
  38.0 2.2 %collective-permute-done.9.refs_3_ = bf16[1024,128]{1,0:T(8,128)(2,1)S(1)} collective-permute-done((bf16[1024,128]{1,0:T(8,128)(2,1)S(1)}, bf16[1024,128]{1,0:T(8,128)(2,1)S(1)}, u32[]{:S(2)}, u32[]{:S(2)}) %collective-permute-start.9) | collective-permute-done | bytes 262176 | tf_op jit(solution)/shard_map/ppermute | solution.py:424
  40.7 0.8 %shard_map.110.left_ref = bf16[256,1024]{1,0:T(8,128)(2,1)S(1)} custom-call(s32[1]{0:T(128)} %bitcast.1.odd_ref, f32[1]{0:T(128)S(6)} %copy.12.center_ref, f32[1]{0:T(128)S(6)} %copy.13.half_ref, bf16[4,384,256]{2,1,0:T(8,128)(2,1)S(1)} %get-tuple-element.95.whole_ref, bf16[4,256,128]{2,1,0:T(8,128)(2,1)S(1)} %get-tuple-element.96.up_ref, ...), custom_call_target="tpu_custom_call" | custom-call | flops 268435456 | bytes 2097152 | tf_op jit(solution)/shard_map/pallas_call | solution.py:339
  42.6 1.3 %collective-permute-start.14 = (bf16[2,32,1024]{2,1,0:T(8,128)(2,1)S(1)}, bf16[2,32,1024]{2,1,0:T(8,128)(2,1)S(1)}, u32[]{:S(2)}, u32[]{:S(2)}) collective-permute-start(bf16[2,32,1024]{2,1,0:T(8,128)(2,1)S(1)} %get-tuple-element.112), channel_id=1, source_target_pairs={{0,8},{1,9},{2,10},{3,11},{4,12},{5,13},{6,14},{7,15},{8,0},{9,1},... | collective-permute-start | bytes 393224 | tf_op jit(solution)/shard_map/ppermute | solution.py:521
  43.9 2.7 %collective-permute-start.15 = (bf16[2,32,1024]{2,1,0:T(8,128)(2,1)S(1)}, bf16[2,32,1024]{2,1,0:T(8,128)(2,1)S(1)}, u32[]{:S(2)}, u32[]{:S(2)}) collective-permute-start(bf16[2,32,1024]{2,1,0:T(8,128)(2,1)S(1)} %get-tuple-element.118), channel_id=1, source_target_pairs={{0,4},{1,5},{2,6},{3,7},{4,0},{5,1},{6,2},{7,3},{8,12},{9,13},{10,... | collective-permute-start | bytes 393224 | tf_op jit(solution)/shard_map/ppermute | solution.py:521
  47.0 6.1 %collective-permute-done.14.refs_2_ = bf16[2,32,1024]{2,1,0:T(8,128)(2,1)S(1)} collective-permute-done((bf16[2,32,1024]{2,1,0:T(8,128)(2,1)S(1)}, bf16[2,32,1024]{2,1,0:T(8,128)(2,1)S(1)}, u32[]{:S(2)}, u32[]{:S(2)}) %collective-permute-start.14) | collective-permute-done | bytes 131104 | tf_op jit(solution)/shard_map/ppermute | solution.py:521
  53.2 1.1 %shard_map.113 = bf16[256,512]{1,0:T(8,128)(2,1)} custom-call(s32[1]{0:T(128)} %bitcast.place_ref, bf16[1024,128]{1,0:T(8,128)(2,1)S(1)} %get-tuple-element.113.filtered_ref.refs_0_, bf16[1024,128]{1,0:T(8,128)(2,1)S(1)} %collective-permute-done.5.refs_1_, bf16[1024,128]{1,0:T(8,128)(2,1)S(1)} %collective-permute-done.8.refs_2_, ...), custom_call_target="tpu_custom_call" | custom-call | bytes 2097152 | tf_op jit(solution)/shard_map/pallas_call | solution.py:339
  54.3 1.3 %collective-permute-done.16.refs_3_ = bf16[2,32,1024]{2,1,0:T(8,128)(2,1)S(1)} collective-permute-done((bf16[2,32,1024]{2,1,0:T(8,128)(2,1)S(1)}, bf16[2,32,1024]{2,1,0:T(8,128)(2,1)S(1)}, u32[]{:S(2)}, u32[]{:S(2)}) %collective-permute-start.16) | collective-permute-done | bytes 131104 | tf_op jit(solution)/shard_map/ppermute | solution.py:521
  55.5 0.9 %shard_map.114 = (f32[32,1024]{1,0:T(8,128)}, f32[32,1024]{1,0:T(8,128)}) custom-call(s32[1]{0:T(128)} %bitcast.place_ref, s32[1]{0:T(128)} %bitcast.6.band_ref, f32[2,32,1024]{2,1,0:T(8,128)S(1)} %get-tuple-element.117.refs_0_, bf16[2,32,1024]{2,1,0:T(8,128)(2,1)S(1)} %collective-permute-done.15.refs_1_, ...), custom_call_target="tpu_custom_call" | custom-call | bytes 2097152 | tf_op jit(solution)/shard_map/pallas_call | solution.py:339
  (34 shorter events, 6.8 us)
Async XLA Ops:
  0.6 1.7 %copy-start = (bf16[256,512]{1,0:T(8,128)(2,1)S(1)}, bf16[256,512]{1,0:T(8,128)(2,1)}, u32[]{:S(2)}) copy-start(bf16[256,512]{1,0:T(8,128)(2,1)} %field_ref.1) | copy-start | bytes 786436
  1.6 0.7 %copy-start.3 = (f32[256]{0:T(256)S(1)}, f32[256]{0:T(256)}, u32[]{:S(2)}) copy-start(f32[256]{0:T(256)} %param.12) | copy-start | bytes 3076
  1.6 0.7 %copy-start.1 = (s32[125,4]{0,1:T(4,128)S(1)}, s32[125,4]{0,1:T(4,128)}, u32[]{:S(2)}) copy-start(s32[125,4]{0,1:T(4,128)} %param.10) | copy-start | bytes 6004
  1.7 0.7 %copy-start.2 = (f32[256]{0:T(256)S(1)}, f32[256]{0:T(256)}, u32[]{:S(2)}) copy-start(f32[256]{0:T(256)} %param.13) | copy-start | bytes 3076
  1.7 0.7 %copy-start.4 = (s32[1,64]{1,0:T(1,128)S(1)}, s32[1,64]{1,0:T(1,128)}, u32[]{:S(2)}) copy-start(s32[1,64]{1,0:T(1,128)} %param.11) | copy-start | bytes 772
  2.9 7.1 %collective-permute-start = (bf16[544,128]{1,0:T(8,128)(2,1)S(1)}, bf16[544,128]{1,0:T(8,128)(2,1)S(1)}, u32[]{:S(2)}, u32[]{:S(2)}) collective-permute-start(bf16[544,128]{1,0:T(8,128)(2,1)S(1)} %get-tuple-element.64), channel_id=1, source_target_pairs={{0,1},{1,0},{2,3},{3,2},{4,5},{5,4},{6,7},{7,6},{8,9},{9,8},{10,11... | collective-permute-start | bytes 417800 | tf_op jit(solution)/shard_map/ppermute | solution.py:424
  5.9 8.1 %collective-permute-start.1 = (bf16[544,128]{1,0:T(8,128)(2,1)S(1)}, bf16[544,128]{1,0:T(8,128)(2,1)S(1)}, u32[]{:S(2)}, u32[]{:S(2)}) collective-permute-start(bf16[544,128]{1,0:T(8,128)(2,1)S(1)} %get-tuple-element.65), channel_id=1, source_target_pairs={{0,2},{1,3},{2,0},{3,1},{4,6},{5,7},{6,4},{7,5},{8,10},{9,11},{10,... | collective-permute-start | bytes 417800 | tf_op jit(solution)/shard_map/ppermute | solution.py:424
  7.4 7.2 %collective-permute-start.2 = (bf16[544,128]{1,0:T(8,128)(2,1)S(1)}, bf16[544,128]{1,0:T(8,128)(2,1)S(1)}, u32[]{:S(2)}, u32[]{:S(2)}) collective-permute-start(bf16[544,128]{1,0:T(8,128)(2,1)S(1)} %get-tuple-element.66), channel_id=1, source_target_pairs={{0,3},{1,2},{2,1},{3,0},{4,7},{5,6},{6,5},{7,4},{8,11},{9,10},{10,... | collective-permute-start | bytes 417800 | tf_op jit(solution)/shard_map/ppermute | solution.py:424
  17.6 5.7 %collective-permute-start.3 = (bf16[384,128]{1,0:T(8,128)(2,1)S(1)}, bf16[384,128]{1,0:T(8,128)(2,1)S(1)}, u32[]{:S(2)}, u32[]{:S(2)}) collective-permute-start(bf16[384,128]{1,0:T(8,128)(2,1)S(1)} %get-tuple-element.102), channel_id=1, source_target_pairs={{0,4},{1,5},{2,6},{3,7},{4,0},{5,1},{6,2},{7,3},{8,12},{9,13},{10,... | collective-permute-start | bytes 294920 | tf_op jit(solution)/shard_map/ppermute | solution.py:481
  19.2 6.4 %collective-permute-start.4 = (bf16[384,128]{1,0:T(8,128)(2,1)S(1)}, bf16[384,128]{1,0:T(8,128)(2,1)S(1)}, u32[]{:S(2)}, u32[]{:S(2)}) collective-permute-start(bf16[384,128]{1,0:T(8,128)(2,1)S(1)} %get-tuple-element.103), channel_id=1, source_target_pairs={{0,12},{1,13},{2,14},{3,15},{4,8},{5,9},{6,10},{7,11},{8,4},{9,5},... | collective-permute-start | bytes 294920 | tf_op jit(solution)/shard_map/ppermute | solution.py:481
  28.4 9.1 %collective-permute-start.5 = (bf16[1024,128]{1,0:T(8,128)(2,1)S(1)}, bf16[1024,128]{1,0:T(8,128)(2,1)S(1)}, u32[]{:S(2)}, u32[]{:S(2)}) collective-permute-start(bf16[1024,128]{1,0:T(8,128)(2,1)S(1)} %get-tuple-element.113.filtered_ref.refs_0_), channel_id=1, source_target_pairs={{0,1},{1,0},{2,3},{3,2},{4,5},{5,4},{6,7},{7,6},{8,9},{9,8},{10,11... | collective-permute-start | bytes 786440 | tf_op jit(solution)/shard_map/ppermute | solution.py:424
  29.0 11.2 %collective-permute-start.9 = (bf16[1024,128]{1,0:T(8,128)(2,1)S(1)}, bf16[1024,128]{1,0:T(8,128)(2,1)S(1)}, u32[]{:S(2)}, u32[]{:S(2)}) collective-permute-start(bf16[1024,128]{1,0:T(8,128)(2,1)S(1)} %get-tuple-element.113.filtered_ref.refs_0_), channel_id=1, source_target_pairs={{0,2},{1,3},{2,0},{3,1},{4,6},{5,7},{6,4},{7,5},{8,10},{9,11},{10,... | collective-permute-start | bytes 786440 | tf_op jit(solution)/shard_map/ppermute | solution.py:424
  30.5 9.7 %collective-permute-start.8 = (bf16[1024,128]{1,0:T(8,128)(2,1)S(1)}, bf16[1024,128]{1,0:T(8,128)(2,1)S(1)}, u32[]{:S(2)}, u32[]{:S(2)}) collective-permute-start(bf16[1024,128]{1,0:T(8,128)(2,1)S(1)} %get-tuple-element.113.filtered_ref.refs_0_), channel_id=1, source_target_pairs={{0,3},{1,2},{2,1},{3,0},{4,7},{5,6},{6,5},{7,4},{8,11},{9,10},{10,... | collective-permute-start | bytes 786440 | tf_op jit(solution)/shard_map/ppermute | solution.py:424
  31.9 3.7 %collective-permute-start.6 = (bf16[64,128]{1,0:T(8,128)(2,1)S(1)}, bf16[64,128]{1,0:T(8,128)(2,1)S(1)}, u32[]{:S(2)}, u32[]{:S(2)}) collective-permute-start(bf16[64,128]{1,0:T(8,128)(2,1)S(1)} %get-tuple-element.105), channel_id=1, source_target_pairs={{0,4},{1,5},{2,6},{3,7},{4,0},{5,1},{6,2},{7,3},{8,12},{9,13},{10,... | collective-permute-start | bytes 49160 | tf_op jit(solution)/shard_map/ppermute | solution.py:481
  31.9 5.5 %collective-permute-start.7 = (bf16[64,128]{1,0:T(8,128)(2,1)S(1)}, bf16[64,128]{1,0:T(8,128)(2,1)S(1)}, u32[]{:S(2)}, u32[]{:S(2)}) collective-permute-start(bf16[64,128]{1,0:T(8,128)(2,1)S(1)} %get-tuple-element.106), channel_id=1, source_target_pairs={{0,12},{1,13},{2,14},{3,15},{4,8},{5,9},{6,10},{7,11},{8,4},{9,5},... | collective-permute-start | bytes 49160 | tf_op jit(solution)/shard_map/ppermute | solution.py:481
  37.5 3.3 %collective-permute-start.10 = (bf16[1024,128]{1,0:T(8,128)(2,1)S(1)}, bf16[1024,128]{1,0:T(8,128)(2,1)S(1)}, u32[]{:S(2)}, u32[]{:S(2)}) collective-permute-start(bf16[1024,128]{1,0:T(8,128)(2,1)S(1)} %get-tuple-element.113.filtered_ref.refs_0_), channel_id=1, source_target_pairs={{0,16},{16,0},{1,17},{17,1},{2,18},{18,2},{3,19},{19,3},{4,20},{20... | collective-permute-start | bytes 786440 | tf_op jit(solution)/shard_map/ppermute | solution.py:430
  37.5 3.3 %collective-permute-start.11 = (bf16[1024,128]{1,0:T(8,128)(2,1)S(1)}, bf16[1024,128]{1,0:T(8,128)(2,1)S(1)}, u32[]{:S(2)}, u32[]{:S(2)}) collective-permute-start(bf16[1024,128]{1,0:T(8,128)(2,1)S(1)} %collective-permute-done.5.refs_1_), channel_id=1, source_target_pairs={{0,16},{16,0},{1,17},{17,1},{2,18},{18,2},{3,19},{19,3},{4,20},{20... | collective-permute-start | bytes 786440 | tf_op jit(solution)/shard_map/ppermute | solution.py:430
  40.2 1.8 %collective-permute-start.13 = (bf16[1024,128]{1,0:T(8,128)(2,1)S(1)}, bf16[1024,128]{1,0:T(8,128)(2,1)S(1)}, u32[]{:S(2)}, u32[]{:S(2)}) collective-permute-start(bf16[1024,128]{1,0:T(8,128)(2,1)S(1)} %collective-permute-done.9.refs_3_), channel_id=1, source_target_pairs={{0,16},{16,0},{1,17},{17,1},{2,18},{18,2},{3,19},{19,3},{4,20},{20... | collective-permute-start | bytes 786440 | tf_op jit(solution)/shard_map/ppermute | solution.py:430
  40.2 1.9 %collective-permute-start.12 = (bf16[1024,128]{1,0:T(8,128)(2,1)S(1)}, bf16[1024,128]{1,0:T(8,128)(2,1)S(1)}, u32[]{:S(2)}, u32[]{:S(2)}) collective-permute-start(bf16[1024,128]{1,0:T(8,128)(2,1)S(1)} %collective-permute-done.8.refs_2_), channel_id=1, source_target_pairs={{0,16},{16,0},{1,17},{17,1},{2,18},{18,2},{3,19},{19,3},{4,20},{20... | collective-permute-start | bytes 786440 | tf_op jit(solution)/shard_map/ppermute | solution.py:430
  42.6 10.6 %collective-permute-start.14 = (bf16[2,32,1024]{2,1,0:T(8,128)(2,1)S(1)}, bf16[2,32,1024]{2,1,0:T(8,128)(2,1)S(1)}, u32[]{:S(2)}, u32[]{:S(2)}) collective-permute-start(bf16[2,32,1024]{2,1,0:T(8,128)(2,1)S(1)} %get-tuple-element.112), channel_id=1, source_target_pairs={{0,8},{1,9},{2,10},{3,11},{4,12},{5,13},{6,14},{7,15},{8,0},{9,1},... | collective-permute-start | bytes 393224 | tf_op jit(solution)/shard_map/ppermute | solution.py:521
  43.9 10.4 %collective-permute-start.15 = (bf16[2,32,1024]{2,1,0:T(8,128)(2,1)S(1)}, bf16[2,32,1024]{2,1,0:T(8,128)(2,1)S(1)}, u32[]{:S(2)}, u32[]{:S(2)}) collective-permute-start(bf16[2,32,1024]{2,1,0:T(8,128)(2,1)S(1)} %get-tuple-element.118), channel_id=1, source_target_pairs={{0,4},{1,5},{2,6},{3,7},{4,0},{5,1},{6,2},{7,3},{8,12},{9,13},{10,... | collective-permute-start | bytes 393224 | tf_op jit(solution)/shard_map/ppermute | solution.py:521
  46.5 9.0 %collective-permute-start.16 = (bf16[2,32,1024]{2,1,0:T(8,128)(2,1)S(1)}, bf16[2,32,1024]{2,1,0:T(8,128)(2,1)S(1)}, u32[]{:S(2)}, u32[]{:S(2)}) collective-permute-start(bf16[2,32,1024]{2,1,0:T(8,128)(2,1)S(1)} %get-tuple-element.120), channel_id=1, source_target_pairs={{0,12},{1,13},{2,14},{3,15},{4,8},{5,9},{6,10},{7,11},{8,4},{9,5},... | collective-permute-start | bytes 393224 | tf_op jit(solution)/shard_map/ppermute | solution.py:521

commit v5 on v4

--- a/solution.py
+++ b/solution.py
@@ -9,7 +9,7 @@
 
 FILTER_DEG = 4
 GROUP = 4
-HELD = (0, 1, 3, 2)
+HELD = (0, 3, 2, 1)
 LANES = 128
 EXTRA = 32
 F32 = jnp.float32
@@ -393,7 +393,7 @@
             chunks = []
             for c in range(GROUP):
                 slot = place ^ c
-                slot = jnp.where(slot > 1, 5 - slot, slot)
+                slot = jnp.where(slot % 2 == 1, 4 - slot, slot)
                 at = pl.ds(pl.multiple_of(j * width + slot * LANES, LANES), LANES)
                 chunks.append(sum(part[mat, :, at].astype(F32) for part in parts) * factor)
             columns = [

time: 56.7 us -> 56.1 us (0.989)
  transfers between devices with their start and end apart: 17 -> 17, of which waited for: 10 -> 11; matrix products, arithmetic and copies ran while one was open for 0% -> 0% of each run, Pallas kernels for 8% -> 8%
where the time goes in v5:
time: 56.1 us; the launch traced here: 55.6 us
  starting transfers between devices  20.6 us (37%)
  waiting for transfers between devices  19.4 us (35%)
  Pallas kernels  11.8 us (21%)
  between operations  2.07 us (4%)
  local copies, waits for them, and re-layouts  1.65 us (3%)
    pallas_call x12, Pallas kernels, call(): pl.pallas_call(kernel, out_shape=[jax.ShapeDtypeStruct(shape, dtype) for...  11.8 us
    ppermute x6, starting transfers between devices, in_plane(): return lax.ppermute(block, 'dom', [(i, i ^ k) for i in everyone])  8.1 us
    ppermute x4, starting transfers between devices, with_neighbour(): lax.ppermute(block, 'dom', route)  7.42 us
    ppermute x3, waiting for transfers between devices, shards(): parts[k] = lax.ppermute(parts[k], 'dom', route)  7.12 us
    ppermute x4, waiting for transfers between devices, with_neighbour(): lax.ppermute(block, 'dom', route)  6.18 us
    ppermute x6, waiting for transfers between devices, in_plane(): return lax.ppermute(block, 'dom', [(i, i ^ k) for i in everyone])  5.98 us
    ppermute x3, starting transfers between devices, shards(): parts[k] = lax.ppermute(parts[k], 'dom', route)  4.45 us
    unnamed x11, local copies, waits for them, and re-layouts  1.65 us
  transfers between devices with their start and end apart: 17, of which 11 were waited for; matrix products, arithmetic and copies ran while one was open for 0% of the time, Pallas kernels for 8%

profile of v5, /device:TPU:0, one launch (start us, length us, event | category | flops | bytes accessed | tf_op | source)
XLA Modules:
  0.0 55.6 jit_solution(2669798338536963388)
XLA Ops:
  0.7 1.0 %copy.11.cells_ref = bf16[4,125,125]{2,1,0:T(8,128)(2,1)S(1)} copy(bf16[4,125,125]{2,0,1:T(4,128)(2,1)} %param.9) | data formatting | bytes 250000 | tf_op args[1]
  2.9 3.0 %collective-permute-start = (bf16[544,128]{1,0:T(8,128)(2,1)S(1)}, bf16[544,128]{1,0:T(8,128)(2,1)S(1)}, u32[]{:S(2)}, u32[]{:S(2)}) collective-permute-start(bf16[544,128]{1,0:T(8,128)(2,1)S(1)} %get-tuple-element.64), channel_id=1, source_target_pairs={{0,1},{1,0},{2,3},{3,2},{4,5},{5,4},{6,7},{7,6},{8,9},{9,8},{10,11... | collective-permute-start | bytes 417800 | tf_op jit(solution)/shard_map/ppermute | solution.py:424
  5.9 1.5 %collective-permute-start.1 = (bf16[544,128]{1,0:T(8,128)(2,1)S(1)}, bf16[544,128]{1,0:T(8,128)(2,1)S(1)}, u32[]{:S(2)}, u32[]{:S(2)}) collective-permute-start(bf16[544,128]{1,0:T(8,128)(2,1)S(1)} %get-tuple-element.65), channel_id=1, source_target_pairs={{0,2},{1,3},{2,0},{3,1},{4,6},{5,7},{6,4},{7,5},{8,10},{9,11},{10,... | collective-permute-start | bytes 417800 | tf_op jit(solution)/shard_map/ppermute | solution.py:424
  10.6 3.4 %collective-permute-done.1.ref.refs_2_ = bf16[544,128]{1,0:T(8,128)(2,1)S(1)} collective-permute-done((bf16[544,128]{1,0:T(8,128)(2,1)S(1)}, bf16[544,128]{1,0:T(8,128)(2,1)S(1)}, u32[]{:S(2)}, u32[]{:S(2)}) %collective-permute-start.1) | collective-permute-done | bytes 139296 | tf_op jit(solution)/shard_map/ppermute | solution.py:424
  14.6 0.6 %shard_map.107 = (f32[256,256]{1,0:T(8,128)S(1)}, f32[64,64]{1,0:T(8,128)S(1)}, bf16[256,128]{1,0:T(8,128)(2,1)S(1)}, bf16[128,256]{1,0:T(8,128)(2,1)S(1)}, f32[...) custom-call(f32[1]{0:T(128)S(6)} %copy.12.center_ref, f32[1]{0:T(128)S(6)} %copy.13.half_ref, ...), custom_call_target="tpu_custom_call" | custom-call | flops 268435456 | bytes 2097152 | tf_op jit(solution)/shard_map/pallas_call | solution.py:339
  15.3 2.3 %shard_map.108 = (bf16[4,384,256]{2,1,0:T(8,128)(2,1)S(1)}, bf16[4,256,128]{2,1,0:T(8,128)(2,1)S(1)}, f32[1024,128]{1,0:T(8,128)S(1)}, f32[1024,128]{1,0:T(8,128...) custom-call(s32[1]{0:T(128)} %bitcast.place_ref, ...), custom_call_target="tpu_custom_call" | custom-call | flops 1073741824 | bytes 2097152 | tf_op jit(solution)/shard_map/pallas_call | solution.py:339
  17.6 1.6 %collective-permute-start.3 = (bf16[384,128]{1,0:T(8,128)(2,1)S(1)}, bf16[384,128]{1,0:T(8,128)(2,1)S(1)}, u32[]{:S(2)}, u32[]{:S(2)}) collective-permute-start(bf16[384,128]{1,0:T(8,128)(2,1)S(1)} %get-tuple-element.102), channel_id=1, source_target_pairs={{0,4},{1,5},{2,6},{3,7},{4,0},{5,1},{6,2},{7,3},{8,12},{9,13},{10,... | collective-permute-start | bytes 294920 | tf_op jit(solution)/shard_map/ppermute | solution.py:481
  19.2 2.5 %collective-permute-start.4 = (bf16[384,128]{1,0:T(8,128)(2,1)S(1)}, bf16[384,128]{1,0:T(8,128)(2,1)S(1)}, u32[]{:S(2)}, u32[]{:S(2)}) collective-permute-start(bf16[384,128]{1,0:T(8,128)(2,1)S(1)} %get-tuple-element.103), channel_id=1, source_target_pairs={{0,12},{1,13},{2,14},{3,15},{4,8},{5,9},{6,10},{7,11},{8,4},{9,5},... | collective-permute-start | bytes 294920 | tf_op jit(solution)/shard_map/ppermute | solution.py:481
  21.7 1.6 %collective-permute-done.3.from0_ref = bf16[384,128]{1,0:T(8,128)(2,1)S(1)} collective-permute-done((bf16[384,128]{1,0:T(8,128)(2,1)S(1)}, bf16[384,128]{1,0:T(8,128)(2,1)S(1)}, u32[]{:S(2)}, u32[]{:S(2)}) %collective-permute-start.3) | collective-permute-done | bytes 98336 | tf_op jit(solution)/shard_map/ppermute | solution.py:481
  23.3 2.3 %collective-permute-done.4.from1_ref = bf16[384,128]{1,0:T(8,128)(2,1)S(1)} collective-permute-done((bf16[384,128]{1,0:T(8,128)(2,1)S(1)}, bf16[384,128]{1,0:T(8,128)(2,1)S(1)}, u32[]{:S(2)}, u32[]{:S(2)}) %collective-permute-start.4) | collective-permute-done | bytes 98336 | tf_op jit(solution)/shard_map/ppermute | solution.py:481
  25.6 2.7 %shard_map.109 = (bf16[1024,128]{1,0:T(8,128)(2,1)S(1)}, bf16[64,128]{1,0:T(8,128)(2,1)S(1)}, bf16[64,128]{1,0:T(8,128)(2,1)S(1)}, bf16[64,128]{1,0:T(8,128)(2,1)S(1)}) custom-call(s32[1]{0:T(128)} %bitcast.1.odd_ref, bf16[4,384,256]{2,1,0:T(8,128)(2,1)S(1)} %get-tuple-element.95.whole_ref, bf16[4,256,128]{2,1,0:T(8,128)(2,1)S(1)} %get-tuple-element.96.up_ref, ...), custom_call_target="tpu_custom_call" | custom-call | flops 1073741824 | bytes 2097152 | tf_op jit(solution)/shard_map/pallas_call | solution.py:339
  28.4 1.6 %collective-permute-start.5 = (bf16[1024,128]{1,0:T(8,128)(2,1)S(1)}, bf16[1024,128]{1,0:T(8,128)(2,1)S(1)}, u32[]{:S(2)}, u32[]{:S(2)}) collective-permute-start(bf16[1024,128]{1,0:T(8,128)(2,1)S(1)} %get-tuple-element.113.filtered_ref.refs_0_), channel_id=1, source_target_pairs={{0,3},{1,2},{2,1},{3,0},{4,7},{5,6},{6,5},{7,4},{8,11},{9,10},{10,... | collective-permute-start | bytes 786440 | tf_op jit(solution)/shard_map/ppermute | solution.py:424
  29.9 1.5 %collective-permute-start.9 = (bf16[1024,128]{1,0:T(8,128)(2,1)S(1)}, bf16[1024,128]{1,0:T(8,128)(2,1)S(1)}, u32[]{:S(2)}, u32[]{:S(2)}) collective-permute-start(bf16[1024,128]{1,0:T(8,128)(2,1)S(1)} %get-tuple-element.113.filtered_ref.refs_0_), channel_id=1, source_target_pairs={{0,1},{1,0},{2,3},{3,2},{4,5},{5,4},{6,7},{7,6},{8,9},{9,8},{10,11... | collective-permute-start | bytes 786440 | tf_op jit(solution)/shard_map/ppermute | solution.py:424
  31.9 3.3 %collective-permute-start.7 = (bf16[64,128]{1,0:T(8,128)(2,1)S(1)}, bf16[64,128]{1,0:T(8,128)(2,1)S(1)}, u32[]{:S(2)}, u32[]{:S(2)}) collective-permute-start(bf16[64,128]{1,0:T(8,128)(2,1)S(1)} %get-tuple-element.106), channel_id=1, source_target_pairs={{0,12},{1,13},{2,14},{3,15},{4,8},{5,9},{6,10},{7,11},{8,4},{9,5},... | collective-permute-start | bytes 49160 | tf_op jit(solution)/shard_map/ppermute | solution.py:481
  35.6 1.8 %collective-permute-done.7.from1_ref = bf16[64,128]{1,0:T(8,128)(2,1)S(1)} collective-permute-done((bf16[64,128]{1,0:T(8,128)(2,1)S(1)}, bf16[64,128]{1,0:T(8,128)(2,1)S(1)}, u32[]{:S(2)}, u32[]{:S(2)}) %collective-permute-start.7) | collective-permute-done | bytes 16416 | tf_op jit(solution)/shard_map/ppermute | solution.py:481
  38.0 1.6 %collective-permute-done.9.refs_3_ = bf16[1024,128]{1,0:T(8,128)(2,1)S(1)} collective-permute-done((bf16[1024,128]{1,0:T(8,128)(2,1)S(1)}, bf16[1024,128]{1,0:T(8,128)(2,1)S(1)}, u32[]{:S(2)}, u32[]{:S(2)}) %collective-permute-start.9) | collective-permute-done | bytes 262176 | tf_op jit(solution)/shard_map/ppermute | solution.py:424
  40.1 0.8 %shard_map.110.left_ref = bf16[256,1024]{1,0:T(8,128)(2,1)S(1)} custom-call(s32[1]{0:T(128)} %bitcast.1.odd_ref, f32[1]{0:T(128)S(6)} %copy.12.center_ref, f32[1]{0:T(128)S(6)} %copy.13.half_ref, bf16[4,384,256]{2,1,0:T(8,128)(2,1)S(1)} %get-tuple-element.95.whole_ref, bf16[4,256,128]{2,1,0:T(8,128)(2,1)S(1)} %get-tuple-element.96.up_ref, ...), custom_call_target="tpu_custom_call" | custom-call | flops 268435456 | bytes 2097152 | tf_op jit(solution)/shard_map/pallas_call | solution.py:339
  42.0 1.9 %collective-permute-start.14 = (bf16[2,32,1024]{2,1,0:T(8,128)(2,1)S(1)}, bf16[2,32,1024]{2,1,0:T(8,128)(2,1)S(1)}, u32[]{:S(2)}, u32[]{:S(2)}) collective-permute-start(bf16[2,32,1024]{2,1,0:T(8,128)(2,1)S(1)} %get-tuple-element.112), channel_id=1, source_target_pairs={{0,8},{1,9},{2,10},{3,11},{4,12},{5,13},{6,14},{7,15},{8,0},{9,1},... | collective-permute-start | bytes 393224 | tf_op jit(solution)/shard_map/ppermute | solution.py:521
  43.9 1.5 %collective-permute-start.15 = (bf16[2,32,1024]{2,1,0:T(8,128)(2,1)S(1)}, bf16[2,32,1024]{2,1,0:T(8,128)(2,1)S(1)}, u32[]{:S(2)}, u32[]{:S(2)}) collective-permute-start(bf16[2,32,1024]{2,1,0:T(8,128)(2,1)S(1)} %get-tuple-element.118), channel_id=1, source_target_pairs={{0,4},{1,5},{2,6},{3,7},{4,0},{5,1},{6,2},{7,3},{8,12},{9,13},{10,... | collective-permute-start | bytes 393224 | tf_op jit(solution)/shard_map/ppermute | solution.py:521
  45.3 1.1 %collective-permute-start.16 = (bf16[2,32,1024]{2,1,0:T(8,128)(2,1)S(1)}, bf16[2,32,1024]{2,1,0:T(8,128)(2,1)S(1)}, u32[]{:S(2)}, u32[]{:S(2)}) collective-permute-start(bf16[2,32,1024]{2,1,0:T(8,128)(2,1)S(1)} %get-tuple-element.120), channel_id=1, source_target_pairs={{0,12},{1,13},{2,14},{3,15},{4,8},{5,9},{6,10},{7,11},{8,4},{9,5},... | collective-permute-start | bytes 393224 | tf_op jit(solution)/shard_map/ppermute | solution.py:521
  46.4 6.2 %collective-permute-done.14.refs_2_ = bf16[2,32,1024]{2,1,0:T(8,128)(2,1)S(1)} collective-permute-done((bf16[2,32,1024]{2,1,0:T(8,128)(2,1)S(1)}, bf16[2,32,1024]{2,1,0:T(8,128)(2,1)S(1)}, u32[]{:S(2)}, u32[]{:S(2)}) %collective-permute-start.14) | collective-permute-done | bytes 131104 | tf_op jit(solution)/shard_map/ppermute | solution.py:521
  52.6 1.1 %shard_map.113 = bf16[256,512]{1,0:T(8,128)(2,1)} custom-call(s32[1]{0:T(128)} %bitcast.place_ref, bf16[1024,128]{1,0:T(8,128)(2,1)S(1)} %get-tuple-element.113.filtered_ref.refs_0_, bf16[1024,128]{1,0:T(8,128)(2,1)S(1)} %collective-permute-done.5.refs_1_, bf16[1024,128]{1,0:T(8,128)(2,1)S(1)} %collective-permute-done.8.refs_2_, ...), custom_call_target="tpu_custom_call" | custom-call | bytes 2097152 | tf_op jit(solution)/shard_map/pallas_call | solution.py:339
  53.7 0.9 %collective-permute-done.16.refs_3_ = bf16[2,32,1024]{2,1,0:T(8,128)(2,1)S(1)} collective-permute-done((bf16[2,32,1024]{2,1,0:T(8,128)(2,1)S(1)}, bf16[2,32,1024]{2,1,0:T(8,128)(2,1)S(1)}, u32[]{:S(2)}, u32[]{:S(2)}) %collective-permute-start.16) | collective-permute-done | bytes 131104 | tf_op jit(solution)/shard_map/ppermute | solution.py:521
  54.7 0.9 %shard_map.114 = (f32[32,1024]{1,0:T(8,128)}, f32[32,1024]{1,0:T(8,128)}) custom-call(s32[1]{0:T(128)} %bitcast.place_ref, s32[1]{0:T(128)} %bitcast.6.band_ref, f32[2,32,1024]{2,1,0:T(8,128)S(1)} %get-tuple-element.117.refs_0_, bf16[2,32,1024]{2,1,0:T(8,128)(2,1)S(1)} %collective-permute-done.15.refs_1_, ...), custom_call_target="tpu_custom_call" | custom-call | bytes 2097152 | tf_op jit(solution)/shard_map/pallas_call | solution.py:339
  (34 shorter events, 6.8 us)
Async XLA Ops:
  0.6 1.7 %copy-start = (bf16[256,512]{1,0:T(8,128)(2,1)S(1)}, bf16[256,512]{1,0:T(8,128)(2,1)}, u32[]{:S(2)}) copy-start(bf16[256,512]{1,0:T(8,128)(2,1)} %field_ref.1) | copy-start | bytes 786436
  1.6 0.7 %copy-start.3 = (f32[256]{0:T(256)S(1)}, f32[256]{0:T(256)}, u32[]{:S(2)}) copy-start(f32[256]{0:T(256)} %param.12) | copy-start | bytes 3076
  1.6 0.7 %copy-start.1 = (s32[125,4]{0,1:T(4,128)S(1)}, s32[125,4]{0,1:T(4,128)}, u32[]{:S(2)}) copy-start(s32[125,4]{0,1:T(4,128)} %param.10) | copy-start | bytes 6004
  1.7 0.7 %copy-start.2 = (f32[256]{0:T(256)S(1)}, f32[256]{0:T(256)}, u32[]{:S(2)}) copy-start(f32[256]{0:T(256)} %param.13) | copy-start | bytes 3076
  1.7 0.7 %copy-start.4 = (s32[1,64]{1,0:T(1,128)S(1)}, s32[1,64]{1,0:T(1,128)}, u32[]{:S(2)}) copy-start(s32[1,64]{1,0:T(1,128)} %param.11) | copy-start | bytes 772
  2.9 7.1 %collective-permute-start = (bf16[544,128]{1,0:T(8,128)(2,1)S(1)}, bf16[544,128]{1,0:T(8,128)(2,1)S(1)}, u32[]{:S(2)}, u32[]{:S(2)}) collective-permute-start(bf16[544,128]{1,0:T(8,128)(2,1)S(1)} %get-tuple-element.64), channel_id=1, source_target_pairs={{0,1},{1,0},{2,3},{3,2},{4,5},{5,4},{6,7},{7,6},{8,9},{9,8},{10,11... | collective-permute-start | bytes 417800 | tf_op jit(solution)/shard_map/ppermute | solution.py:424
  5.9 8.1 %collective-permute-start.1 = (bf16[544,128]{1,0:T(8,128)(2,1)S(1)}, bf16[544,128]{1,0:T(8,128)(2,1)S(1)}, u32[]{:S(2)}, u32[]{:S(2)}) collective-permute-start(bf16[544,128]{1,0:T(8,128)(2,1)S(1)} %get-tuple-element.65), channel_id=1, source_target_pairs={{0,2},{1,3},{2,0},{3,1},{4,6},{5,7},{6,4},{7,5},{8,10},{9,11},{10,... | collective-permute-start | bytes 417800 | tf_op jit(solution)/shard_map/ppermute | solution.py:424
  7.4 7.2 %collective-permute-start.2 = (bf16[544,128]{1,0:T(8,128)(2,1)S(1)}, bf16[544,128]{1,0:T(8,128)(2,1)S(1)}, u32[]{:S(2)}, u32[]{:S(2)}) collective-permute-start(bf16[544,128]{1,0:T(8,128)(2,1)S(1)} %get-tuple-element.66), channel_id=1, source_target_pairs={{0,3},{1,2},{2,1},{3,0},{4,7},{5,6},{6,5},{7,4},{8,11},{9,10},{10,... | collective-permute-start | bytes 417800 | tf_op jit(solution)/shard_map/ppermute | solution.py:424
  17.6 5.7 %collective-permute-start.3 = (bf16[384,128]{1,0:T(8,128)(2,1)S(1)}, bf16[384,128]{1,0:T(8,128)(2,1)S(1)}, u32[]{:S(2)}, u32[]{:S(2)}) collective-permute-start(bf16[384,128]{1,0:T(8,128)(2,1)S(1)} %get-tuple-element.102), channel_id=1, source_target_pairs={{0,4},{1,5},{2,6},{3,7},{4,0},{5,1},{6,2},{7,3},{8,12},{9,13},{10,... | collective-permute-start | bytes 294920 | tf_op jit(solution)/shard_map/ppermute | solution.py:481
  19.2 6.4 %collective-permute-start.4 = (bf16[384,128]{1,0:T(8,128)(2,1)S(1)}, bf16[384,128]{1,0:T(8,128)(2,1)S(1)}, u32[]{:S(2)}, u32[]{:S(2)}) collective-permute-start(bf16[384,128]{1,0:T(8,128)(2,1)S(1)} %get-tuple-element.103), channel_id=1, source_target_pairs={{0,12},{1,13},{2,14},{3,15},{4,8},{5,9},{6,10},{7,11},{8,4},{9,5},... | collective-permute-start | bytes 294920 | tf_op jit(solution)/shard_map/ppermute | solution.py:481
  28.4 9.1 %collective-permute-start.5 = (bf16[1024,128]{1,0:T(8,128)(2,1)S(1)}, bf16[1024,128]{1,0:T(8,128)(2,1)S(1)}, u32[]{:S(2)}, u32[]{:S(2)}) collective-permute-start(bf16[1024,128]{1,0:T(8,128)(2,1)S(1)} %get-tuple-element.113.filtered_ref.refs_0_), channel_id=1, source_target_pairs={{0,3},{1,2},{2,1},{3,0},{4,7},{5,6},{6,5},{7,4},{8,11},{9,10},{10,... | collective-permute-start | bytes 786440 | tf_op jit(solution)/shard_map/ppermute | solution.py:424
  29.9 9.7 %collective-permute-start.9 = (bf16[1024,128]{1,0:T(8,128)(2,1)S(1)}, bf16[1024,128]{1,0:T(8,128)(2,1)S(1)}, u32[]{:S(2)}, u32[]{:S(2)}) collective-permute-start(bf16[1024,128]{1,0:T(8,128)(2,1)S(1)} %get-tuple-element.113.filtered_ref.refs_0_), channel_id=1, source_target_pairs={{0,1},{1,0},{2,3},{3,2},{4,5},{5,4},{6,7},{7,6},{8,9},{9,8},{10,11... | collective-permute-start | bytes 786440 | tf_op jit(solution)/shard_map/ppermute | solution.py:424
  31.4 8.5 %collective-permute-start.8 = (bf16[1024,128]{1,0:T(8,128)(2,1)S(1)}, bf16[1024,128]{1,0:T(8,128)(2,1)S(1)}, u32[]{:S(2)}, u32[]{:S(2)}) collective-permute-start(bf16[1024,128]{1,0:T(8,128)(2,1)S(1)} %get-tuple-element.113.filtered_ref.refs_0_), channel_id=1, source_target_pairs={{0,2},{1,3},{2,0},{3,1},{4,6},{5,7},{6,4},{7,5},{8,10},{9,11},{10,... | collective-permute-start | bytes 786440 | tf_op jit(solution)/shard_map/ppermute | solution.py:424
  31.9 3.7 %collective-permute-start.6 = (bf16[64,128]{1,0:T(8,128)(2,1)S(1)}, bf16[64,128]{1,0:T(8,128)(2,1)S(1)}, u32[]{:S(2)}, u32[]{:S(2)}) collective-permute-start(bf16[64,128]{1,0:T(8,128)(2,1)S(1)} %get-tuple-element.105), channel_id=1, source_target_pairs={{0,4},{1,5},{2,6},{3,7},{4,0},{5,1},{6,2},{7,3},{8,12},{9,13},{10,... | collective-permute-start | bytes 49160 | tf_op jit(solution)/shard_map/ppermute | solution.py:481
  31.9 5.5 %collective-permute-start.7 = (bf16[64,128]{1,0:T(8,128)(2,1)S(1)}, bf16[64,128]{1,0:T(8,128)(2,1)S(1)}, u32[]{:S(2)}, u32[]{:S(2)}) collective-permute-start(bf16[64,128]{1,0:T(8,128)(2,1)S(1)} %get-tuple-element.106), channel_id=1, source_target_pairs={{0,12},{1,13},{2,14},{3,15},{4,8},{5,9},{6,10},{7,11},{8,4},{9,5},... | collective-permute-start | bytes 49160 | tf_op jit(solution)/shard_map/ppermute | solution.py:481
  37.5 2.6 %collective-permute-start.10 = (bf16[1024,128]{1,0:T(8,128)(2,1)S(1)}, bf16[1024,128]{1,0:T(8,128)(2,1)S(1)}, u32[]{:S(2)}, u32[]{:S(2)}) collective-permute-start(bf16[1024,128]{1,0:T(8,128)(2,1)S(1)} %get-tuple-element.113.filtered_ref.refs_0_), channel_id=1, source_target_pairs={{0,16},{16,0},{1,17},{17,1},{2,18},{18,2},{3,19},{19,3},{4,20},{20... | collective-permute-start | bytes 786440 | tf_op jit(solution)/shard_map/ppermute | solution.py:430
  37.5 2.6 %collective-permute-start.11 = (bf16[1024,128]{1,0:T(8,128)(2,1)S(1)}, bf16[1024,128]{1,0:T(8,128)(2,1)S(1)}, u32[]{:S(2)}, u32[]{:S(2)}) collective-permute-start(bf16[1024,128]{1,0:T(8,128)(2,1)S(1)} %collective-permute-done.5.refs_1_), channel_id=1, source_target_pairs={{0,16},{16,0},{1,17},{17,1},{2,18},{18,2},{3,19},{19,3},{4,20},{20... | collective-permute-start | bytes 786440 | tf_op jit(solution)/shard_map/ppermute | solution.py:430
  39.6 1.8 %collective-permute-start.13 = (bf16[1024,128]{1,0:T(8,128)(2,1)S(1)}, bf16[1024,128]{1,0:T(8,128)(2,1)S(1)}, u32[]{:S(2)}, u32[]{:S(2)}) collective-permute-start(bf16[1024,128]{1,0:T(8,128)(2,1)S(1)} %collective-permute-done.9.refs_3_), channel_id=1, source_target_pairs={{0,16},{16,0},{1,17},{17,1},{2,18},{18,2},{3,19},{19,3},{4,20},{20... | collective-permute-start | bytes 786440 | tf_op jit(solution)/shard_map/ppermute | solution.py:430
  40.0 1.5 %collective-permute-start.12 = (bf16[1024,128]{1,0:T(8,128)(2,1)S(1)}, bf16[1024,128]{1,0:T(8,128)(2,1)S(1)}, u32[]{:S(2)}, u32[]{:S(2)}) collective-permute-start(bf16[1024,128]{1,0:T(8,128)(2,1)S(1)} %collective-permute-done.8.refs_2_), channel_id=1, source_target_pairs={{0,16},{16,0},{1,17},{17,1},{2,18},{18,2},{3,19},{19,3},{4,20},{20... | collective-permute-start | bytes 786440 | tf_op jit(solution)/shard_map/ppermute | solution.py:430
  42.0 10.7 %collective-permute-start.14 = (bf16[2,32,1024]{2,1,0:T(8,128)(2,1)S(1)}, bf16[2,32,1024]{2,1,0:T(8,128)(2,1)S(1)}, u32[]{:S(2)}, u32[]{:S(2)}) collective-permute-start(bf16[2,32,1024]{2,1,0:T(8,128)(2,1)S(1)} %get-tuple-element.112), channel_id=1, source_target_pairs={{0,8},{1,9},{2,10},{3,11},{4,12},{5,13},{6,14},{7,15},{8,0},{9,1},... | collective-permute-start | bytes 393224 | tf_op jit(solution)/shard_map/ppermute | solution.py:521
  43.9 9.9 %collective-permute-start.15 = (bf16[2,32,1024]{2,1,0:T(8,128)(2,1)S(1)}, bf16[2,32,1024]{2,1,0:T(8,128)(2,1)S(1)}, u32[]{:S(2)}, u32[]{:S(2)}) collective-permute-start(bf16[2,32,1024]{2,1,0:T(8,128)(2,1)S(1)} %get-tuple-element.118), channel_id=1, source_target_pairs={{0,4},{1,5},{2,6},{3,7},{4,0},{5,1},{6,2},{7,3},{8,12},{9,13},{10,... | collective-permute-start | bytes 393224 | tf_op jit(solution)/shard_map/ppermute | solution.py:521
  45.3 9.4 %collective-permute-start.16 = (bf16[2,32,1024]{2,1,0:T(8,128)(2,1)S(1)}, bf16[2,32,1024]{2,1,0:T(8,128)(2,1)S(1)}, u32[]{:S(2)}, u32[]{:S(2)}) collective-permute-start(bf16[2,32,1024]{2,1,0:T(8,128)(2,1)S(1)} %get-tuple-element.120), channel_id=1, source_target_pairs={{0,12},{1,13},{2,14},{3,15},{4,8},{5,9},{6,10},{7,11},{8,4},{9,5},... | collective-permute-start | bytes 393224 | tf_op jit(solution)/shard_map/ppermute | solution.py:521

commit v6 on v5

--- a/solution.py
+++ b/solution.py
@@ -94,7 +94,8 @@
 
 
 def build_kernel(
-    nodes, cells, corners, shared, center_ref, half_ref, ref, _, own_ref, corner_ref, up_ref, down_ref, mass_ref, scale_ref, diag_ref,
+    nodes, cells, corners, shared, center_ref, half_ref, ref, _, own_ref, corner_ref, up_ref, down_ref, mass_ref, recip_ref,
+    scale_ref, diag_ref,
 ):
     center, half = center_ref[0], half_ref[0]
     both = nodes + shared
@@ -138,28 +139,30 @@
         off = cells + halves + h
         pot = jnp.broadcast_to(columns[:, off : off + 1], (LANES, LANES))
         mass_ref[at, :] = mass
-        scale_ref[at, :] = mass / half
+        recip_ref[at, :] = 1.0 / mass
+        scale_ref[at, :] = mass * mass / half
         diag_ref[at, :] = (pot - center) / half
 
 
 def first_kernel(shared, place_ref, odd_ref, *refs):
     messages, refs = refs[:GROUP], refs[GROUP:]
-    slabs = [refs[7 * k : 7 * k + 7] for k in range(GROUP)]
-    whole_ref, up_ref, mass_ref, scale_ref, diag_ref, start_ref = refs[7 * GROUP : 7 * GROUP + 6]
-    keep_ref, pair0_ref, pair1_ref, raw, corner, cur, prev, box = refs[7 * GROUP + 6 :]
+    slabs = [refs[8 * k : 8 * k + 8] for k in range(GROUP)]
+    whole_ref, up_ref, mass_ref, recip_ref, scale_ref, diag_ref, start_ref = refs[8 * GROUP : 8 * GROUP + 7]
+    keep_ref, pair0_ref, pair1_ref, raw, corner, cur, prev, box = refs[8 * GROUP + 7 :]
     next_ref, previous_ref = box.at[0], box.at[1]
     place = place_ref[0]
     nodes = whole_ref.shape[2]
     for k in range(GROUP):
         slab = place ^ k
         at = pl.ds(pl.multiple_of(slab * nodes, nodes), nodes)
-        own_k, corner_k, up_k, down_k, mass_k, scale_k, diag_k = slabs[k]
+        own_k, corner_k, up_k, down_k, mass_k, recip_k, scale_k, diag_k = slabs[k]
         start_ref[at, :] = messages[k][0:nodes, :]
         raw[slab] = own_k[...]
         corner[slab] = corner_k[...]
         up_ref[slab] = up_k[...]
         whole_ref[slab, nodes:, :] = down_k[...]
         mass_ref[at, :] = mass_k[...]
+        recip_ref[at, :] = recip_k[...]
         scale_ref[at, :] = scale_k[...]
         diag_ref[at, :] = diag_k[...]
     whole_ref[0, 0:nodes, :] = raw[0].astype(BF16)
@@ -168,7 +171,7 @@
         moved = jnp.concatenate([jnp.zeros_like(moved), moved], axis=0).astype(BF16)
         whole_ref[i, 0:nodes, :] = (raw[i] + dot(up_ref[i], moved)).astype(BF16)
 
-    cur[:, 0:LANES] = start_ref[...].astype(F32)
+    cur[:, 0:LANES] = mass_ref[...] * start_ref[...].astype(F32)
     cur[:, LANES:] = jnp.zeros((GROUP * nodes, 2 * shared), F32)
     top = (GROUP - 1) * nodes
     first = up_ref[0].astype(F32)
@@ -178,7 +181,6 @@
     cur[0:nodes, LANES:] = jnp.where(lane < shared, swapped * scale_ref[0:nodes, :], 0.0)
     swapped = jnp.concatenate([last[:, shared:], last[:, :shared]], axis=1)
     cur[top:, LANES:] = cur[top:, LANES:] + jnp.where(lane >= shared, swapped * scale_ref[top:, :], 0.0)
-    prev[...] = jnp.zeros_like(prev)
 
     whole = [whole_ref[i] for i in range(GROUP)]
     up = [up_ref[i] for i in range(GROUP)]
@@ -191,12 +193,12 @@
     for k in range(FILTER_DEG):
         last_step = k == FILTER_DEG - 1
         if last_step:
-            field0 = (mass_ref[0:nodes, :] * cur[0:nodes, 0:LANES]).astype(BF16)
-            field3 = (mass_ref[top:, :] * cur[top:, 0:LANES]).astype(BF16)
+            field0 = cur[0:nodes, 0:LANES].astype(BF16)
+            field3 = cur[top:, 0:LANES].astype(BF16)
             next_ref[k * shared : (k + 1) * shared, :] = dot(whole_ref[GROUP - 1, nodes:, :], field3)[:shared].astype(BF16)
             previous_ref[k * shared : (k + 1) * shared, :] = dot(whole_ref[0, nodes:, :], field0)[shared:].astype(BF16)
             break
-        fields = [(wide(mass_ref, i) * cur[i * nodes : (i + 1) * nodes, :]).astype(BF16) for i in range(GROUP)]
+        fields = [cur[i * nodes : (i + 1) * nodes, :].astype(BF16) for i in range(GROUP)]
         keep = range(GROUP) if k < FILTER_DEG - 2 else (0, GROUP - 1)
         sums, to_next, to_previous = apply_plane(whole, up, fields, None, keep)
         next_ref[k * shared : (k + 1) * shared, :] = to_next[:, 0:LANES].astype(BF16)
@@ -233,7 +235,7 @@
 
 
 def second_kernel(
-    shared, odd_ref, whole_ref, up_ref, mass_ref, scale_ref, diag_ref, start_ref, keep_ref, from0_ref, from1_ref,
+    shared, odd_ref, whole_ref, up_ref, mass_ref, recip_ref, scale_ref, diag_ref, start_ref, keep_ref, from0_ref, from1_ref,
     filtered_ref, corner_ref, pair0_ref, pair1_ref, cur, prev, box,
 ):
     odd = odd_ref[0]
@@ -278,15 +280,15 @@
         fields, values = [], []
         for i in range(GROUP):
             rows = slice(i * nodes, (i + 1) * nodes)
-            values.append(start_ref[rows, :].astype(F32) if k == 0 else cur[rows, :])
-            fields.append((mass_ref[rows, :] * values[i]).astype(BF16))
+            values.append(mass_ref[rows, :] * start_ref[rows, :].astype(F32) if k == 0 else cur[rows, :])
+            fields.append(values[i].astype(BF16))
         sums, _, _ = apply_plane(whole, up, fields, outside)
         for i in range(GROUP):
             rows = slice(i * nodes, (i + 1) * nodes)
             image = scale_ref[rows, :] * sums[i] + diag_ref[rows, :] * values[i]
             new = image if k == 0 else 2.0 * image - prev[rows, :]
             if k == FILTER_DEG - 1:
-                filtered_ref[rows, :] = new.astype(BF16)
+                filtered_ref[rows, :] = (recip_ref[rows, :] * new).astype(BF16)
             else:
                 prev[rows, :] = values[i]
                 cur[rows, :] = new
@@ -449,8 +451,8 @@
             functools.partial(build_kernel, nodes, cells, corners, shared),
             [
                 ((nodes, nodes), F32), ((shared, shared), F32), ((nodes, 2 * shared), BF16), ((2 * shared, nodes), BF16),
-            ] + [((nodes, LANES), F32)] * 3,
-            (filter_center, filter_halfwidth, message, slabs[-6] if slabs else message),
+            ] + [((nodes, LANES), F32)] * 4,
+            (filter_center, filter_halfwidth, message, slabs[-7] if slabs else message),
             spaces="ssva",
             flops=1 << 28,
         )
@@ -458,14 +460,14 @@
     column = ((height, LANES), F32)
     trace = ((FILTER_DEG * shared + 2 * shared, LANES), BF16)
     odd_arg = (plane % 2).astype(jnp.int32).reshape(1)
-    whole, up, mass, scale, diag, start, keep, *pairs = call(
+    whole, up, mass, recip, scale, diag, start, keep, *pairs = call(
         functools.partial(first_kernel, shared),
         [
             ((GROUP, nodes + 2 * shared, nodes), BF16), ((GROUP, nodes, 2 * shared), BF16),
-            column, column, column, ((height, LANES), BF16), ((shared, LANES), BF16), trace, trace,
+            column, column, column, column, ((height, LANES), BF16), ((shared, LANES), BF16), trace, trace,
         ],
         (place_arg, odd_arg, *messages, *slabs),
-        spaces="ss" + "v" * (GROUP * 8),
+        spaces="ss" + "v" * (GROUP * 9),
         scratch=[
             pltpu.VMEM((GROUP, nodes, nodes), F32), pltpu.VMEM((GROUP, shared, shared), F32),
             pltpu.VMEM((height, 2 * LANES), F32), pltpu.VMEM((height, 2 * LANES), F32),
@@ -484,8 +486,8 @@
     mine, corner, *pairs = call(
         functools.partial(second_kernel, shared),
         [((height, LANES), BF16)] + [((shared, LANES), BF16)] * 3,
-        (odd_arg, whole, up, mass, scale, diag, start, keep, *heard),
-        spaces="s" + "v" * 9,
+        (odd_arg, whole, up, mass, recip, scale, diag, start, keep, *heard),
+        spaces="s" + "v" * 10,
         scratch=[pltpu.VMEM((height, LANES), F32), pltpu.VMEM((height, LANES), F32), pltpu.VMEM((2, *trace[0]), BF16)],
         flops=1 << 30,
     )

time: 56.1 us -> 56 us (level)
  no operation moved by 1% of the time
where the time goes in v6:
time: 56 us; the launch traced here: 55.5 us
  starting transfers between devices  20.6 us (37%)
  waiting for transfers between devices  19.4 us (35%)
  Pallas kernels  11.7 us (21%)
  between operations  2.07 us (4%)
  local copies, waits for them, and re-layouts  1.65 us (3%)
    pallas_call x12, Pallas kernels, call(): pl.pallas_call(kernel, out_shape=[jax.ShapeDtypeStruct(shape, dtype) for...  11.7 us
    ppermute x6, starting transfers between devices, in_plane(): return lax.ppermute(block, 'dom', [(i, i ^ k) for i in everyone])  8.1 us
    ppermute x4, starting transfers between devices, with_neighbour(): lax.ppermute(block, 'dom', route)  7.43 us
    ppermute x3, waiting for transfers between devices, shards(): parts[k] = lax.ppermute(parts[k], 'dom', route)  7.11 us
    ppermute x4, waiting for transfers between devices, with_neighbour(): lax.ppermute(block, 'dom', route)  6.17 us
    ppermute x6, waiting for transfers between devices, in_plane(): return lax.ppermute(block, 'dom', [(i, i ^ k) for i in everyone])  5.98 us
    ppermute x3, starting transfers between devices, shards(): parts[k] = lax.ppermute(parts[k], 'dom', route)  4.45 us
    unnamed x11, local copies, waits for them, and re-layouts  1.65 us
  transfers between devices with their start and end apart: 17, of which 11 were waited for; matrix products, arithmetic and copies ran while one was open for 0% of the time, Pallas kernels for 8%

profile of v6, /device:TPU:0, one launch (start us, length us, event | category | flops | bytes accessed | tf_op | source)
XLA Modules:
  0.0 55.5 jit_solution(11327502202646989642)
XLA Ops:
  0.7 1.0 %copy.11.cells_ref = bf16[4,125,125]{2,1,0:T(8,128)(2,1)S(1)} copy(bf16[4,125,125]{2,0,1:T(4,128)(2,1)} %param.9) | data formatting | bytes 250000 | tf_op args[1]
  2.9 3.0 %collective-permute-start = (bf16[544,128]{1,0:T(8,128)(2,1)S(1)}, bf16[544,128]{1,0:T(8,128)(2,1)S(1)}, u32[]{:S(2)}, u32[]{:S(2)}) collective-permute-start(bf16[544,128]{1,0:T(8,128)(2,1)S(1)} %get-tuple-element.69), channel_id=1, source_target_pairs={{0,1},{1,0},{2,3},{3,2},{4,5},{5,4},{6,7},{7,6},{8,9},{9,8},{10,11... | collective-permute-start | bytes 417800 | tf_op jit(solution)/shard_map/ppermute | solution.py:426
  5.9 1.5 %collective-permute-start.1 = (bf16[544,128]{1,0:T(8,128)(2,1)S(1)}, bf16[544,128]{1,0:T(8,128)(2,1)S(1)}, u32[]{:S(2)}, u32[]{:S(2)}) collective-permute-start(bf16[544,128]{1,0:T(8,128)(2,1)S(1)} %get-tuple-element.70), channel_id=1, source_target_pairs={{0,2},{1,3},{2,0},{3,1},{4,6},{5,7},{6,4},{7,5},{8,10},{9,11},{10,... | collective-permute-start | bytes 417800 | tf_op jit(solution)/shard_map/ppermute | solution.py:426
  10.6 3.4 %collective-permute-done.1.ref.refs_2_ = bf16[544,128]{1,0:T(8,128)(2,1)S(1)} collective-permute-done((bf16[544,128]{1,0:T(8,128)(2,1)S(1)}, bf16[544,128]{1,0:T(8,128)(2,1)S(1)}, u32[]{:S(2)}, u32[]{:S(2)}) %collective-permute-start.1) | collective-permute-done | bytes 139296 | tf_op jit(solution)/shard_map/ppermute | solution.py:426
  14.6 0.6 %shard_map.107 = (f32[256,256]{1,0:T(8,128)S(1)}, f32[64,64]{1,0:T(8,128)S(1)}, bf16[256,128]{1,0:T(8,128)(2,1)S(1)}, bf16[128,256]{1,0:T(8,128)(2,1)S(1)}, f32[...) custom-call(f32[1]{0:T(128)S(6)} %copy.12.center_ref, ...), custom_call_target="tpu_custom_call" | custom-call | flops 268435456 | bytes 2097152 | tf_op jit(solution)/shard_map/pallas_call | solution.py:341
  15.3 2.2 %shard_map.108 = (bf16[4,384,256]{2,1,0:T(8,128)(2,1)S(1)}, bf16[4,256,128]{2,1,0:T(8,128)(2,1)S(1)}, f32[1024,128]{1,0:T(8,128)S(1)}, f32[1024,128]{1,0:T(8,128...) custom-call(s32[1]{0:T(128)} %bitcast.place_ref, ...), custom_call_target="tpu_custom_call" | custom-call | flops 1073741824 | bytes 2097152 | tf_op jit(solution)/shard_map/pallas_call | solution.py:341
  17.5 1.6 %collective-permute-start.3 = (bf16[384,128]{1,0:T(8,128)(2,1)S(1)}, bf16[384,128]{1,0:T(8,128)(2,1)S(1)}, u32[]{:S(2)}, u32[]{:S(2)}) collective-permute-start(bf16[384,128]{1,0:T(8,128)(2,1)S(1)} %get-tuple-element.112), channel_id=1, source_target_pairs={{0,4},{1,5},{2,6},{3,7},{4,0},{5,1},{6,2},{7,3},{8,12},{9,13},{10,... | collective-permute-start | bytes 294920 | tf_op jit(solution)/shard_map/ppermute | solution.py:483
  19.1 2.5 %collective-permute-start.4 = (bf16[384,128]{1,0:T(8,128)(2,1)S(1)}, bf16[384,128]{1,0:T(8,128)(2,1)S(1)}, u32[]{:S(2)}, u32[]{:S(2)}) collective-permute-start(bf16[384,128]{1,0:T(8,128)(2,1)S(1)} %get-tuple-element.113), channel_id=1, source_target_pairs={{0,12},{1,13},{2,14},{3,15},{4,8},{5,9},{6,10},{7,11},{8,4},{9,5},... | collective-permute-start | bytes 294920 | tf_op jit(solution)/shard_map/ppermute | solution.py:483
  21.6 1.6 %collective-permute-done.3.from0_ref = bf16[384,128]{1,0:T(8,128)(2,1)S(1)} collective-permute-done((bf16[384,128]{1,0:T(8,128)(2,1)S(1)}, bf16[384,128]{1,0:T(8,128)(2,1)S(1)}, u32[]{:S(2)}, u32[]{:S(2)}) %collective-permute-start.3) | collective-permute-done | bytes 98336 | tf_op jit(solution)/shard_map/ppermute | solution.py:483
  23.2 2.3 %collective-permute-done.4.from1_ref = bf16[384,128]{1,0:T(8,128)(2,1)S(1)} collective-permute-done((bf16[384,128]{1,0:T(8,128)(2,1)S(1)}, bf16[384,128]{1,0:T(8,128)(2,1)S(1)}, u32[]{:S(2)}, u32[]{:S(2)}) %collective-permute-start.4) | collective-permute-done | bytes 98336 | tf_op jit(solution)/shard_map/ppermute | solution.py:483
  25.6 2.6 %shard_map.109 = (bf16[1024,128]{1,0:T(8,128)(2,1)S(1)}, bf16[64,128]{1,0:T(8,128)(2,1)S(1)}, bf16[64,128]{1,0:T(8,128)(2,1)S(1)}, bf16[64,128]{1,0:T(8,128)(2,1)S(1)}) custom-call(s32[1]{0:T(128)} %bitcast.1.odd_ref, bf16[4,384,256]{2,1,0:T(8,128)(2,1)S(1)} %get-tuple-element.104.whole_ref, bf16[4,256,128]{2,1,0:T(8,128)(2,1)S(1)} %get-tuple-element.105.up_ref, ...), custom_call_target="tpu_custom_call" | custom-call | flops 1073741824 | bytes 2097152 | tf_op jit(solution)/shard_map/pallas_call | solution.py:341
  28.2 1.6 %collective-permute-start.5 = (bf16[1024,128]{1,0:T(8,128)(2,1)S(1)}, bf16[1024,128]{1,0:T(8,128)(2,1)S(1)}, u32[]{:S(2)}, u32[]{:S(2)}) collective-permute-start(bf16[1024,128]{1,0:T(8,128)(2,1)S(1)} %get-tuple-element.123.filtered_ref.refs_0_), channel_id=1, source_target_pairs={{0,3},{1,2},{2,1},{3,0},{4,7},{5,6},{6,5},{7,4},{8,11},{9,10},{10,... | collective-permute-start | bytes 786440 | tf_op jit(solution)/shard_map/ppermute | solution.py:426
  29.8 1.5 %collective-permute-start.9 = (bf16[1024,128]{1,0:T(8,128)(2,1)S(1)}, bf16[1024,128]{1,0:T(8,128)(2,1)S(1)}, u32[]{:S(2)}, u32[]{:S(2)}) collective-permute-start(bf16[1024,128]{1,0:T(8,128)(2,1)S(1)} %get-tuple-element.123.filtered_ref.refs_0_), channel_id=1, source_target_pairs={{0,1},{1,0},{2,3},{3,2},{4,5},{5,4},{6,7},{7,6},{8,9},{9,8},{10,11... | collective-permute-start | bytes 786440 | tf_op jit(solution)/shard_map/ppermute | solution.py:426
  31.8 3.3 %collective-permute-start.7 = (bf16[64,128]{1,0:T(8,128)(2,1)S(1)}, bf16[64,128]{1,0:T(8,128)(2,1)S(1)}, u32[]{:S(2)}, u32[]{:S(2)}) collective-permute-start(bf16[64,128]{1,0:T(8,128)(2,1)S(1)} %get-tuple-element.116), channel_id=1, source_target_pairs={{0,12},{1,13},{2,14},{3,15},{4,8},{5,9},{6,10},{7,11},{8,4},{9,5},... | collective-permute-start | bytes 49160 | tf_op jit(solution)/shard_map/ppermute | solution.py:483
  35.5 1.8 %collective-permute-done.7.from1_ref = bf16[64,128]{1,0:T(8,128)(2,1)S(1)} collective-permute-done((bf16[64,128]{1,0:T(8,128)(2,1)S(1)}, bf16[64,128]{1,0:T(8,128)(2,1)S(1)}, u32[]{:S(2)}, u32[]{:S(2)}) %collective-permute-start.7) | collective-permute-done | bytes 16416 | tf_op jit(solution)/shard_map/ppermute | solution.py:483
  37.8 1.6 %collective-permute-done.9.refs_3_ = bf16[1024,128]{1,0:T(8,128)(2,1)S(1)} collective-permute-done((bf16[1024,128]{1,0:T(8,128)(2,1)S(1)}, bf16[1024,128]{1,0:T(8,128)(2,1)S(1)}, u32[]{:S(2)}, u32[]{:S(2)}) %collective-permute-start.9) | collective-permute-done | bytes 262176 | tf_op jit(solution)/shard_map/ppermute | solution.py:426
  40.0 0.8 %shard_map.110.left_ref = bf16[256,1024]{1,0:T(8,128)(2,1)S(1)} custom-call(s32[1]{0:T(128)} %bitcast.1.odd_ref, f32[1]{0:T(128)S(6)} %copy.12.center_ref, f32[1]{0:T(128)S(6)} %copy.13.half_ref, bf16[4,384,256]{2,1,0:T(8,128)(2,1)S(1)} %get-tuple-element.104.whole_ref, bf16[4,256,128]{2,1,0:T(8,128)(2,1)S(1)} %get-tuple-element.105.up_ref, ...), custom_call_target="tpu_custom_call" | custom-call | flops 268435456 | bytes 2097152 | tf_op jit(solution)/shard_map/pallas_call | solution.py:341
  41.8 1.9 %collective-permute-start.14 = (bf16[2,32,1024]{2,1,0:T(8,128)(2,1)S(1)}, bf16[2,32,1024]{2,1,0:T(8,128)(2,1)S(1)}, u32[]{:S(2)}, u32[]{:S(2)}) collective-permute-start(bf16[2,32,1024]{2,1,0:T(8,128)(2,1)S(1)} %get-tuple-element.122), channel_id=1, source_target_pairs={{0,8},{1,9},{2,10},{3,11},{4,12},{5,13},{6,14},{7,15},{8,0},{9,1},... | collective-permute-start | bytes 393224 | tf_op jit(solution)/shard_map/ppermute | solution.py:523
  43.7 1.5 %collective-permute-start.15 = (bf16[2,32,1024]{2,1,0:T(8,128)(2,1)S(1)}, bf16[2,32,1024]{2,1,0:T(8,128)(2,1)S(1)}, u32[]{:S(2)}, u32[]{:S(2)}) collective-permute-start(bf16[2,32,1024]{2,1,0:T(8,128)(2,1)S(1)} %get-tuple-element.128), channel_id=1, source_target_pairs={{0,4},{1,5},{2,6},{3,7},{4,0},{5,1},{6,2},{7,3},{8,12},{9,13},{10,... | collective-permute-start | bytes 393224 | tf_op jit(solution)/shard_map/ppermute | solution.py:523
  45.2 1.1 %collective-permute-start.16 = (bf16[2,32,1024]{2,1,0:T(8,128)(2,1)S(1)}, bf16[2,32,1024]{2,1,0:T(8,128)(2,1)S(1)}, u32[]{:S(2)}, u32[]{:S(2)}) collective-permute-start(bf16[2,32,1024]{2,1,0:T(8,128)(2,1)S(1)} %get-tuple-element.130), channel_id=1, source_target_pairs={{0,12},{1,13},{2,14},{3,15},{4,8},{5,9},{6,10},{7,11},{8,4},{9,5},... | collective-permute-start | bytes 393224 | tf_op jit(solution)/shard_map/ppermute | solution.py:523
  46.3 6.2 %collective-permute-done.14.refs_2_ = bf16[2,32,1024]{2,1,0:T(8,128)(2,1)S(1)} collective-permute-done((bf16[2,32,1024]{2,1,0:T(8,128)(2,1)S(1)}, bf16[2,32,1024]{2,1,0:T(8,128)(2,1)S(1)}, u32[]{:S(2)}, u32[]{:S(2)}) %collective-permute-start.14) | collective-permute-done | bytes 131104 | tf_op jit(solution)/shard_map/ppermute | solution.py:523
  52.5 1.1 %shard_map.113 = bf16[256,512]{1,0:T(8,128)(2,1)} custom-call(s32[1]{0:T(128)} %bitcast.place_ref, bf16[1024,128]{1,0:T(8,128)(2,1)S(1)} %get-tuple-element.123.filtered_ref.refs_0_, bf16[1024,128]{1,0:T(8,128)(2,1)S(1)} %collective-permute-done.5.refs_1_, bf16[1024,128]{1,0:T(8,128)(2,1)S(1)} %collective-permute-done.8.refs_2_, ...), custom_call_target="tpu_custom_call" | custom-call | bytes 2097152 | tf_op jit(solution)/shard_map/pallas_call | solution.py:341
  53.6 0.9 %collective-permute-done.16.refs_3_ = bf16[2,32,1024]{2,1,0:T(8,128)(2,1)S(1)} collective-permute-done((bf16[2,32,1024]{2,1,0:T(8,128)(2,1)S(1)}, bf16[2,32,1024]{2,1,0:T(8,128)(2,1)S(1)}, u32[]{:S(2)}, u32[]{:S(2)}) %collective-permute-start.16) | collective-permute-done | bytes 131104 | tf_op jit(solution)/shard_map/ppermute | solution.py:523
  54.5 0.9 %shard_map.114 = (f32[32,1024]{1,0:T(8,128)}, f32[32,1024]{1,0:T(8,128)}) custom-call(s32[1]{0:T(128)} %bitcast.place_ref, s32[1]{0:T(128)} %bitcast.6.band_ref, f32[2,32,1024]{2,1,0:T(8,128)S(1)} %get-tuple-element.127.refs_0_, bf16[2,32,1024]{2,1,0:T(8,128)(2,1)S(1)} %collective-permute-done.15.refs_1_, ...), custom_call_target="tpu_custom_call" | custom-call | bytes 2097152 | tf_op jit(solution)/shard_map/pallas_call | solution.py:341
  (34 shorter events, 6.8 us)
Async XLA Ops:
  0.6 1.7 %copy-start = (bf16[256,512]{1,0:T(8,128)(2,1)S(1)}, bf16[256,512]{1,0:T(8,128)(2,1)}, u32[]{:S(2)}) copy-start(bf16[256,512]{1,0:T(8,128)(2,1)} %field_ref.1) | copy-start | bytes 786436
  1.6 0.7 %copy-start.3 = (f32[256]{0:T(256)S(1)}, f32[256]{0:T(256)}, u32[]{:S(2)}) copy-start(f32[256]{0:T(256)} %param.12) | copy-start | bytes 3076
  1.6 0.7 %copy-start.1 = (s32[125,4]{0,1:T(4,128)S(1)}, s32[125,4]{0,1:T(4,128)}, u32[]{:S(2)}) copy-start(s32[125,4]{0,1:T(4,128)} %param.10) | copy-start | bytes 6004
  1.7 0.7 %copy-start.2 = (f32[256]{0:T(256)S(1)}, f32[256]{0:T(256)}, u32[]{:S(2)}) copy-start(f32[256]{0:T(256)} %param.13) | copy-start | bytes 3076
  1.7 0.7 %copy-start.4 = (s32[1,64]{1,0:T(1,128)S(1)}, s32[1,64]{1,0:T(1,128)}, u32[]{:S(2)}) copy-start(s32[1,64]{1,0:T(1,128)} %param.11) | copy-start | bytes 772
  2.9 7.1 %collective-permute-start = (bf16[544,128]{1,0:T(8,128)(2,1)S(1)}, bf16[544,128]{1,0:T(8,128)(2,1)S(1)}, u32[]{:S(2)}, u32[]{:S(2)}) collective-permute-start(bf16[544,128]{1,0:T(8,128)(2,1)S(1)} %get-tuple-element.69), channel_id=1, source_target_pairs={{0,1},{1,0},{2,3},{3,2},{4,5},{5,4},{6,7},{7,6},{8,9},{9,8},{10,11... | collective-permute-start | bytes 417800 | tf_op jit(solution)/shard_map/ppermute | solution.py:426
  5.9 8.1 %collective-permute-start.1 = (bf16[544,128]{1,0:T(8,128)(2,1)S(1)}, bf16[544,128]{1,0:T(8,128)(2,1)S(1)}, u32[]{:S(2)}, u32[]{:S(2)}) collective-permute-start(bf16[544,128]{1,0:T(8,128)(2,1)S(1)} %get-tuple-element.70), channel_id=1, source_target_pairs={{0,2},{1,3},{2,0},{3,1},{4,6},{5,7},{6,4},{7,5},{8,10},{9,11},{10,... | collective-permute-start | bytes 417800 | tf_op jit(solution)/shard_map/ppermute | solution.py:426
  7.4 7.2 %collective-permute-start.2 = (bf16[544,128]{1,0:T(8,128)(2,1)S(1)}, bf16[544,128]{1,0:T(8,128)(2,1)S(1)}, u32[]{:S(2)}, u32[]{:S(2)}) collective-permute-start(bf16[544,128]{1,0:T(8,128)(2,1)S(1)} %get-tuple-element.71), channel_id=1, source_target_pairs={{0,3},{1,2},{2,1},{3,0},{4,7},{5,6},{6,5},{7,4},{8,11},{9,10},{10,... | collective-permute-start | bytes 417800 | tf_op jit(solution)/shard_map/ppermute | solution.py:426
  17.5 5.7 %collective-permute-start.3 = (bf16[384,128]{1,0:T(8,128)(2,1)S(1)}, bf16[384,128]{1,0:T(8,128)(2,1)S(1)}, u32[]{:S(2)}, u32[]{:S(2)}) collective-permute-start(bf16[384,128]{1,0:T(8,128)(2,1)S(1)} %get-tuple-element.112), channel_id=1, source_target_pairs={{0,4},{1,5},{2,6},{3,7},{4,0},{5,1},{6,2},{7,3},{8,12},{9,13},{10,... | collective-permute-start | bytes 294920 | tf_op jit(solution)/shard_map/ppermute | solution.py:483
  19.1 6.4 %collective-permute-start.4 = (bf16[384,128]{1,0:T(8,128)(2,1)S(1)}, bf16[384,128]{1,0:T(8,128)(2,1)S(1)}, u32[]{:S(2)}, u32[]{:S(2)}) collective-permute-start(bf16[384,128]{1,0:T(8,128)(2,1)S(1)} %get-tuple-element.113), channel_id=1, source_target_pairs={{0,12},{1,13},{2,14},{3,15},{4,8},{5,9},{6,10},{7,11},{8,4},{9,5},... | collective-permute-start | bytes 294920 | tf_op jit(solution)/shard_map/ppermute | solution.py:483
  28.2 9.1 %collective-permute-start.5 = (bf16[1024,128]{1,0:T(8,128)(2,1)S(1)}, bf16[1024,128]{1,0:T(8,128)(2,1)S(1)}, u32[]{:S(2)}, u32[]{:S(2)}) collective-permute-start(bf16[1024,128]{1,0:T(8,128)(2,1)S(1)} %get-tuple-element.123.filtered_ref.refs_0_), channel_id=1, source_target_pairs={{0,3},{1,2},{2,1},{3,0},{4,7},{5,6},{6,5},{7,4},{8,11},{9,10},{10,... | collective-permute-start | bytes 786440 | tf_op jit(solution)/shard_map/ppermute | solution.py:426
  29.8 9.7 %collective-permute-start.9 = (bf16[1024,128]{1,0:T(8,128)(2,1)S(1)}, bf16[1024,128]{1,0:T(8,128)(2,1)S(1)}, u32[]{:S(2)}, u32[]{:S(2)}) collective-permute-start(bf16[1024,128]{1,0:T(8,128)(2,1)S(1)} %get-tuple-element.123.filtered_ref.refs_0_), channel_id=1, source_target_pairs={{0,1},{1,0},{2,3},{3,2},{4,5},{5,4},{6,7},{7,6},{8,9},{9,8},{10,11... | collective-permute-start | bytes 786440 | tf_op jit(solution)/shard_map/ppermute | solution.py:426
  31.3 8.6 %collective-permute-start.8 = (bf16[1024,128]{1,0:T(8,128)(2,1)S(1)}, bf16[1024,128]{1,0:T(8,128)(2,1)S(1)}, u32[]{:S(2)}, u32[]{:S(2)}) collective-permute-start(bf16[1024,128]{1,0:T(8,128)(2,1)S(1)} %get-tuple-element.123.filtered_ref.refs_0_), channel_id=1, source_target_pairs={{0,2},{1,3},{2,0},{3,1},{4,6},{5,7},{6,4},{7,5},{8,10},{9,11},{10,... | collective-permute-start | bytes 786440 | tf_op jit(solution)/shard_map/ppermute | solution.py:426
  31.8 3.7 %collective-permute-start.6 = (bf16[64,128]{1,0:T(8,128)(2,1)S(1)}, bf16[64,128]{1,0:T(8,128)(2,1)S(1)}, u32[]{:S(2)}, u32[]{:S(2)}) collective-permute-start(bf16[64,128]{1,0:T(8,128)(2,1)S(1)} %get-tuple-element.115), channel_id=1, source_target_pairs={{0,4},{1,5},{2,6},{3,7},{4,0},{5,1},{6,2},{7,3},{8,12},{9,13},{10,... | collective-permute-start | bytes 49160 | tf_op jit(solution)/shard_map/ppermute | solution.py:483
  31.8 5.5 %collective-permute-start.7 = (bf16[64,128]{1,0:T(8,128)(2,1)S(1)}, bf16[64,128]{1,0:T(8,128)(2,1)S(1)}, u32[]{:S(2)}, u32[]{:S(2)}) collective-permute-start(bf16[64,128]{1,0:T(8,128)(2,1)S(1)} %get-tuple-element.116), channel_id=1, source_target_pairs={{0,12},{1,13},{2,14},{3,15},{4,8},{5,9},{6,10},{7,11},{8,4},{9,5},... | collective-permute-start | bytes 49160 | tf_op jit(solution)/shard_map/ppermute | solution.py:483
  37.3 2.6 %collective-permute-start.10 = (bf16[1024,128]{1,0:T(8,128)(2,1)S(1)}, bf16[1024,128]{1,0:T(8,128)(2,1)S(1)}, u32[]{:S(2)}, u32[]{:S(2)}) collective-permute-start(bf16[1024,128]{1,0:T(8,128)(2,1)S(1)} %get-tuple-element.123.filtered_ref.refs_0_), channel_id=1, source_target_pairs={{0,16},{16,0},{1,17},{17,1},{2,18},{18,2},{3,19},{19,3},{4,20},{20... | collective-permute-start | bytes 786440 | tf_op jit(solution)/shard_map/ppermute | solution.py:432
  37.3 2.6 %collective-permute-start.11 = (bf16[1024,128]{1,0:T(8,128)(2,1)S(1)}, bf16[1024,128]{1,0:T(8,128)(2,1)S(1)}, u32[]{:S(2)}, u32[]{:S(2)}) collective-permute-start(bf16[1024,128]{1,0:T(8,128)(2,1)S(1)} %collective-permute-done.5.refs_1_), channel_id=1, source_target_pairs={{0,16},{16,0},{1,17},{17,1},{2,18},{18,2},{3,19},{19,3},{4,20},{20... | collective-permute-start | bytes 786440 | tf_op jit(solution)/shard_map/ppermute | solution.py:432
  39.4 1.8 %collective-permute-start.13 = (bf16[1024,128]{1,0:T(8,128)(2,1)S(1)}, bf16[1024,128]{1,0:T(8,128)(2,1)S(1)}, u32[]{:S(2)}, u32[]{:S(2)}) collective-permute-start(bf16[1024,128]{1,0:T(8,128)(2,1)S(1)} %collective-permute-done.9.refs_3_), channel_id=1, source_target_pairs={{0,16},{16,0},{1,17},{17,1},{2,18},{18,2},{3,19},{19,3},{4,20},{20... | collective-permute-start | bytes 786440 | tf_op jit(solution)/shard_map/ppermute | solution.py:432
  39.8 1.5 %collective-permute-start.12 = (bf16[1024,128]{1,0:T(8,128)(2,1)S(1)}, bf16[1024,128]{1,0:T(8,128)(2,1)S(1)}, u32[]{:S(2)}, u32[]{:S(2)}) collective-permute-start(bf16[1024,128]{1,0:T(8,128)(2,1)S(1)} %collective-permute-done.8.refs_2_), channel_id=1, source_target_pairs={{0,16},{16,0},{1,17},{17,1},{2,18},{18,2},{3,19},{19,3},{4,20},{20... | collective-permute-start | bytes 786440 | tf_op jit(solution)/shard_map/ppermute | solution.py:432
  41.8 10.6 %collective-permute-start.14 = (bf16[2,32,1024]{2,1,0:T(8,128)(2,1)S(1)}, bf16[2,32,1024]{2,1,0:T(8,128)(2,1)S(1)}, u32[]{:S(2)}, u32[]{:S(2)}) collective-permute-start(bf16[2,32,1024]{2,1,0:T(8,128)(2,1)S(1)} %get-tuple-element.122), channel_id=1, source_target_pairs={{0,8},{1,9},{2,10},{3,11},{4,12},{5,13},{6,14},{7,15},{8,0},{9,1},... | collective-permute-start | bytes 393224 | tf_op jit(solution)/shard_map/ppermute | solution.py:523
  43.7 9.9 %collective-permute-start.15 = (bf16[2,32,1024]{2,1,0:T(8,128)(2,1)S(1)}, bf16[2,32,1024]{2,1,0:T(8,128)(2,1)S(1)}, u32[]{:S(2)}, u32[]{:S(2)}) collective-permute-start(bf16[2,32,1024]{2,1,0:T(8,128)(2,1)S(1)} %get-tuple-element.128), channel_id=1, source_target_pairs={{0,4},{1,5},{2,6},{3,7},{4,0},{5,1},{6,2},{7,3},{8,12},{9,13},{10,... | collective-permute-start | bytes 393224 | tf_op jit(solution)/shard_map/ppermute | solution.py:523
  45.2 9.3 %collective-permute-start.16 = (bf16[2,32,1024]{2,1,0:T(8,128)(2,1)S(1)}, bf16[2,32,1024]{2,1,0:T(8,128)(2,1)S(1)}, u32[]{:S(2)}, u32[]{:S(2)}) collective-permute-start(bf16[2,32,1024]{2,1,0:T(8,128)(2,1)S(1)} %get-tuple-element.130), channel_id=1, source_target_pairs={{0,12},{1,13},{2,14},{3,15},{4,8},{5,9},{6,10},{7,11},{8,4},{9,5},... | collective-permute-start | bytes 393224 | tf_op jit(solution)/shard_map/ppermute | solution.py:523
